TPU v7x, 512 devices: a whole 4x4x16 slice. The times are simulated.
512 devices in a mesh: tm: 8 (over y, core), row: 16 (over z), col: 4 (over x).
Axes of the slice: x: 4, y: 4, z: 16, core: 2. Of those that a mesh axis runs over, the one named last changes fastest.
Arguments:
- right_side: float32 [3, 8, 512, 1024], P(None, 'tm', 'row', 'col'), may hold values from -6 to 6
- seam_mask: int32 [8, 512, 1024], P('tm', 'row', 'col'), may hold values 0 or 1
- patch_inverse: float32 [1024, 1024], replicated, may hold values from -0.5 to 1.5, as said below
- row_coupling: float32 [32, 32], replicated, may hold values from -0.5 to 1.5, as said below
- col_coupling: float32 [64, 64], replicated, may hold values from -0.5 to 1.5, as said below
Outputs:
- solution: float32 [3, 8, 512, 1024], P(None, 'tm', 'row', 'col')
Inputs may be any that keep to these rules, and one draw needn't show every extreme that they name: `patch_inverse`: symmetric and positive definite. `row_coupling`: symmetric and positive definite. `col_coupling`: symmetric and positive definite.
All inputs are finite; a program needn't handle non-finite values. No bound on the sum of `seam_mask` on one device may be relied on, other than what follows from the above.
Results may differ from a plain program's by a relative error of at most 0.0015.
Values sent between devices are 32-bit elements; how exact they have to be, the bound alone decides.
No kernel may reach another device: no remote copies, remote signals or barrier semaphores. Data moves between devices by JAX's collectives and lax.ppermute only.
A program may use at most 64 MiB of HBM per device.

v0:
```python
import jax
import jax.numpy as jnp
from jax import lax
from jax.sharding import PartitionSpec as P

COARSE = 16
ITERS = 2
CORE = 16
OVER = 8


seam_screen = 0.1
keep_screen = 2.0
time_coupling = 1.0
highest = lax.Precision.HIGHEST


def with_halo(block, sides, width):
    for axis, dim in sides:
        count = lax.axis_size(axis)
        forward = [(i, i + 1) for i in range(count - 1)]
        backward = [(target, source) for source, target in forward]
        low = lax.ppermute(
            lax.slice_in_dim(block, block.shape[dim] - width, None, axis=dim), axis, forward
        )
        high = lax.ppermute(lax.slice_in_dim(block, 0, width, axis=dim), axis, backward)
        block = jnp.concatenate([low, block, high], axis=dim)
    return block


def operate(values, seam_mask):
    screen = jnp.where(seam_mask == 1, seam_screen, keep_screen).astype(jnp.float32)
    padded = with_halo(values, (("tm", 1), ("row", 2), ("col", 3)), 1)
    in_plane = (
        padded[:, 1:-1, 2:, 1:-1]
        + padded[:, 1:-1, :-2, 1:-1]
        + padded[:, 1:-1, 1:-1, 2:]
        + padded[:, 1:-1, 1:-1, :-2]
    )
    across = padded[:, 2:, 1:-1, 1:-1] + padded[:, :-2, 1:-1, 1:-1]
    return (screen + 4.0 + 2.0 * time_coupling) * values - in_plane - time_coupling * across


def patch_sums(extended, inverse, core_size, patch_keep):
    channels, frames, ext_rows, ext_cols = extended.shape
    row_blocks = ext_rows // core_size
    col_blocks = ext_cols // core_size
    blocks = extended.reshape(channels, frames, row_blocks, core_size, col_blocks, core_size)
    row_pairs = jnp.concatenate([blocks[:, :, :-1], blocks[:, :, 1:]], axis=3)
    both_pairs = jnp.concatenate([row_pairs[:, :, :, :, :-1], row_pairs[:, :, :, :, 1:]], axis=5)
    flattened = both_pairs.transpose(0, 1, 2, 4, 3, 5).reshape(-1, 4 * core_size * core_size)
    solved = jnp.dot(flattened, inverse, precision=highest, preferred_element_type=jnp.float32)
    solved = solved.reshape(
        channels, frames, row_blocks - 1, col_blocks - 1, 2 * core_size, 2 * core_size
    )
    solved = solved * patch_keep[None, None, :, :, None, None]
    solved = solved.transpose(0, 1, 2, 4, 3, 5)
    zero_rows = jnp.zeros(
        (channels, frames, 1, core_size, col_blocks - 1, 2 * core_size), jnp.float32
    )
    row_sums = jnp.concatenate([solved[:, :, :, :core_size], zero_rows], axis=2) + jnp.concatenate(
        [zero_rows, solved[:, :, :, core_size:]], axis=2
    )
    zero_cols = jnp.zeros((channels, frames, row_blocks, core_size, 1, core_size), jnp.float32)
    col_sums = jnp.concatenate([row_sums[..., :core_size], zero_cols], axis=4) + jnp.concatenate(
        [zero_cols, row_sums[..., core_size:]], axis=4
    )
    return col_sums.reshape(channels, frames, ext_rows, ext_cols)


def fold_rim(received, along, extent, margin):
    center = lax.slice_in_dim(received, 2 * margin, 2 * margin + extent, axis=along)
    upper = lax.slice_in_dim(received, 0, margin, axis=along)
    lower = lax.slice_in_dim(received, extent + 3 * margin, extent + 4 * margin, axis=along)
    upper_pad = tuple(
        ((0, extent - margin) if position == along else (0, 0) for position in range(received.ndim))
    )
    lower_pad = tuple(
        ((extent - margin, 0) if position == along else (0, 0) for position in range(received.ndim))
    )
    return center + jnp.pad(upper, upper_pad) + jnp.pad(lower, lower_pad)


def coarse_fix(residual, row_coupling, col_coupling):
    channels, frames, height, width = residual.shape
    coarse_rows = height // COARSE
    coarse_cols = width // COARSE
    coarse_sum = residual.reshape(channels, frames, coarse_rows, COARSE, coarse_cols, COARSE).sum(
        axis=(3, 5)
    )
    all_cols = lax.all_gather(coarse_sum, "col", axis=3, tiled=True)
    col_start = lax.axis_index("col") * coarse_cols
    own_cols = lax.dynamic_slice_in_dim(col_coupling, col_start, coarse_cols, axis=0)
    row_start = lax.axis_index("row") * coarse_rows
    own_rows = lax.dynamic_slice_in_dim(row_coupling, row_start, coarse_rows, axis=0)
    all_grid = lax.all_gather(all_cols, "row", axis=2, tiled=True)
    half_done = jnp.einsum("cfjk,lk->cfjl", all_grid, own_cols, precision=highest)
    coarse_done = jnp.einsum("ij,cfjl->cfil", own_rows, half_done, precision=highest)
    spread = jnp.broadcast_to(
        coarse_done[:, :, :, None, :, None],
        (channels, frames, coarse_rows, COARSE, coarse_cols, COARSE),
    )
    return spread.reshape(residual.shape)


def precondition(residual, patch_inverse, row_coupling, col_coupling):
    height = residual.shape[2]
    width = residual.shape[3]
    extended = with_halo(residual, (("row", 2), ("col", 3)), OVER)
    patch_keep = jnp.ones((height // CORE, width // CORE), jnp.float32)
    spread = patch_sums(extended, patch_inverse, CORE, patch_keep)
    received = with_halo(spread, (("row", 2), ("col", 3)), OVER)
    local = fold_rim(fold_rim(received, 2, height, OVER), 3, width, OVER)
    return local + coarse_fix(residual, row_coupling, col_coupling)


def inner_product(left_vec, right_vec):
    return lax.psum(jnp.sum(left_vec * right_vec), ("tm", "row", "col"))


def shards(right_side, seam_mask, patch_inverse, row_coupling, col_coupling):
    solution = jnp.zeros_like(right_side)
    residual = right_side
    precond = precondition(residual, patch_inverse, row_coupling, col_coupling)
    direction = precond
    inner_now = inner_product(residual, precond)
    for iteration in range(ITERS):
        image = operate(direction, seam_mask)
        step_size = inner_now / lax.psum(jnp.sum(direction * image), ("tm", "row", "col"))
        solution = solution + step_size * direction
        if iteration + 1 < ITERS:
            residual = residual - step_size * image
            precond = precondition(residual, patch_inverse, row_coupling, col_coupling)
            inner_next = inner_product(residual, precond)
            direction = precond + inner_next / inner_now * direction
            inner_now = inner_next
    return solution


def solution(mesh):
    in_specs = (P(None, "tm", "row", "col"), P("tm", "row", "col"), P(), P(), P())
    out_specs = P(None, "tm", "row", "col")
    return jax.shard_map(shards, mesh=mesh, in_specs=in_specs, out_specs=out_specs, check_vma=False)
```

profile of v0, /device:TPU:1, one launch (start us, length us, event | category | flops | bytes accessed | tf_op | source)
XLA Modules:
  0.0 561.7 jit_solution(360284734353489579)
XLA Ops:
  0.8 4.4 collective-permute-start
  7.9 9.7 %all-gather = f32[3,2,64]{0,1,2:T(2,128)S(1)} all-gather(f32[3,2,16]{0,1,2:T(2,128)S(1)} %copy.42), channel_id=2, replica_groups=mesh['tm'=8,'row'=16,'col'=4] {'col'}, dimensions={2}, use_global_device_ids=true | all-gather | bytes 1920 | tf_op jit(solution)/shard_map/all_gather | solution.py:91
  17.8 2.5 collective-permute-start.2
  21.6 29.1 %all-gather.1 = f32[3,32,64]{2,0,1:T(4,128)S(1)} all-gather(f32[3,2,64]{2,0,1:T(4,128)S(1)} %copy.43), channel_id=3, replica_groups=mesh['tm'=8,'row'=16,'col'=4] {'row'}, dimensions={1}, use_global_device_ids=true | all-gather | bytes 26112 | tf_op jit(solution)/shard_map/all_gather | solution.py:96
  50.7 5.3 copy.41
  61.5 11.9 %convolution_bitcast_fusion.1 = f32[3,1,2,32,16,32]{5,4,3,2,0,1:T(8,128)S(1)} fusion(f32[32,32,1024,1,1]{2,1,0,4,3:T(8,128)} %bitcast.89, f32[3,2,16,1024,1]{3,2,1,0,4:T(8,128)S(1)} %reshape.87), kind=kOutput, calls=%fused_computation.9 | convolution fusion | flops 1207959552 | bytes 4980736 | tf_op jit(solution)/shard_map/dot_general | solution.py:52
  78.1 3.3 collective-permute-done.5
  81.6 4.3 collective-permute-start.6
  88.6 2.6 collective-permute-done.7
  91.8 17.1 %collective-permute-start.8 = (f32[3,1,32,256]{3,2,0,1:T(8,128)S(1)}, f32[3,1,32,256]{3,2,0,1:T(8,128)S(1)}, u32[]{:S(2)}, u32[]{:S(2)}) collective-permute-start(f32[3,1,32,256]{3,2,0,1:T(8,128)S(1)} %fusion.29), channel_id=1, source_target_pairs={{0,64},{64,128},{128,192},{192,256},{256,320},{320,384},{384,448},... | collective-permute-start | bytes 294920 | tf_op jit(solution)/shard_map/ppermute | solution.py:23
  108.8 1.9 collective-permute-start.9
  110.8 4.0 collective-permute-done.9
  116.1 4.0 collective-permute-start.11
  122.3 4.0 collective-permute-start.13
  126.4 1.8 collective-permute-done.12
  130.7 107.0 %all-reduce.12 = (f32[]{:T(128)}, f32[]{:T(128)}) all-reduce(f32[]{:T(128)} %get-tuple-element.6, f32[]{:T(128)} %get-tuple-element.5), channel_id=1, replica_groups=mesh['tm'=8,'row'=16,'col'=4] {'tm','row','col'}, use_global_device_ids=true, to_apply=%region_2.3 | all-reduce | flops 2 | bytes 16 | tf_op jit(solution)/shard_map/psum | solution.py:118
  239.0 3.5 collective-permute-start.14
  244.3 9.0 %all-gather.2 = f32[3,2,64]{0,1,2:T(2,128)S(1)} all-gather(f32[3,2,16]{0,1,2:T(2,128)S(1)} %copy.50), channel_id=4, replica_groups=mesh['tm'=8,'row'=16,'col'=4] {'col'}, dimensions={2}, use_global_device_ids=true | all-gather | bytes 1920 | tf_op jit(solution)/shard_map/all_gather | solution.py:91
  256.5 25.1 %all-gather.3 = f32[3,32,64]{2,0,1:T(4,128)} all-gather(f32[3,2,64]{2,0,1:T(4,128)S(1)} %copy.51), channel_id=5, replica_groups=mesh['tm'=8,'row'=16,'col'=4] {'row'}, dimensions={1}, use_global_device_ids=true | all-gather | bytes 26112 | tf_op jit(solution)/shard_map/all_gather | solution.py:96
  287.1 11.9 %convolution_bitcast_fusion = f32[3,1,2,32,16,32]{5,4,3,2,0,1:T(8,128)S(1)} fusion(f32[32,32,1024,1,1]{2,1,0,4,3:T(8,128)} %bitcast.90, f32[3,2,16,1024,1]{3,2,1,0,4:T(8,128)S(1)} %reshape.91), kind=kOutput, calls=%fused_computation.8 | convolution fusion | flops 1207959552 | bytes 4980736 | tf_op jit(solution)/shard_map/dot_general | solution.py:52
  300.4 1.9 collective-permute-start.18
  303.9 3.4 collective-permute-done.19
  307.4 4.0 collective-permute-start.20
  314.1 2.6 collective-permute-done.21
  317.8 114.9 %psum.30 = f32[]{:T(128)} all-reduce(f32[]{:T(128)} %get-tuple-element.9), channel_id=1, replica_groups=mesh['tm'=8,'row'=16,'col'=4] {'tm','row','col'}, use_global_device_ids=true, to_apply=%region_7.8 | all-reduce | flops 1 | bytes 8 | tf_op jit(solution)/shard_map/psum | solution.py:118
  434.0 2.8 collective-permute-start.22
  436.8 1.9 collective-permute-start.23
  438.7 4.0 collective-permute-done.23
  444.0 4.0 collective-permute-start.25
  450.3 4.0 collective-permute-start.27
  454.3 1.8 collective-permute-done.26
  458.6 101.1 %psum.31 = f32[]{:T(128)} all-reduce(f32[]{:T(128)} %fusion.16), channel_id=1, replica_groups=mesh['tm'=8,'row'=16,'col'=4] {'tm','row','col'}, use_global_device_ids=true, to_apply=%region_9.10 | all-reduce | flops 1 | bytes 8 | tf_op jit(solution)/shard_map/psum | solution.py:129
  (128 shorter events, 48.3 us)
Async XLA Ops:
  0.0 76.5 %copy-start = (f32[64,64]{1,0:T(8,128)S(1)}, f32[64,64]{1,0:T(8,128)}, u32[]{:S(2)}) copy-start(f32[64,64]{1,0:T(8,128)} %param.9) | copy-start | bytes 49156
  0.0 17.7 %copy-start.1 = (f32[3,1,32,256]{3,2,1,0:T(8,128)S(1)}, f32[3,1,32,256]{3,2,1,0:T(8,128)}, u32[]{:S(2)}) copy-start(f32[3,1,32,256]{3,2,1,0:T(8,128)} %param.5) | copy-start | bytes 294916
  0.8 16.8 %collective-permute-start = (f32[3,1,8,256]{3,2,1,0:T(8,128)S(1)}, f32[3,1,8,256]{3,2,1,0:T(8,128)S(1)}, u32[]{:S(2)}, u32[]{:S(2)}) collective-permute-start(f32[3,1,8,256]{3,2,1,0:T(8,128)S(1)} %get-tuple-element.47), channel_id=1, source_target_pairs={{0,4},{4,8},{8,12},{12,16},{16,20},{20,24},{24,28},{28,32},{32,36}... | collective-permute-start | bytes 73736 | tf_op jit(solution)/shard_map/ppermute | solution.py:23
  5.2 12.5 %collective-permute-start.1 = (f32[3,1,8,256]{3,2,1,0:T(8,128)S(1)}, f32[3,1,8,256]{3,2,1,0:T(8,128)S(1)}, u32[]{:S(2)}, u32[]{:S(2)}) collective-permute-start(f32[3,1,8,256]{3,2,1,0:T(8,128)S(1)} %get-tuple-element.46), channel_id=1, source_target_pairs={{4,0},{8,4},{12,8},{16,12},{20,16},{24,20},{28,24},{32,28},{36,32}... | collective-permute-start | bytes 73736 | tf_op jit(solution)/shard_map/ppermute | solution.py:26
  17.8 38.2 %collective-permute-start.2 = (f32[3,1,48,8]{3,2,1,0:T(8,128)S(1)}, f32[3,1,48,8]{3,2,1,0:T(8,128)S(1)}, u32[]{:S(2)}, u32[]{:S(2)}) collective-permute-start(f32[3,1,48,8]{3,2,1,0:T(8,128)S(1)} %get-tuple-element.42), channel_id=1, source_target_pairs={{0,1},{1,2},{2,3},{4,5},{5,6},{6,7},{8,9},{9,10},{10,11},{12,13},{... | collective-permute-start | bytes 13832 | tf_op jit(solution)/shard_map/ppermute | solution.py:23
  20.3 35.7 %collective-permute-start.3 = (f32[3,1,48,8]{3,2,1,0:T(8,128)S(1)}, f32[3,1,48,8]{3,2,1,0:T(8,128)S(1)}, u32[]{:S(2)}, u32[]{:S(2)}) collective-permute-start(f32[3,1,48,8]{3,2,1,0:T(8,128)S(1)} %get-tuple-element.43), channel_id=1, source_target_pairs={{1,0},{2,1},{3,2},{5,4},{6,5},{7,6},{9,8},{10,9},{11,10},{13,12},{... | collective-permute-start | bytes 13832 | tf_op jit(solution)/shard_map/ppermute | solution.py:26
  74.8 3.3 collective-permute-start.4
  76.7 4.7 collective-permute-start.5
  81.6 7.1 %collective-permute-start.6 = (f32[3,1,64,8]{3,2,0,1:T(8,128)S(1)}, f32[3,1,64,8]{3,2,0,1:T(8,128)S(1)}, u32[]{:S(2)}, u32[]{:S(2)}) collective-permute-start(f32[3,1,64,8]{3,2,0,1:T(8,128)S(1)} %get-tuple-element.34), channel_id=1, source_target_pairs={{0,1},{1,2},{2,3},{4,5},{5,6},{6,7},{8,9},{9,10},{10,11},{12,13},{... | collective-permute-start | bytes 18440 | tf_op jit(solution)/shard_map/ppermute | solution.py:23
  85.9 5.4 collective-permute-start.7
  91.5 34.9 %copy-start.4 = (s32[1,32,256]{2,1,0:T(8,128)S(1)}, s32[1,32,256]{2,1,0:T(8,128)}, u32[]{:S(2)}) copy-start(s32[1,32,256]{2,1,0:T(8,128)} %param.6) | copy-start | bytes 98308
  91.6 147.4 %copy-start.2 = (f32[3,1,32,256]{3,2,1,0:T(8,128)S(1)}, f32[3,1,32,256]{3,2,1,0:T(8,128)}, u32[]{:S(2)}) copy-start(f32[3,1,32,256]{3,2,1,0:T(8,128)} %param.5) | copy-start | bytes 294916
  91.8 19.0 %collective-permute-start.8 = (f32[3,1,32,256]{3,2,0,1:T(8,128)S(1)}, f32[3,1,32,256]{3,2,0,1:T(8,128)S(1)}, u32[]{:S(2)}, u32[]{:S(2)}) collective-permute-start(f32[3,1,32,256]{3,2,0,1:T(8,128)S(1)} %fusion.29), channel_id=1, source_target_pairs={{0,64},{64,128},{128,192},{192,256},{256,320},{320,384},{384,448},... | collective-permute-start | bytes 294920 | tf_op jit(solution)/shard_map/ppermute | solution.py:23
  108.8 5.9 %collective-permute-start.9 = (f32[3,1,32,256]{3,2,0,1:T(8,128)S(1)}, f32[3,1,32,256]{3,2,0,1:T(8,128)S(1)}, u32[]{:S(2)}, u32[]{:S(2)}) collective-permute-start(f32[3,1,32,256]{3,2,0,1:T(8,128)S(1)} %fusion.29), channel_id=1, source_target_pairs={{64,0},{128,64},{192,128},{256,192},{320,256},{384,320},{448,384},... | collective-permute-start | bytes 294920 | tf_op jit(solution)/shard_map/ppermute | solution.py:26
  114.8 5.3 collective-permute-start.10
  116.1 4.8 collective-permute-start.11
  121.0 7.1 %collective-permute-start.12 = (f32[3,3,34,1]{3,2,0,1:T(8,128)S(1)}, f32[3,3,34,1]{3,2,0,1:T(8,128)S(1)}, u32[]{:S(2)}, u32[]{:S(2)}) collective-permute-start(f32[3,3,34,1]{3,2,0,1:T(8,128)S(1)} %get-tuple-element.26), channel_id=1, source_target_pairs={{1,0},{2,1},{3,2},{5,4},{6,5},{7,6},{9,8},{10,9},{11,10},{13,12},{... | collective-permute-start | bytes 3680 | tf_op jit(solution)/shard_map/ppermute | solution.py:26
  122.3 7.6 %collective-permute-start.13 = (f32[3,3,34,1]{3,2,0,1:T(8,128)S(1)}, f32[3,3,34,1]{3,2,0,1:T(8,128)S(1)}, u32[]{:S(2)}, u32[]{:S(2)}) collective-permute-start(f32[3,3,34,1]{3,2,0,1:T(8,128)S(1)} %get-tuple-element.27), channel_id=1, source_target_pairs={{0,1},{1,2},{2,3},{4,5},{5,6},{6,7},{8,9},{9,10},{10,11},{12,13},{... | collective-permute-start | bytes 3680 | tf_op jit(solution)/shard_map/ppermute | solution.py:23
  239.0 14.3 %collective-permute-start.14 = (f32[3,1,8,256]{3,2,0,1:T(8,128)S(1)}, f32[3,1,8,256]{3,2,0,1:T(8,128)S(1)}, u32[]{:S(2)}, u32[]{:S(2)}) collective-permute-start(f32[3,1,8,256]{3,2,0,1:T(8,128)S(1)} %get-tuple-element.44), channel_id=1, source_target_pairs={{0,4},{4,8},{8,12},{12,16},{16,20},{20,24},{24,28},{28,32},{32,36}... | collective-permute-start | bytes 73736 | tf_op jit(solution)/shard_map/ppermute | solution.py:23
  242.5 10.9 %collective-permute-start.15 = (f32[3,1,8,256]{3,2,0,1:T(8,128)S(1)}, f32[3,1,8,256]{3,2,0,1:T(8,128)S(1)}, u32[]{:S(2)}, u32[]{:S(2)}) collective-permute-start(f32[3,1,8,256]{3,2,0,1:T(8,128)S(1)} %get-tuple-element.45), channel_id=1, source_target_pairs={{4,0},{8,4},{12,8},{16,12},{20,16},{24,20},{28,24},{32,28},{36,32}... | collective-permute-start | bytes 73736 | tf_op jit(solution)/shard_map/ppermute | solution.py:26
  253.5 28.1 %collective-permute-start.16 = (f32[3,1,48,8]{3,2,0,1:T(8,128)S(1)}, f32[3,1,48,8]{3,2,0,1:T(8,128)S(1)}, u32[]{:S(2)}, u32[]{:S(2)}) collective-permute-start(f32[3,1,48,8]{3,2,0,1:T(8,128)S(1)} %get-tuple-element.40), channel_id=1, source_target_pairs={{0,1},{1,2},{2,3},{4,5},{5,6},{6,7},{8,9},{9,10},{10,11},{12,13},{... | collective-permute-start | bytes 13832 | tf_op jit(solution)/shard_map/ppermute | solution.py:23
  255.2 26.4 %collective-permute-start.17 = (f32[3,1,48,8]{3,2,0,1:T(8,128)S(1)}, f32[3,1,48,8]{3,2,0,1:T(8,128)S(1)}, u32[]{:S(2)}, u32[]{:S(2)}) collective-permute-start(f32[3,1,48,8]{3,2,0,1:T(8,128)S(1)} %get-tuple-element.41), channel_id=1, source_target_pairs={{1,0},{2,1},{3,2},{5,4},{6,5},{7,6},{9,8},{10,9},{11,10},{13,12},{... | collective-permute-start | bytes 13832 | tf_op jit(solution)/shard_map/ppermute | solution.py:26
  300.4 3.5 collective-permute-start.18
  302.6 4.7 collective-permute-start.19
  307.4 6.7 %collective-permute-start.20 = (f32[3,1,64,8]{3,2,0,1:T(8,128)S(1)}, f32[3,1,64,8]{3,2,0,1:T(8,128)S(1)}, u32[]{:S(2)}, u32[]{:S(2)}) collective-permute-start(f32[3,1,64,8]{3,2,0,1:T(8,128)S(1)} %get-tuple-element.30), channel_id=1, source_target_pairs={{0,1},{1,2},{2,3},{4,5},{5,6},{6,7},{8,9},{9,10},{10,11},{12,13},{... | collective-permute-start | bytes 18440 | tf_op jit(solution)/shard_map/ppermute | solution.py:23
  311.4 5.4 collective-permute-start.21
  434.0 4.7 collective-permute-start.22
  436.8 5.9 %collective-permute-start.23 = (f32[3,1,32,256]{3,2,0,1:T(8,128)S(1)}, f32[3,1,32,256]{3,2,0,1:T(8,128)S(1)}, u32[]{:S(2)}, u32[]{:S(2)}) collective-permute-start(f32[3,1,32,256]{3,2,0,1:T(8,128)S(1)} %multiply_add_fusion), channel_id=1, source_target_pairs={{64,0},{128,64},{192,128},{256,192},{320,256},{384,320},{448,384},... | collective-permute-start | bytes 294920 | tf_op jit(solution)/shard_map/ppermute | solution.py:26
  442.7 5.3 collective-permute-start.24
  444.0 4.8 collective-permute-start.25
  449.0 7.1 %collective-permute-start.26 = (f32[3,3,34,1]{3,2,0,1:T(8,128)S(1)}, f32[3,3,34,1]{3,2,0,1:T(8,128)S(1)}, u32[]{:S(2)}, u32[]{:S(2)}) collective-permute-start(f32[3,3,34,1]{3,2,0,1:T(8,128)S(1)} %get-tuple-element.24), channel_id=1, source_target_pairs={{1,0},{2,1},{3,2},{5,4},{6,5},{7,6},{9,8},{10,9},{11,10},{13,12},{... | collective-permute-start | bytes 3680 | tf_op jit(solution)/shard_map/ppermute | solution.py:26
  450.3 7.6 %collective-permute-start.27 = (f32[3,3,34,1]{3,2,0,1:T(8,128)S(1)}, f32[3,3,34,1]{3,2,0,1:T(8,128)S(1)}, u32[]{:S(2)}, u32[]{:S(2)}) collective-permute-start(f32[3,3,34,1]{3,2,0,1:T(8,128)S(1)} %get-tuple-element.25), channel_id=1, source_target_pairs={{0,1},{1,2},{2,3},{4,5},{5,6},{6,7},{8,9},{9,10},{10,11},{12,13},{... | collective-permute-start | bytes 3680 | tf_op jit(solution)/shard_map/ppermute | solution.py:23
  (3 other events, 19.2 us)
where the time goes:
time: 563 us; the launch traced here: 562 us
  blocking collectives  396 us (70%)
  starting transfers between devices  79.1 us (14%)
  waiting for transfers between devices  28.7 us (5%)
  matrix products  26.1 us (5%)
  local copies, waits for them, and re-layouts  20.1 us (4%)
  other arithmetic  7.2 us (1%)
    psum x2, blocking collectives, inner_product(): return lax.psum(jnp.sum(left_vec * right_vec), ('tm', 'row', 'col'))  222 us
    psum x1, blocking collectives, shards(): lax.psum(jnp.sum(direction * image), ('tm', 'row', 'col'))  101 us
    ppermute x14, starting transfers between devices, with_halo(): lax.ppermute(lax.slice_in_dim(block, block.shape[dim] - width, None, axis...  59.8 us
    all_gather x2, blocking collectives, coarse_fix(): all_grid = lax.all_gather(all_cols, 'row', axis=2, tiled=True)  54.2 us
    dot_general x2, matrix products, patch_sums(): jnp.dot(flattened, inverse, precision=highest, preferred_element_type=jnp...  23.7 us
    ppermute x14, waiting for transfers between devices, with_halo(): lax.ppermute(lax.slice_in_dim(block, 0, width, axis=dim), axis, backward)  23.6 us
    ppermute x14, starting transfers between devices, with_halo(): lax.ppermute(lax.slice_in_dim(block, 0, width, axis=dim), axis, backward)  19.4 us
    all_gather x2, blocking collectives, coarse_fix(): all_cols = lax.all_gather(coarse_sum, 'col', axis=3, tiled=True)  18.7 us
  transfers between devices with their start and end apart: 28, of which 12 were waited for; matrix products, arithmetic and copies ran while one was open for 2% of the time, Pallas kernels for 0%

commit v1 on v0

--- a/solution.py
+++ b/solution.py
@@ -4,7 +4,6 @@
 from jax.sharding import PartitionSpec as P
 
 COARSE = 16
-ITERS = 2
 CORE = 16
 OVER = 8
 
@@ -30,18 +29,24 @@
 
 def operate(values, seam_mask):
     screen = jnp.where(seam_mask == 1, seam_screen, keep_screen).astype(jnp.float32)
-    padded = with_halo(values, (("tm", 1), ("row", 2), ("col", 3)), 1)
-    in_plane = (
-        padded[:, 1:-1, 2:, 1:-1]
-        + padded[:, 1:-1, :-2, 1:-1]
-        + padded[:, 1:-1, 1:-1, 2:]
-        + padded[:, 1:-1, 1:-1, :-2]
-    )
-    across = padded[:, 2:, 1:-1, 1:-1] + padded[:, :-2, 1:-1, 1:-1]
+    low_row, high_row = shifted(values[:, :, -1:], values[:, :, :1], "row")
+    low_col, high_col = shifted(values[:, :, :, -1:], values[:, :, :, :1], "col")
+    before, after = shifted(values, values, "tm")
+    rows = jnp.concatenate([low_row, values, high_row], axis=2)
+    cols = jnp.concatenate([low_col, values, high_col], axis=3)
+    in_plane = rows[:, :, 2:] + rows[:, :, :-2] + cols[:, :, :, 2:] + cols[:, :, :, :-2]
+    across = before + after
     return (screen + 4.0 + 2.0 * time_coupling) * values - in_plane - time_coupling * across
 
 
-def patch_sums(extended, inverse, core_size, patch_keep):
+def shifted(last, first, axis):
+    count = lax.axis_size(axis)
+    forward = [(i, i + 1) for i in range(count - 1)]
+    backward = [(target, source) for source, target in forward]
+    return lax.ppermute(last, axis, forward), lax.ppermute(first, axis, backward)
+
+
+def patch_sums(extended, inverse, core_size):
     channels, frames, ext_rows, ext_cols = extended.shape
     row_blocks = ext_rows // core_size
     col_blocks = ext_cols // core_size
@@ -49,11 +54,10 @@
     row_pairs = jnp.concatenate([blocks[:, :, :-1], blocks[:, :, 1:]], axis=3)
     both_pairs = jnp.concatenate([row_pairs[:, :, :, :, :-1], row_pairs[:, :, :, :, 1:]], axis=5)
     flattened = both_pairs.transpose(0, 1, 2, 4, 3, 5).reshape(-1, 4 * core_size * core_size)
-    solved = jnp.dot(flattened, inverse, precision=highest, preferred_element_type=jnp.float32)
+    solved = jnp.dot(flattened, inverse, precision=lax.Precision.HIGH, preferred_element_type=jnp.float32)
     solved = solved.reshape(
         channels, frames, row_blocks - 1, col_blocks - 1, 2 * core_size, 2 * core_size
     )
-    solved = solved * patch_keep[None, None, :, :, None, None]
     solved = solved.transpose(0, 1, 2, 4, 3, 5)
     zero_rows = jnp.zeros(
         (channels, frames, 1, core_size, col_blocks - 1, 2 * core_size), jnp.float32
@@ -81,6 +85,12 @@
     return center + jnp.pad(upper, upper_pad) + jnp.pad(lower, lower_pad)
 
 
+def everyone(value, axes):
+    count = lax.axis_size(axes)
+    copies = jnp.broadcast_to(value[None], (count,) + value.shape)
+    return lax.all_to_all(copies, axes, 0, 0)
+
+
 def coarse_fix(residual, row_coupling, col_coupling):
     channels, frames, height, width = residual.shape
     coarse_rows = height // COARSE
@@ -88,12 +98,17 @@
     coarse_sum = residual.reshape(channels, frames, coarse_rows, COARSE, coarse_cols, COARSE).sum(
         axis=(3, 5)
     )
-    all_cols = lax.all_gather(coarse_sum, "col", axis=3, tiled=True)
+    rows = lax.axis_size("row")
+    cols = lax.axis_size("col")
+    gathered = everyone(coarse_sum, ("row", "col"))
+    all_grid = gathered.reshape(rows, cols, channels, frames, coarse_rows, coarse_cols)
+    all_grid = all_grid.transpose(2, 3, 0, 4, 1, 5).reshape(
+        channels, frames, rows * coarse_rows, cols * coarse_cols
+    )
     col_start = lax.axis_index("col") * coarse_cols
     own_cols = lax.dynamic_slice_in_dim(col_coupling, col_start, coarse_cols, axis=0)
     row_start = lax.axis_index("row") * coarse_rows
     own_rows = lax.dynamic_slice_in_dim(row_coupling, row_start, coarse_rows, axis=0)
-    all_grid = lax.all_gather(all_cols, "row", axis=2, tiled=True)
     half_done = jnp.einsum("cfjk,lk->cfjl", all_grid, own_cols, precision=highest)
     coarse_done = jnp.einsum("ij,cfjl->cfil", own_rows, half_done, precision=highest)
     spread = jnp.broadcast_to(
@@ -107,34 +122,32 @@
     height = residual.shape[2]
     width = residual.shape[3]
     extended = with_halo(residual, (("row", 2), ("col", 3)), OVER)
-    patch_keep = jnp.ones((height // CORE, width // CORE), jnp.float32)
-    spread = patch_sums(extended, patch_inverse, CORE, patch_keep)
+    spread = patch_sums(extended, patch_inverse, CORE)
     received = with_halo(spread, (("row", 2), ("col", 3)), OVER)
     local = fold_rim(fold_rim(received, 2, height, OVER), 3, width, OVER)
     return local + coarse_fix(residual, row_coupling, col_coupling)
 
 
-def inner_product(left_vec, right_vec):
-    return lax.psum(jnp.sum(left_vec * right_vec), ("tm", "row", "col"))
-
-
 def shards(right_side, seam_mask, patch_inverse, row_coupling, col_coupling):
-    solution = jnp.zeros_like(right_side)
-    residual = right_side
-    precond = precondition(residual, patch_inverse, row_coupling, col_coupling)
-    direction = precond
-    inner_now = inner_product(residual, precond)
-    for iteration in range(ITERS):
-        image = operate(direction, seam_mask)
-        step_size = inner_now / lax.psum(jnp.sum(direction * image), ("tm", "row", "col"))
-        solution = solution + step_size * direction
-        if iteration + 1 < ITERS:
-            residual = residual - step_size * image
-            precond = precondition(residual, patch_inverse, row_coupling, col_coupling)
-            inner_next = inner_product(residual, precond)
-            direction = precond + inner_next / inner_now * direction
-            inner_now = inner_next
-    return solution
+    first = precondition(right_side, patch_inverse, row_coupling, col_coupling)
+    image = operate(first, seam_mask)
+    second = precondition(image, patch_inverse, row_coupling, col_coupling)
+    second_image = operate(second, seam_mask)
+    pairs = jnp.stack([
+        jnp.sum(right_side * first),
+        jnp.sum(first * image),
+        jnp.sum(image * second),
+        jnp.sum(second * second_image),
+    ])
+    pairs = jnp.sum(everyone(pairs, ("tm", "col")), axis=0)
+    pairs = jnp.sum(everyone(pairs, "row"), axis=0)
+    inner0, curve0, cross, curve_second = pairs[0], pairs[1], pairs[2], pairs[3]
+    step0 = inner0 / curve0
+    inner1 = inner0 - 2.0 * step0 * curve0 + step0 * step0 * cross
+    grow = 1.0 + inner1 / inner0
+    curve1 = grow * grow * curve0 - 2.0 * grow * step0 * cross + step0 * step0 * curve_second
+    step1 = inner1 / curve1
+    return (step0 + step1 * grow) * first - (step1 * step0) * second
 
 
 def solution(mesh):

time: 563 us -> 248 us (0.44)
  blocking collectives: 396 us -> 31.7 us
  starting transfers between devices: 79.1 us -> 106 us
  waiting for transfers between devices: 28.7 us -> 55.5 us
  matrix products: 26.1 us -> 16.2 us
    psum x3 -> x0, blocking collectives: 323 us -> none  [the longest x2 222 us: inner_product(): return lax.psum(jnp.sum(left_vec * right_vec), ('tm', 'row', 'col'))]
    all_gather x4 -> x0, blocking collectives: 72.9 us -> none  [the longest x2 54.2 us: coarse_fix(): all_grid = lax.all_gather(all_cols, 'row', axis=2, tiled=True)]
    ppermute x0 -> x12, starting transfers between devices: none -> 43.6 us  [the longest x6 34.6 us: shifted(): lax.ppermute(last, axis, forward)]
    ppermute x14 -> x8, starting transfers between devices: 59.8 us -> 25.9 us  [with_halo(): lax.ppermute(lax.slice_in_dim(block, block.shape[dim] - width, None, axis...]
    all_to_all x0 -> x2, waiting for transfers between devices: none -> 31.9 us  [everyone(): return lax.all_to_all(copies, axes, 0, 0)]
    all_to_all x0 -> x2, blocking collectives: none -> 31.7 us  [everyone(): return lax.all_to_all(copies, axes, 0, 0)]
    all_to_all x0 -> x2, starting transfers between devices: none -> 25.9 us  [everyone(): return lax.all_to_all(copies, axes, 0, 0)]
    dot_general x2, matrix products: 23.7 us -> 13.8 us  [patch_sums(): jnp.dot(flattened, inverse, precision=lax.Precision.HIGH, preferred_eleme...]
  transfers between devices with their start and end apart: 28 -> 30, of which waited for: 12 -> 10; matrix products, arithmetic and copies ran while one was open for 2% -> 4% of each run, Pallas kernels for 0% -> 0%
where the time goes in v1:
time: 248 us; the launch traced here: 246 us
  starting transfers between devices  106 us (43%)
  waiting for transfers between devices  55.5 us (22%)
  blocking collectives  31.7 us (13%)
  local copies, waits for them, and re-layouts  22.2 us (9%)
  matrix products  16.2 us (7%)
  other arithmetic  8.41 us (3%)
  between operations  6.54 us (3%)
    ppermute x6, starting transfers between devices, shifted(): lax.ppermute(last, axis, forward)  34.6 us
    all_to_all x2, waiting for transfers between devices, everyone(): return lax.all_to_all(copies, axes, 0, 0)  31.9 us
    all_to_all x2, blocking collectives, everyone(): return lax.all_to_all(copies, axes, 0, 0)  31.7 us
    all_to_all x2, starting transfers between devices, everyone(): return lax.all_to_all(copies, axes, 0, 0)  25.9 us
    ppermute x8, starting transfers between devices, with_halo(): lax.ppermute(lax.slice_in_dim(block, block.shape[dim] - width, None, axis...  25.9 us
    ppermute x8, waiting for transfers between devices, with_halo(): lax.ppermute(lax.slice_in_dim(block, 0, width, axis=dim), axis, backward)  18.1 us
    dot_general x2, matrix products, patch_sums(): jnp.dot(flattened, inverse, precision=lax.Precision.HIGH, preferred_eleme...  13.8 us
    ppermute x8, starting transfers between devices, with_halo(): lax.ppermute(lax.slice_in_dim(block, 0, width, axis=dim), axis, backward)  10.5 us
  transfers between devices with their start and end apart: 30, of which 10 were waited for; matrix products, arithmetic and copies ran while one was open for 4% of the time, Pallas kernels for 0%

profile of v1, /device:TPU:1, one launch (start us, length us, event | category | flops | bytes accessed | tf_op | source)
XLA Modules:
  0.0 246.2 jit_solution(13518883668720108479)
XLA Ops:
  0.8 4.4 %collective-permute-start = (f32[3,1,8,256]{3,2,1,0:T(8,128)S(1)}, f32[3,1,8,256]{3,2,1,0:T(8,128)S(1)}, u32[]{:S(2)}, u32[]{:S(2)}) collective-permute-start(f32[3,1,8,256]{3,2,1,0:T(8,128)S(1)} %get-tuple-element.44), channel_id=1, source_target_pairs={{0,4},{4,8},{8,12},{12,16},{16,20},{20,24},{24,28},{28,32},{32,36}... | collective-permute-start | bytes 73736 | tf_op jit(solution)/shard_map/ppermute | solution.py:22
  7.4 2.5 %collective-permute-done.1 = f32[3,1,8,256]{3,2,1,0:T(8,128)S(1)} collective-permute-done((f32[3,1,8,256]{3,2,1,0:T(8,128)S(1)}, f32[3,1,8,256]{3,2,1,0:T(8,128)S(1)}, u32[]{:S(2)}, u32[]{:S(2)}) %collective-permute-start.1) | collective-permute-done | bytes 24608 | tf_op jit(solution)/shard_map/ppermute | solution.py:25
  10.0 3.1 %collective-permute-start.2 = (f32[3,1,48,8]{3,2,1,0:T(8,128)S(1)}, f32[3,1,48,8]{3,2,1,0:T(8,128)S(1)}, u32[]{:S(2)}, u32[]{:S(2)}) collective-permute-start(f32[3,1,48,8]{3,2,1,0:T(8,128)S(1)} %get-tuple-element.31), channel_id=1, source_target_pairs={{0,1},{1,2},{2,3},{4,5},{5,6},{6,7},{8,9},{9,10},{10,11},{12,13},{... | collective-permute-start | bytes 13832 | tf_op jit(solution)/shard_map/ppermute | solution.py:22
  14.4 5.4 %copy.59 = f32[1024,1024]{0,1:T(8,128)} copy(f32[1024,1024]{1,0:T(8,128)} %param.7) | data formatting | bytes 8388608 | tf_op args[2]
  25.3 6.9 %convolution_bitcast_fusion.1 = f32[3,1,2,32,16,32]{5,4,3,2,0,1:T(8,128)S(1)} fusion(f32[32,32,1024,1,1]{2,1,0,4,3:T(8,128)} %bitcast.107, f32[3,2,16,1024,1]{3,2,1,0,4:T(8,128)S(1)} %reshape.113), kind=kOutput, calls=%fused_computation.9 | convolution fusion | flops 603979776 | bytes 4980736 | tf_op jit(solution)/shard_map/dot_general | solution.py:57
  33.6 3.5 %collective-permute-start.4 = (f32[3,1,8,272]{3,2,0,1:T(8,128)S(1)}, f32[3,1,8,272]{3,2,0,1:T(8,128)S(1)}, u32[]{:S(2)}, u32[]{:S(2)}) collective-permute-start(f32[3,1,8,272]{3,2,0,1:T(8,128)S(1)} %get-tuple-element.28), channel_id=1, source_target_pairs={{0,4},{4,8},{8,12},{12,16},{16,20},{20,24},{24,28},{28,32},{32,36}... | collective-permute-start | bytes 78344 | tf_op jit(solution)/shard_map/ppermute | solution.py:22
  38.5 4.8 %collective-permute-done.5 = f32[3,1,8,272]{3,2,0,1:T(8,128)S(1)} collective-permute-done((f32[3,1,8,272]{3,2,0,1:T(8,128)S(1)}, f32[3,1,8,272]{3,2,0,1:T(8,128)S(1)}, u32[]{:S(2)}, u32[]{:S(2)}) %collective-permute-start.5) | collective-permute-done | bytes 26144 | tf_op jit(solution)/shard_map/ppermute | solution.py:25
  43.3 4.0 %collective-permute-start.6 = (f32[3,1,64,8]{3,2,0,1:T(8,128)S(1)}, f32[3,1,64,8]{3,2,0,1:T(8,128)S(1)}, u32[]{:S(2)}, u32[]{:S(2)}) collective-permute-start(f32[3,1,64,8]{3,2,0,1:T(8,128)S(1)} %get-tuple-element.23), channel_id=1, source_target_pairs={{0,1},{1,2},{2,3},{4,5},{5,6},{6,7},{8,9},{9,10},{10,11},{12,13},{... | collective-permute-start | bytes 18440 | tf_op jit(solution)/shard_map/ppermute | solution.py:22
  49.8 17.0 %all-to-all-start = ((f32[64,3,1,2,16]{4,3,1,2,0:T(2,128)}), f32[64,3,1,2,16]{4,3,1,2,0:T(2,128)S(1)}, u32[]{:S(2)}, u32[]{:S(2)}) async-start(f32[64,3,1,2,16]{4,3,1,2,0:T(2,128)} %broadcast_in_dim.56), calls=%async_computation | async-start | bytes 393216 | tf_op jit(solution)/shard_map/all_to_all | solution.py:91
  67.2 15.9 %all-to-all-done = f32[64,3,1,2,16]{4,3,1,2,0:T(2,128)S(1)} async-done(((f32[64,3,1,2,16]{4,3,1,2,0:T(2,128)}), f32[64,3,1,2,16]{4,3,1,2,0:T(2,128)S(1)}, u32[]{:S(2)}, u32[]{:S(2)}) %all-to-all-start) | async-done | bytes 24608 | tf_op jit(solution)/shard_map/all_to_all | solution.py:91
  85.2 8.8 %collective-permute-start.12 = (f32[3,1,32,256]{3,2,0,1:T(8,128)S(1)}, f32[3,1,32,256]{3,2,0,1:T(8,128)S(1)}, u32[]{:S(2)}, u32[]{:S(2)}) collective-permute-start(f32[3,1,32,256]{3,2,0,1:T(8,128)S(1)} %fusion.29), channel_id=1, source_target_pairs={{0,64},{64,128},{128,192},{192,256},{256,320},{320,384},{384,448},... | collective-permute-start | bytes 294920 | tf_op jit(solution)/shard_map/ppermute | solution.py:46
  94.1 1.9 collective-permute-start.13
  97.3 4.0 %collective-permute-start.11 = (f32[3,1,32,1]{3,2,0,1:T(8,128)S(1)}, f32[3,1,32,1]{3,2,0,1:T(8,128)S(1)}, u32[]{:S(2)}, u32[]{:S(2)}) collective-permute-start(f32[3,1,32,1]{3,2,0,1:T(8,128)S(1)} %get-tuple-element.42), channel_id=1, source_target_pairs={{0,1},{1,2},{2,3},{4,5},{5,6},{6,7},{8,9},{9,10},{10,11},{12,13},{... | collective-permute-start | bytes 1160 | tf_op jit(solution)/shard_map/ppermute | solution.py:46
  102.6 4.0 %collective-permute-start.9 = (f32[3,1,1,256]{3,2,0,1:T(1,128)S(1)}, f32[3,1,1,256]{3,2,0,1:T(1,128)S(1)}, u32[]{:S(2)}, u32[]{:S(2)}) collective-permute-start(f32[3,1,1,256]{3,2,0,1:T(1,128)S(1)} %get-tuple-element.40), channel_id=1, source_target_pairs={{0,4},{4,8},{8,12},{12,16},{16,20},{20,24},{24,28},{28,32},{32,36}... | collective-permute-start | bytes 9224 | tf_op jit(solution)/shard_map/ppermute | solution.py:46
  107.5 3.6 %collective-permute-start.14 = (f32[3,1,8,256]{3,2,0,1:T(8,128)S(1)}, f32[3,1,8,256]{3,2,0,1:T(8,128)S(1)}, u32[]{:S(2)}, u32[]{:S(2)}) collective-permute-start(f32[3,1,8,256]{3,2,0,1:T(8,128)S(1)} %get-tuple-element.37), channel_id=1, source_target_pairs={{0,4},{4,8},{8,12},{12,16},{16,20},{20,24},{24,28},{28,32},{32,36}... | collective-permute-start | bytes 73736 | tf_op jit(solution)/shard_map/ppermute | solution.py:22
  112.4 3.3 %collective-permute-done.15 = f32[3,1,8,256]{3,2,0,1:T(8,128)S(1)} collective-permute-done((f32[3,1,8,256]{3,2,0,1:T(8,128)S(1)}, f32[3,1,8,256]{3,2,0,1:T(8,128)S(1)}, u32[]{:S(2)}, u32[]{:S(2)}) %collective-permute-start.15) | collective-permute-done | bytes 24608 | tf_op jit(solution)/shard_map/ppermute | solution.py:25
  115.8 2.1 collective-permute-start.16
  119.4 3.6 %collective-permute-done.17 = f32[3,1,48,8]{3,2,0,1:T(8,128)S(1)} collective-permute-done((f32[3,1,48,8]{3,2,0,1:T(8,128)S(1)}, f32[3,1,48,8]{3,2,0,1:T(8,128)S(1)}, u32[]{:S(2)}, u32[]{:S(2)}) %collective-permute-start.17) | collective-permute-done | bytes 4640 | tf_op jit(solution)/shard_map/ppermute | solution.py:25
  128.5 6.9 %convolution_bitcast_fusion = f32[3,1,2,32,16,32]{5,4,3,2,0,1:T(8,128)S(1)} fusion(f32[32,32,1024,1,1]{2,1,0,4,3:T(8,128)} %bitcast.108, f32[3,2,16,1024,1]{3,2,1,0,4:T(8,128)S(1)} %reshape.117), kind=kOutput, calls=%fused_computation.8 | convolution fusion | flops 603979776 | bytes 4980736 | tf_op jit(solution)/shard_map/dot_general | solution.py:57
  136.8 2.7 %collective-permute-start.18 = (f32[3,1,8,272]{3,2,0,1:T(8,128)S(1)}, f32[3,1,8,272]{3,2,0,1:T(8,128)S(1)}, u32[]{:S(2)}, u32[]{:S(2)}) collective-permute-start(f32[3,1,8,272]{3,2,0,1:T(8,128)S(1)} %get-tuple-element.26), channel_id=1, source_target_pairs={{0,4},{4,8},{8,12},{12,16},{16,20},{20,24},{24,28},{28,32},{32,36}... | collective-permute-start | bytes 78344 | tf_op jit(solution)/shard_map/ppermute | solution.py:22
  140.8 4.0 %collective-permute-done.19 = f32[3,1,8,272]{3,2,0,1:T(8,128)S(1)} collective-permute-done((f32[3,1,8,272]{3,2,0,1:T(8,128)S(1)}, f32[3,1,8,272]{3,2,0,1:T(8,128)S(1)}, u32[]{:S(2)}, u32[]{:S(2)}) %collective-permute-start.19) | collective-permute-done | bytes 26144 | tf_op jit(solution)/shard_map/ppermute | solution.py:25
  144.9 2.4 collective-permute-start.20
  149.8 8.9 %all-to-all-start.1 = ((f32[64,3,1,2,16]{4,3,1,2,0:T(2,128)}), f32[64,3,1,2,16]{4,3,1,2,0:T(2,128)S(1)}, u32[]{:S(2)}, u32[]{:S(2)}) async-start(f32[64,3,1,2,16]{4,3,1,2,0:T(2,128)} %broadcast_in_dim.62), calls=%async_computation.1 | async-start | bytes 393216 | tf_op jit(solution)/shard_map/all_to_all | solution.py:91
  159.0 16.0 %all-to-all-done.1 = f32[64,3,1,2,16]{4,3,1,2,0:T(2,128)S(1)} async-done(((f32[64,3,1,2,16]{4,3,1,2,0:T(2,128)}), f32[64,3,1,2,16]{4,3,1,2,0:T(2,128)S(1)}, u32[]{:S(2)}, u32[]{:S(2)}) %all-to-all-start.1) | async-done | bytes 24608 | tf_op jit(solution)/shard_map/all_to_all | solution.py:91
  177.0 11.6 %collective-permute-start.26 = (f32[3,1,32,256]{3,2,0,1:T(8,128)S(1)}, f32[3,1,32,256]{3,2,0,1:T(8,128)S(1)}, u32[]{:S(2)}, u32[]{:S(2)}) collective-permute-start(f32[3,1,32,256]{3,2,0,1:T(8,128)S(1)} %fusion.21), channel_id=1, source_target_pairs={{0,64},{64,128},{128,192},{192,256},{256,320},{320,384},{384,448},... | collective-permute-start | bytes 294920 | tf_op jit(solution)/shard_map/ppermute | solution.py:46
  188.6 1.9 collective-permute-start.27
  191.8 4.0 %collective-permute-start.23 = (f32[3,1,1,256]{3,2,0,1:T(1,128)S(1)}, f32[3,1,1,256]{3,2,0,1:T(1,128)S(1)}, u32[]{:S(2)}, u32[]{:S(2)}) collective-permute-start(f32[3,1,1,256]{3,2,0,1:T(1,128)S(1)} %get-tuple-element.34), channel_id=1, source_target_pairs={{0,4},{4,8},{8,12},{12,16},{16,20},{20,24},{24,28},{28,32},{32,36}... | collective-permute-start | bytes 9224 | tf_op jit(solution)/shard_map/ppermute | solution.py:46
  197.2 3.5 %collective-permute-done.24 = f32[3,1,32,1]{3,2,0,1:T(8,128)S(1)} collective-permute-done((f32[3,1,32,1]{3,2,0,1:T(8,128)S(1)}, f32[3,1,32,1]{3,2,0,1:T(8,128)S(1)}, u32[]{:S(2)}, u32[]{:S(2)}) %collective-permute-start.24) | collective-permute-done | bytes 416 | tf_op jit(solution)/shard_map/ppermute | solution.py:46
  200.7 2.2 collective-permute-start.25
  204.9 2.6 %pad_maximum_fusion.15 = f32[4]{0:T(128)S(1)} fusion(f32[1]{0:T(128)} %bitcast.34, f32[1]{0:T(128)} %bitcast.33, f32[1]{0:T(128)} %bitcast.19, f32[1]{0:T(128)} %bitcast.17), kind=kLoop, calls=%fused_computation.93 | loop fusion | flops 12 | bytes 32 | tf_op jit(solution)/shard_map/stack | solution.py:136
  207.5 17.0 %all_to_all.22 = f32[32,1,4]{2,1,0:T(1,128)S(1)} all-to-all(f32[32,1,4]{2,1,0:T(1,128)S(1)} %broadcast_in_dim.66), channel_id=1, replica_groups=mesh['tm'=8,'row'=16,'col'=4] {'tm','col'}, dimensions={0} | all-to-all | bytes 1024 | tf_op jit(solution)/shard_map/all_to_all | solution.py:91
  224.6 14.6 %all_to_all.23 = f32[16,1,4]{2,1,0:T(1,128)S(1)} all-to-all(f32[16,1,4]{2,1,0:T(1,128)S(1)} %broadcast_in_dim.67), channel_id=1, replica_groups=mesh['tm'=8,'row'=16,'col'=4] {'row'}, dimensions={0} | all-to-all | bytes 512 | tf_op jit(solution)/shard_map/all_to_all | solution.py:91
  (131 shorter events, 42.6 us)
Async XLA Ops:
  0.0 83.3 %copy-start = (f32[64,64]{1,0:T(8,128)S(1)}, f32[64,64]{1,0:T(8,128)}, u32[]{:S(2)}) copy-start(f32[64,64]{1,0:T(8,128)} %param.9) | copy-start | bytes 49156
  0.8 5.7 %collective-permute-start = (f32[3,1,8,256]{3,2,1,0:T(8,128)S(1)}, f32[3,1,8,256]{3,2,1,0:T(8,128)S(1)}, u32[]{:S(2)}, u32[]{:S(2)}) collective-permute-start(f32[3,1,8,256]{3,2,1,0:T(8,128)S(1)} %get-tuple-element.44), channel_id=1, source_target_pairs={{0,4},{4,8},{8,12},{12,16},{16,20},{20,24},{24,28},{28,32},{32,36}... | collective-permute-start | bytes 73736 | tf_op jit(solution)/shard_map/ppermute | solution.py:22
  5.1 4.8 %collective-permute-start.1 = (f32[3,1,8,256]{3,2,1,0:T(8,128)S(1)}, f32[3,1,8,256]{3,2,1,0:T(8,128)S(1)}, u32[]{:S(2)}, u32[]{:S(2)}) collective-permute-start(f32[3,1,8,256]{3,2,1,0:T(8,128)S(1)} %get-tuple-element.43), channel_id=1, source_target_pairs={{4,0},{8,4},{12,8},{16,12},{20,16},{24,20},{28,24},{32,28},{36,32}... | collective-permute-start | bytes 73736 | tf_op jit(solution)/shard_map/ppermute | solution.py:25
  10.0 9.8 %collective-permute-start.2 = (f32[3,1,48,8]{3,2,1,0:T(8,128)S(1)}, f32[3,1,48,8]{3,2,1,0:T(8,128)S(1)}, u32[]{:S(2)}, u32[]{:S(2)}) collective-permute-start(f32[3,1,48,8]{3,2,1,0:T(8,128)S(1)} %get-tuple-element.31), channel_id=1, source_target_pairs={{0,1},{1,2},{2,3},{4,5},{5,6},{6,7},{8,9},{9,10},{10,11},{12,13},{... | collective-permute-start | bytes 13832 | tf_op jit(solution)/shard_map/ppermute | solution.py:22
  13.1 6.7 %collective-permute-start.3 = (f32[3,1,48,8]{3,2,1,0:T(8,128)S(1)}, f32[3,1,48,8]{3,2,1,0:T(8,128)S(1)}, u32[]{:S(2)}, u32[]{:S(2)}) collective-permute-start(f32[3,1,48,8]{3,2,1,0:T(8,128)S(1)} %get-tuple-element.32), channel_id=1, source_target_pairs={{1,0},{2,1},{3,2},{5,4},{6,5},{7,6},{9,8},{10,9},{11,10},{13,12},{... | collective-permute-start | bytes 13832 | tf_op jit(solution)/shard_map/ppermute | solution.py:25
  33.6 4.9 %collective-permute-start.4 = (f32[3,1,8,272]{3,2,0,1:T(8,128)S(1)}, f32[3,1,8,272]{3,2,0,1:T(8,128)S(1)}, u32[]{:S(2)}, u32[]{:S(2)}) collective-permute-start(f32[3,1,8,272]{3,2,0,1:T(8,128)S(1)} %get-tuple-element.28), channel_id=1, source_target_pairs={{0,4},{4,8},{8,12},{12,16},{16,20},{20,24},{24,28},{28,32},{32,36}... | collective-permute-start | bytes 78344 | tf_op jit(solution)/shard_map/ppermute | solution.py:22
  37.1 6.1 %collective-permute-start.5 = (f32[3,1,8,272]{3,2,0,1:T(8,128)S(1)}, f32[3,1,8,272]{3,2,0,1:T(8,128)S(1)}, u32[]{:S(2)}, u32[]{:S(2)}) collective-permute-start(f32[3,1,8,272]{3,2,0,1:T(8,128)S(1)} %get-tuple-element.27), channel_id=1, source_target_pairs={{4,0},{8,4},{12,8},{16,12},{20,16},{24,20},{28,24},{32,28},{36,32}... | collective-permute-start | bytes 78344 | tf_op jit(solution)/shard_map/ppermute | solution.py:25
  43.3 23.5 %collective-permute-start.6 = (f32[3,1,64,8]{3,2,0,1:T(8,128)S(1)}, f32[3,1,64,8]{3,2,0,1:T(8,128)S(1)}, u32[]{:S(2)}, u32[]{:S(2)}) collective-permute-start(f32[3,1,64,8]{3,2,0,1:T(8,128)S(1)} %get-tuple-element.23), channel_id=1, source_target_pairs={{0,1},{1,2},{2,3},{4,5},{5,6},{6,7},{8,9},{9,10},{10,11},{12,13},{... | collective-permute-start | bytes 18440 | tf_op jit(solution)/shard_map/ppermute | solution.py:22
  47.3 19.5 %collective-permute-start.7 = (f32[3,1,64,8]{3,2,0,1:T(8,128)S(1)}, f32[3,1,64,8]{3,2,0,1:T(8,128)S(1)}, u32[]{:S(2)}, u32[]{:S(2)}) collective-permute-start(f32[3,1,64,8]{3,2,0,1:T(8,128)S(1)} %get-tuple-element.24), channel_id=1, source_target_pairs={{1,0},{2,1},{3,2},{5,4},{6,5},{7,6},{9,8},{10,9},{11,10},{13,12},{... | collective-permute-start | bytes 18440 | tf_op jit(solution)/shard_map/ppermute | solution.py:25
  49.8 33.3 %all-to-all-start = ((f32[64,3,1,2,16]{4,3,1,2,0:T(2,128)}), f32[64,3,1,2,16]{4,3,1,2,0:T(2,128)S(1)}, u32[]{:S(2)}, u32[]{:S(2)}) async-start(f32[64,3,1,2,16]{4,3,1,2,0:T(2,128)} %broadcast_in_dim.56), calls=%async_computation | async-start | bytes 393216 | tf_op jit(solution)/shard_map/all_to_all | solution.py:91
  85.2 22.1 %collective-permute-start.12 = (f32[3,1,32,256]{3,2,0,1:T(8,128)S(1)}, f32[3,1,32,256]{3,2,0,1:T(8,128)S(1)}, u32[]{:S(2)}, u32[]{:S(2)}) collective-permute-start(f32[3,1,32,256]{3,2,0,1:T(8,128)S(1)} %fusion.29), channel_id=1, source_target_pairs={{0,64},{64,128},{128,192},{192,256},{256,320},{320,384},{384,448},... | collective-permute-start | bytes 294920 | tf_op jit(solution)/shard_map/ppermute | solution.py:46
  94.1 13.3 %collective-permute-start.13 = (f32[3,1,32,256]{3,2,0,1:T(8,128)S(1)}, f32[3,1,32,256]{3,2,0,1:T(8,128)S(1)}, u32[]{:S(2)}, u32[]{:S(2)}) collective-permute-start(f32[3,1,32,256]{3,2,0,1:T(8,128)S(1)} %fusion.29), channel_id=1, source_target_pairs={{64,0},{128,64},{192,128},{256,192},{320,256},{384,320},{448,384},... | collective-permute-start | bytes 294920 | tf_op jit(solution)/shard_map/ppermute | solution.py:46
  96.0 6.6 %collective-permute-start.10 = (f32[3,1,32,1]{3,2,0,1:T(8,128)S(1)}, f32[3,1,32,1]{3,2,0,1:T(8,128)S(1)}, u32[]{:S(2)}, u32[]{:S(2)}) collective-permute-start(f32[3,1,32,1]{3,2,0,1:T(8,128)S(1)} %get-tuple-element.41), channel_id=1, source_target_pairs={{1,0},{2,1},{3,2},{5,4},{6,5},{7,6},{9,8},{10,9},{11,10},{13,12},{... | collective-permute-start | bytes 1160 | tf_op jit(solution)/shard_map/ppermute | solution.py:46
  97.3 9.3 %collective-permute-start.11 = (f32[3,1,32,1]{3,2,0,1:T(8,128)S(1)}, f32[3,1,32,1]{3,2,0,1:T(8,128)S(1)}, u32[]{:S(2)}, u32[]{:S(2)}) collective-permute-start(f32[3,1,32,1]{3,2,0,1:T(8,128)S(1)} %get-tuple-element.42), channel_id=1, source_target_pairs={{0,1},{1,2},{2,3},{4,5},{5,6},{6,7},{8,9},{9,10},{10,11},{12,13},{... | collective-permute-start | bytes 1160 | tf_op jit(solution)/shard_map/ppermute | solution.py:46
  101.3 5.3 %collective-permute-start.8 = (f32[3,1,1,256]{3,2,0,1:T(1,128)S(1)}, f32[3,1,1,256]{3,2,0,1:T(1,128)S(1)}, u32[]{:S(2)}, u32[]{:S(2)}) collective-permute-start(f32[3,1,1,256]{3,2,0,1:T(1,128)S(1)} %get-tuple-element.39), channel_id=1, source_target_pairs={{4,0},{8,4},{12,8},{16,12},{20,16},{24,20},{28,24},{32,28},{36,32}... | collective-permute-start | bytes 9224 | tf_op jit(solution)/shard_map/ppermute | solution.py:46
  102.6 4.7 %collective-permute-start.9 = (f32[3,1,1,256]{3,2,0,1:T(1,128)S(1)}, f32[3,1,1,256]{3,2,0,1:T(1,128)S(1)}, u32[]{:S(2)}, u32[]{:S(2)}) collective-permute-start(f32[3,1,1,256]{3,2,0,1:T(1,128)S(1)} %get-tuple-element.40), channel_id=1, source_target_pairs={{0,4},{4,8},{8,12},{12,16},{16,20},{20,24},{24,28},{28,32},{32,36}... | collective-permute-start | bytes 9224 | tf_op jit(solution)/shard_map/ppermute | solution.py:46
  107.5 4.9 %collective-permute-start.14 = (f32[3,1,8,256]{3,2,0,1:T(8,128)S(1)}, f32[3,1,8,256]{3,2,0,1:T(8,128)S(1)}, u32[]{:S(2)}, u32[]{:S(2)}) collective-permute-start(f32[3,1,8,256]{3,2,0,1:T(8,128)S(1)} %get-tuple-element.37), channel_id=1, source_target_pairs={{0,4},{4,8},{8,12},{12,16},{16,20},{20,24},{24,28},{28,32},{32,36}... | collective-permute-start | bytes 73736 | tf_op jit(solution)/shard_map/ppermute | solution.py:22
  111.1 4.6 %collective-permute-start.15 = (f32[3,1,8,256]{3,2,0,1:T(8,128)S(1)}, f32[3,1,8,256]{3,2,0,1:T(8,128)S(1)}, u32[]{:S(2)}, u32[]{:S(2)}) collective-permute-start(f32[3,1,8,256]{3,2,0,1:T(8,128)S(1)} %get-tuple-element.38), channel_id=1, source_target_pairs={{4,0},{8,4},{12,8},{16,12},{20,16},{24,20},{28,24},{32,28},{36,32}... | collective-permute-start | bytes 73736 | tf_op jit(solution)/shard_map/ppermute | solution.py:25
  115.8 3.6 %collective-permute-start.16 = (f32[3,1,48,8]{3,2,0,1:T(8,128)S(1)}, f32[3,1,48,8]{3,2,0,1:T(8,128)S(1)}, u32[]{:S(2)}, u32[]{:S(2)}) collective-permute-start(f32[3,1,48,8]{3,2,0,1:T(8,128)S(1)} %get-tuple-element.29), channel_id=1, source_target_pairs={{0,1},{1,2},{2,3},{4,5},{5,6},{6,7},{8,9},{9,10},{10,11},{12,13},{... | collective-permute-start | bytes 13832 | tf_op jit(solution)/shard_map/ppermute | solution.py:22
  117.9 5.1 %collective-permute-start.17 = (f32[3,1,48,8]{3,2,0,1:T(8,128)S(1)}, f32[3,1,48,8]{3,2,0,1:T(8,128)S(1)}, u32[]{:S(2)}, u32[]{:S(2)}) collective-permute-start(f32[3,1,48,8]{3,2,0,1:T(8,128)S(1)} %get-tuple-element.30), channel_id=1, source_target_pairs={{1,0},{2,1},{3,2},{5,4},{6,5},{7,6},{9,8},{10,9},{11,10},{13,12},{... | collective-permute-start | bytes 13832 | tf_op jit(solution)/shard_map/ppermute | solution.py:25
  136.8 4.0 %collective-permute-start.18 = (f32[3,1,8,272]{3,2,0,1:T(8,128)S(1)}, f32[3,1,8,272]{3,2,0,1:T(8,128)S(1)}, u32[]{:S(2)}, u32[]{:S(2)}) collective-permute-start(f32[3,1,8,272]{3,2,0,1:T(8,128)S(1)} %get-tuple-element.26), channel_id=1, source_target_pairs={{0,4},{4,8},{8,12},{12,16},{16,20},{20,24},{24,28},{28,32},{32,36}... | collective-permute-start | bytes 78344 | tf_op jit(solution)/shard_map/ppermute | solution.py:22
  139.5 5.3 %collective-permute-start.19 = (f32[3,1,8,272]{3,2,0,1:T(8,128)S(1)}, f32[3,1,8,272]{3,2,0,1:T(8,128)S(1)}, u32[]{:S(2)}, u32[]{:S(2)}) collective-permute-start(f32[3,1,8,272]{3,2,0,1:T(8,128)S(1)} %get-tuple-element.25), channel_id=1, source_target_pairs={{4,0},{8,4},{12,8},{16,12},{20,16},{24,20},{28,24},{32,28},{36,32}... | collective-permute-start | bytes 78344 | tf_op jit(solution)/shard_map/ppermute | solution.py:25
  144.9 13.8 %collective-permute-start.20 = (f32[3,1,64,8]{3,2,0,1:T(8,128)S(1)}, f32[3,1,64,8]{3,2,0,1:T(8,128)S(1)}, u32[]{:S(2)}, u32[]{:S(2)}) collective-permute-start(f32[3,1,64,8]{3,2,0,1:T(8,128)S(1)} %get-tuple-element.21), channel_id=1, source_target_pairs={{0,1},{1,2},{2,3},{4,5},{5,6},{6,7},{8,9},{9,10},{10,11},{12,13},{... | collective-permute-start | bytes 18440 | tf_op jit(solution)/shard_map/ppermute | solution.py:22
  147.4 11.3 %collective-permute-start.21 = (f32[3,1,64,8]{3,2,0,1:T(8,128)S(1)}, f32[3,1,64,8]{3,2,0,1:T(8,128)S(1)}, u32[]{:S(2)}, u32[]{:S(2)}) collective-permute-start(f32[3,1,64,8]{3,2,0,1:T(8,128)S(1)} %get-tuple-element.22), channel_id=1, source_target_pairs={{1,0},{2,1},{3,2},{5,4},{6,5},{7,6},{9,8},{10,9},{11,10},{13,12},{... | collective-permute-start | bytes 18440 | tf_op jit(solution)/shard_map/ppermute | solution.py:25
  149.8 25.2 %all-to-all-start.1 = ((f32[64,3,1,2,16]{4,3,1,2,0:T(2,128)}), f32[64,3,1,2,16]{4,3,1,2,0:T(2,128)S(1)}, u32[]{:S(2)}, u32[]{:S(2)}) async-start(f32[64,3,1,2,16]{4,3,1,2,0:T(2,128)} %broadcast_in_dim.62), calls=%async_computation.1 | async-start | bytes 393216 | tf_op jit(solution)/shard_map/all_to_all | solution.py:91
  175.0 29.1 %copy-start.2 = (f32[3,1,32,256]{3,2,1,0:T(8,128)S(1)}, f32[3,1,32,256]{3,2,1,0:T(8,128)}, u32[]{:S(2)}) copy-start(f32[3,1,32,256]{3,2,1,0:T(8,128)} %param.5) | copy-start | bytes 294916
  177.0 27.1 %collective-permute-start.26 = (f32[3,1,32,256]{3,2,0,1:T(8,128)S(1)}, f32[3,1,32,256]{3,2,0,1:T(8,128)S(1)}, u32[]{:S(2)}, u32[]{:S(2)}) collective-permute-start(f32[3,1,32,256]{3,2,0,1:T(8,128)S(1)} %fusion.21), channel_id=1, source_target_pairs={{0,64},{64,128},{128,192},{192,256},{256,320},{320,384},{384,448},... | collective-permute-start | bytes 294920 | tf_op jit(solution)/shard_map/ppermute | solution.py:46
  188.6 15.5 %collective-permute-start.27 = (f32[3,1,32,256]{3,2,0,1:T(8,128)S(1)}, f32[3,1,32,256]{3,2,0,1:T(8,128)S(1)}, u32[]{:S(2)}, u32[]{:S(2)}) collective-permute-start(f32[3,1,32,256]{3,2,0,1:T(8,128)S(1)} %fusion.21), channel_id=1, source_target_pairs={{64,0},{128,64},{192,128},{256,192},{320,256},{384,320},{448,384},... | collective-permute-start | bytes 294920 | tf_op jit(solution)/shard_map/ppermute | solution.py:46
  190.5 13.6 %collective-permute-start.22 = (f32[3,1,1,256]{3,2,0,1:T(1,128)S(1)}, f32[3,1,1,256]{3,2,0,1:T(1,128)S(1)}, u32[]{:S(2)}, u32[]{:S(2)}) collective-permute-start(f32[3,1,1,256]{3,2,0,1:T(1,128)S(1)} %get-tuple-element.33), channel_id=1, source_target_pairs={{4,0},{8,4},{12,8},{16,12},{20,16},{24,20},{28,24},{32,28},{36,32}... | collective-permute-start | bytes 9224 | tf_op jit(solution)/shard_map/ppermute | solution.py:46
  191.8 12.3 %collective-permute-start.23 = (f32[3,1,1,256]{3,2,0,1:T(1,128)S(1)}, f32[3,1,1,256]{3,2,0,1:T(1,128)S(1)}, u32[]{:S(2)}, u32[]{:S(2)}) collective-permute-start(f32[3,1,1,256]{3,2,0,1:T(1,128)S(1)} %get-tuple-element.34), channel_id=1, source_target_pairs={{0,4},{4,8},{8,12},{12,16},{16,20},{20,24},{24,28},{28,32},{32,36}... | collective-permute-start | bytes 9224 | tf_op jit(solution)/shard_map/ppermute | solution.py:46
  195.9 4.8 %collective-permute-start.24 = (f32[3,1,32,1]{3,2,0,1:T(8,128)S(1)}, f32[3,1,32,1]{3,2,0,1:T(8,128)S(1)}, u32[]{:S(2)}, u32[]{:S(2)}) collective-permute-start(f32[3,1,32,1]{3,2,0,1:T(8,128)S(1)} %get-tuple-element.35), channel_id=1, source_target_pairs={{1,0},{2,1},{3,2},{5,4},{6,5},{7,6},{9,8},{10,9},{11,10},{13,12},{... | collective-permute-start | bytes 1160 | tf_op jit(solution)/shard_map/ppermute | solution.py:46
  200.7 3.4 %collective-permute-start.25 = (f32[3,1,32,1]{3,2,0,1:T(8,128)S(1)}, f32[3,1,32,1]{3,2,0,1:T(8,128)S(1)}, u32[]{:S(2)}, u32[]{:S(2)}) collective-permute-start(f32[3,1,32,1]{3,2,0,1:T(8,128)S(1)} %get-tuple-element.36), channel_id=1, source_target_pairs={{0,1},{1,2},{2,3},{4,5},{5,6},{6,7},{8,9},{9,10},{10,11},{12,13},{... | collective-permute-start | bytes 1160 | tf_op jit(solution)/shard_map/ppermute | solution.py:46
  (4 other events, 80.6 us)

commit v2 on v0

v2 whole, which is shorter than its diff:
```python
import functools

import jax
import jax.numpy as jnp
from jax import lax
from jax.experimental import pallas as pl
from jax.experimental.pallas import tpu as pltpu
from jax.sharding import PartitionSpec as P

CELL = 16
RIM = 24
seam_screen = 0.1
keep_screen = 2.0
highest = lax.Precision.HIGHEST
f32 = jnp.float32
bf16 = jnp.bfloat16

ROWS = 32
COLS = 256
TALL = ROWS + 2 * RIM
LANES = 384
PATCH_ROWS = 16
PATCH_COLS = 18
PATCHES = PATCH_ROWS * PATCH_COLS
FLAT = 272
SPREAD = 96


def call(body, outs, scratch=(), limit=40):
    shapes = [jax.ShapeDtypeStruct(shape, f32) for shape in outs]
    return pl.pallas_call(
        body,
        out_shape=shapes,
        scratch_shapes=list(scratch),
        compiler_params=pltpu.CompilerParams(vmem_limit_bytes=limit * 1024 * 1024),
    )


def lanes_of(shape):
    return lax.broadcasted_iota(jnp.int32, shape, len(shape) - 1)


def rows_of(ref, start, count):
    return jnp.concatenate([ref[group, pl.ds(start, count), :] for group in range(3)], axis=1)


def put_rows(ref, start, count, value):
    for group in range(3):
        ref[group, pl.ds(start, count), :] = value[:, 128 * group : 128 * group + 128]


def stripe_of(ref, start):
    return jnp.concatenate([ref.at[group][pl.ds(start, PATCH_ROWS, stride=CELL), :] for group in range(3)], axis=1)


def swap_blocks(parts):
    lane = lanes_of(parts[0].shape)
    for step in (1, 2):
        taken = (lane // (32 * step)) % 2 == 1
        fresh = list(parts)
        for low in range(4):
            if low & step:
                continue
            first, second = parts[low], parts[low + step]
            fresh[low] = jnp.where(taken, pltpu.roll(second, 32 * step, 1), first)
            fresh[low + step] = jnp.where(taken, second, pltpu.roll(first, 128 - 32 * step, 1))
        parts = fresh
    return parts


def patch_apply(field, result, high_w, low_w, keep, high_x, low_x, solved):
    for block in range(8):
        slabs = [stripe_of(field, 4 * block + row) for row in range(4)]
        for parity in range(2):
            if parity:
                slabs = [pltpu.roll(slab, LANES - CELL, 1) for slab in slabs]
            for group in range(3):
                parts = swap_blocks([slab[:, 128 * group : 128 * group + 128] for slab in slabs])
                for inner in range(4):
                    place = 8 * group + 2 * inner + parity
                    if place >= PATCH_COLS:
                        continue
                    upper = parts[inner].astype(bf16)
                    lower = (parts[inner] - upper.astype(f32)).astype(bf16)
                    where = (pl.ds(PATCH_ROWS * place, PATCH_ROWS), pl.ds(128 * block, 128))
                    high_x[where] = upper
                    low_x[where] = lower
    for part in range(4):
        span = pl.ds(256 * part, 256)
        dot = functools.partial(jnp.dot, preferred_element_type=f32)
        total = dot(high_x[...], high_w[:, span]) + dot(high_x[...], low_w[:, span])
        total = total + dot(low_x[...], high_w[:, span])
        solved[:, span] = total * keep[...]
    put_rows(result, FLAT - CELL, CELL, jnp.zeros((CELL, LANES), f32))
    for block in range(8):
        sums = None
        for parity in range(2):
            slabs = [[] for _ in range(4)]
            for group in range(3):
                parts = []
                for inner in range(4):
                    place = 8 * group + 2 * inner + parity
                    if place >= PATCH_COLS:
                        parts.append(jnp.zeros((PATCH_ROWS, 128), f32))
                    else:
                        parts.append(solved[pl.ds(PATCH_ROWS * place, PATCH_ROWS), pl.ds(128 * block, 128)])
                for row, piece in enumerate(swap_blocks(parts)):
                    slabs[row].append(piece)
            wide = [jnp.concatenate(pieces, axis=1) for pieces in slabs]
            if parity:
                sums = [total + pltpu.roll(slab, CELL, 1) for total, slab in zip(sums, wide)]
            else:
                sums = wide
        for row in range(4):
            total = sums[row]
            if block >= 4:
                total = total + stripe_of(result, 4 * block + row)
            for group in range(3):
                spot = pl.ds(4 * block + row, PATCH_ROWS, stride=CELL)
                result.at[group][spot, :] = total[:, 128 * group : 128 * group + 128]


def merge_sides(middle, left, right):
    lane = lanes_of(left.shape)
    first = jnp.where(lane < RIM, left, middle[:, :128])
    last = jnp.where((lane >= RIM) & (lane < 2 * RIM), right, middle[:, 256:])
    return jnp.concatenate([first, middle[:, 128:256], last], axis=1)


def cell_sums(blocks):
    rows = [jnp.sum(block[CELL * half : CELL * half + CELL], axis=0, keepdims=True) for block in blocks for half in range(2)]
    lane = lax.broadcasted_iota(jnp.int32, (LANES, 128), 0) - RIM
    cell = lanes_of((LANES, 128))
    inside = (lane >= CELL * cell) & (lane < CELL * cell + CELL) & (cell < COLS // CELL)
    stacked = jnp.concatenate(rows, axis=0)
    return jnp.dot(stacked, inside.astype(f32), precision=highest, preferred_element_type=f32)


def assemble(low, block, mask, high, tall, to_right, to_left, cells):
    own = []
    for channel in range(4):
        if channel < 3:
            middle = block[channel]
        else:
            middle = jnp.where(mask[...] == 1, seam_screen, keep_screen).astype(f32)
        column = jnp.concatenate([low[channel], middle, high[channel]], axis=0)
        wide = jnp.concatenate([column, jnp.zeros((TALL, 128), f32)], axis=1)
        wide = pltpu.roll(wide, RIM, 1)
        tall[channel] = wide
        to_right[channel] = wide[:, 256:]
        to_left[channel] = wide[:, :128]
        own.append(wide[RIM : RIM + ROWS])
    cells[...] = cell_sums(own)


def first_apply(tall, left, right, cells, high_w, low_w, keep, result, screen, share, field, high_x, low_x, solved):
    put_rows(field, 240, FLAT - 240, jnp.zeros((FLAT - 240, LANES), f32))
    for channel in range(3):
        put_rows(field, TALL * channel, TALL, merge_sides(tall[channel], left[channel], right[channel]))
    screen[...] = merge_sides(tall[3], left[3], right[3])
    patch_apply(field, result, high_w, low_w, keep, high_x, low_x, solved)
    for channel in range(3):
        share[pl.ds(ROWS * channel, ROWS), :] = rows_of(result, TALL * channel + RIM, ROWS)
    share[pl.ds(3 * ROWS, 8), :] = jnp.concatenate([cells[...], jnp.zeros((8, 256), f32)], axis=1)


def first_image(result, before, after, screen, cells, image, message):
    lane = lanes_of((ROWS, LANES))
    own = (lane >= RIM) & (lane < RIM + COLS)
    blocks = []
    for channel in range(3):
        base = TALL * channel + RIM
        center = rows_of(result, base, ROWS)
        near = rows_of(result, base - 1, ROWS) + rows_of(result, base + 1, ROWS)
        near = near + pltpu.roll(center, 1, 1) + pltpu.roll(center, LANES - 1, 1)
        span = pl.ds(ROWS * channel, ROWS)
        value = (screen[pl.ds(RIM, ROWS), :] + 6.0) * center - near - before[span, :] - after[span, :]
        value = jnp.where(own, value, 0.0)
        image[channel] = value
        blocks.append(value)
    sums = cell_sums(blocks)
    beside = before[pl.ds(3 * ROWS, 8), :128] + after[pl.ds(3 * ROWS, 8), :128]
    rows = [cells[0:6], beside[0:6], sums, cells[6:8]]
    rows = [part[row : row + 1] for part in rows for row in range(part.shape[0])]
    lane = lanes_of((1, 128))
    packed = []
    for group in range(3):
        total = jnp.zeros((1, 128), f32)
        for spot in range(8):
            if 8 * group + spot < len(rows):
                row = rows[8 * group + spot]
                row = pltpu.roll(row, CELL * spot, 1) if spot else row
                total = jnp.where(lane // CELL == spot, row, total)
        packed.append(total)
    message[...] = jnp.concatenate(packed, axis=1)


def second_apply(
    row_count, col_count, place, gathered, block, result, image, low, high, left, right, screen, high_w, low_w, keep,
    row_mix, col_mix, row_spread, col_spread, first, second, partial,
    field, output, high_x, low_x, solved, coarse, beside, letters,
):
    dot = functools.partial(jnp.dot, precision=highest, preferred_element_type=f32)
    lane = lanes_of((row_count, 128))
    put_rows(letters, 0, row_count * col_count, gathered[...])

    def grid_of(index):
        halves = []
        for half in range(2):
            chunk = 2 * index + half
            total = jnp.zeros((row_count, 128), f32)
            for col in range(col_count):
                piece = letters.at[chunk // 8][pl.ds(col, row_count, stride=col_count), :]
                shift = (CELL * col - CELL * (chunk % 8)) % 128
                piece = pltpu.roll(piece, shift, 1) if shift else piece
                total = jnp.where(lane // CELL == col, piece, total)
            halves.append(total)
        return jnp.concatenate(halves, axis=0)

    def spread(grid):
        return dot(row_spread[...], dot(grid, col_spread[...]))

    screen_cells = grid_of(9)
    grid_lane = lanes_of((2 * row_count, 128))
    zero_row = jnp.zeros((1, 128), f32)
    row0 = 2 * place[0] * CELL - RIM
    col0 = place[1] * COLS - RIM
    tall_row = lax.broadcasted_iota(jnp.int32, (TALL, LANES), 0) + row0
    tall_col = lanes_of((TALL, LANES))
    real = tall_col < COLS + 2 * RIM
    tall_col = tall_col + col0
    inside = (tall_row >= 0) & (tall_row < ROWS * row_count) & (tall_col >= 0) & (tall_col < COLS * col_count) & real
    tall_lane = lanes_of((ROWS, LANES))
    own = (tall_lane >= RIM) & (tall_lane < RIM + COLS)
    put_rows(field, 240, FLAT - 240, jnp.zeros((FLAT - 240, LANES), f32))
    first_grids = []
    for channel in range(3):
        sums = grid_of(channel)
        beside_sums = grid_of(3 + channel)
        level = dot(dot(row_mix[...], sums), col_mix[...])
        level_beside = dot(dot(row_mix[...], beside_sums), col_mix[...])
        even, odd = level[:row_count], level[row_count:]
        above = jnp.concatenate([zero_row, odd[:-1], even], axis=0)
        below = jnp.concatenate([odd, even[1:], zero_row], axis=0)
        before = jnp.where(grid_lane == 0, 0.0, pltpu.roll(level, 1, 1))
        after = jnp.where(grid_lane == CELL * col_count - 1, 0.0, pltpu.roll(level, 127, 1))
        image_sums = grid_of(6 + channel) + (screen_cells + 576.0) * level
        image_sums = image_sums - 16.0 * (above + below + before + after) - 256.0 * level_beside
        first_grids.append(image_sums)
        coarse[channel] = spread(sums)
        beside[channel] = spread(beside_sums)
    for channel in range(3):
        center = coarse[channel, pl.ds(8, TALL), :]
        near = coarse[channel, pl.ds(7, TALL), :] + coarse[channel, pl.ds(9, TALL), :]
        near = near + pltpu.roll(center, 1, 1) + pltpu.roll(center, LANES - 1, 1)
        value = (screen[...] + 6.0) * center - near - beside[channel, pl.ds(8, TALL), :]
        middle = jnp.concatenate([low[channel], image[channel], high[channel]], axis=0)
        value = value + merge_sides(middle, left[channel], right[channel])
        put_rows(field, TALL * channel, TALL, jnp.where(inside, value, 0.0))
    patch_apply(field, output, high_w, low_w, keep, high_x, low_x, solved)
    totals = [jnp.zeros((ROWS, LANES), f32) for _ in range(4)]
    for channel in range(3):
        whole = rows_of(output, TALL * channel, TALL) + spread(first_grids[channel])[8 : 8 + TALL]
        put_rows(output, TALL * channel, TALL, jnp.where(inside, whole, 0.0))
        base = TALL * channel + RIM
        new = rows_of(output, base, ROWS)
        near = rows_of(output, base - 1, ROWS) + rows_of(output, base + 1, ROWS)
        near = near + pltpu.roll(new, 1, 1) + pltpu.roll(new, LANES - 1, 1)
        new_image = (screen[pl.ds(RIM, ROWS), :] + 6.0) * new - near
        old = jnp.where(own, rows_of(result, base, ROWS) + coarse[channel, pl.ds(8 + RIM, ROWS), :], 0.0)
        new = jnp.where(own, new, 0.0)
        old_image = rows_of(field, base, ROWS)
        totals[0] = totals[0] + block[channel, pl.ds(RIM, ROWS), :] * old
        totals[1] = totals[1] + old * old_image
        totals[2] = totals[2] + old_image * new
        totals[3] = totals[3] + new * new_image
        first[pl.ds(ROWS * channel, ROWS), :] = pltpu.roll(old, LANES - RIM, 1)[:, :COLS]
        second[pl.ds(ROWS * channel, ROWS), :] = pltpu.roll(new, LANES - RIM, 1)[:, :COLS]
    lane = lanes_of((1, 128))
    packed = jnp.zeros((1, 128), f32)
    for index, total in enumerate(totals):
        value = jnp.sum(jnp.sum(total, axis=0, keepdims=True), axis=1, keepdims=True)
        packed = jnp.where(lane == index, value, packed)
    partial[...] = packed


def couple(copies, second, before, partial, shared):
    product = second[...] * before[...]
    value = jnp.sum(jnp.sum(product, axis=0, keepdims=True), axis=1, keepdims=True)
    packed = partial[...] - jnp.where(lanes_of((1, 128)) == 3, 2.0 * value, 0.0)
    shared[...] = jnp.broadcast_to(packed[None], (copies, 1, 128))


def regroup(copies, received, shared):
    total = jnp.sum(received[...], axis=0, keepdims=True)
    shared[...] = jnp.broadcast_to(total, (copies, 1, 128))


def combine(received, first, second, solution_block):
    total = jnp.sum(received[...], axis=0)
    lane = lanes_of((1, 128))
    inner0, curve0, cross, curve_second = [
        jnp.sum(jnp.where(lane == index, total, 0.0), axis=1, keepdims=True) for index in range(4)
    ]
    step0 = inner0 / curve0
    inner1 = inner0 - 2.0 * step0 * curve0 + step0 * step0 * cross
    grow = 1.0 + inner1 / inner0
    curve1 = grow * grow * curve0 - 2.0 * grow * step0 * cross + step0 * step0 * curve_second
    step1 = inner1 / curve1
    solution_block[...] = (step0 + step1 * grow) * first[...] - (step1 * step0) * second[...]


def exchange(last, first, axis):
    count = lax.axis_size(axis)
    forward = [(i, i + 1) for i in range(count - 1)]
    backward = [(target, source) for source, target in forward]
    return lax.ppermute(last, axis, forward), lax.ppermute(first, axis, backward)


def shards(right_side, seam_mask, patch_inverse, row_coupling, col_coupling):
    frame_count, row_count, col_count = (lax.axis_size(axis) for axis in ("tm", "row", "col"))
    own_row, own_col = lax.axis_index("row"), lax.axis_index("col")
    block = right_side[:, 0]
    mask = seam_mask[0]
    screen_edge = jnp.where(seam_mask == 1, seam_screen, keep_screen).astype(f32)
    edge = jnp.concatenate([block, screen_edge], axis=0)
    low, high = exchange(edge[:, ROWS - RIM :], edge[:, :RIM], "row")

    rounded = lax.reduce_precision(patch_inverse, 8, 7)
    high_w = rounded.astype(bf16)
    low_w = (patch_inverse - rounded).astype(bf16)
    index = jnp.arange(PATCHES)
    kind = index % PATCH_ROWS
    patch_row = 2 * own_row + kind % 5 - 1
    patch_col = 16 * own_col + index // PATCH_ROWS - 1
    keep = (kind < 15) & (kind % 5 < 4) & (patch_row >= 0) & (patch_row < 2 * row_count)
    keep = keep & (patch_col >= 0) & (patch_col < 16 * col_count)
    keep = keep.astype(f32)[:, None]
    coarse_rows, coarse_cols = 2 * row_count, 16 * col_count
    row_of = 2 * own_row + (jnp.arange(SPREAD) - ROWS) // CELL
    lane_col = jnp.arange(LANES) - RIM
    lane_col = jnp.where(lane_col >= 320, lane_col - LANES, lane_col)
    col_of = 16 * own_col + lane_col // CELL
    row_pick = (row_of[:, None] == jnp.arange(coarse_rows)[None]).astype(f32)
    col_pick = (jnp.arange(coarse_cols)[:, None] == col_of[None]).astype(f32)
    swapped = row_coupling.reshape(coarse_rows, row_count, 2).transpose(0, 2, 1).reshape(coarse_rows, coarse_rows)
    row_spread = jnp.dot(row_pick, swapped, precision=highest)
    row_mix = swapped.reshape(row_count, 2, coarse_rows).transpose(1, 0, 2).reshape(coarse_rows, coarse_rows)
    col_turned = jnp.pad(col_coupling.T, ((0, 128 - coarse_cols), (0, 128 - coarse_cols)))
    col_spread = jnp.dot(col_turned[:, :coarse_cols], col_pick, precision=highest)
    place = jnp.stack([own_row, own_col]).astype(jnp.int32)

    tall, to_right, to_left, cells = call(
        assemble, [(4, TALL, LANES), (4, TALL, 128), (4, TALL, 128), (8, 128)]
    )(low, block, mask, high)
    left, right = exchange(to_right, to_left, "col")
    work = [
        pltpu.VMEM((PATCHES, 1024), bf16),
        pltpu.VMEM((PATCHES, 1024), bf16),
        pltpu.VMEM((PATCHES, 1024), f32),
    ]
    result, screen, share = call(
        first_apply,
        [(3, FLAT, 128), (TALL, LANES), (3 * ROWS + 8, LANES)],
        [pltpu.VMEM((3, FLAT, 128), f32)] + work,
    )(tall, left, right, cells, high_w, low_w, keep)
    before, after = exchange(share, share, "tm")
    image, message = call(first_image, [(3, ROWS, LANES), (1, LANES)])(result, before, after, screen, cells)
    low, high = exchange(image[:, ROWS - RIM :], image[:, :RIM], "row")
    peers = row_count * col_count
    gathered = lax.all_to_all(jnp.broadcast_to(message[None], (peers, 1, LANES)), ("row", "col"), 0, 0)
    gathered = gathered.reshape(peers, LANES)
    column = jnp.concatenate([low, image, high], axis=1)
    left, right = exchange(column[:, :, 256:], column[:, :, :128], "col")
    plain = pl.BlockSpec(memory_space=pltpu.VMEM)
    first, second, partial = pl.pallas_call(
        functools.partial(second_apply, row_count, col_count),
        out_shape=[
            jax.ShapeDtypeStruct((3 * ROWS, COLS), f32),
            jax.ShapeDtypeStruct((3 * ROWS, COLS), f32),
            jax.ShapeDtypeStruct((1, 128), f32),
        ],
        in_specs=[pl.BlockSpec(memory_space=pltpu.SMEM)] + [plain] * 16,
        out_specs=[plain] * 3,
        scratch_shapes=[pltpu.VMEM((3, FLAT, 128), f32)] * 2
        + work
        + [pltpu.VMEM((3, SPREAD, LANES), f32)] * 2
        + [pltpu.VMEM((3, peers, 128), f32)],
        compiler_params=pltpu.CompilerParams(vmem_limit_bytes=40 * 1024 * 1024),
    )(
        place, gathered, tall, result, image, low, high, left, right, screen, high_w, low_w, keep,
        row_mix, col_turned, row_spread, col_spread,
    )
    forward = [(i, i + 1) for i in range(frame_count - 1)]
    previous = lax.ppermute(second, "tm", forward)
    group = frame_count * col_count
    (shared,) = call(functools.partial(couple, group), [(group, 1, 128)])(second, previous, partial)
    received = lax.all_to_all(shared, ("tm", "col"), 0, 0)
    (shared,) = call(functools.partial(regroup, row_count), [(row_count, 1, 128)])(received)
    received = lax.all_to_all(shared, "row", 0, 0)
    (answer,) = call(combine, [(3 * ROWS, COLS)])(received, first, second)
    return answer.reshape(right_side.shape)


def solution(mesh):
    in_specs = (P(None, "tm", "row", "col"), P("tm", "row", "col"), P(), P(), P())
    out_specs = P(None, "tm", "row", "col")
    return jax.shard_map(shards, mesh=mesh, in_specs=in_specs, out_specs=out_specs, check_vma=False)
```

time: 563 us -> 142 us (0.25)
  blocking collectives: 396 us -> 35.6 us
  matrix products: 26.1 us -> 1.16 us
  starting transfers between devices: 79.1 us -> 54.4 us
  waiting for transfers between devices: 28.7 us -> 10.3 us
  Pallas kernels: 0 us -> 14.2 us
    psum x3 -> x0, blocking collectives: 323 us -> none  [the longest x2 222 us: inner_product(): return lax.psum(jnp.sum(left_vec * right_vec), ('tm', 'row', 'col'))]
    all_gather x4 -> x0, blocking collectives: 72.9 us -> none  [the longest x2 54.2 us: coarse_fix(): all_grid = lax.all_gather(all_cols, 'row', axis=2, tiled=True)]
    ppermute x28 -> x11, starting transfers between devices: 79.1 us -> 33.9 us  [the longest x5 21.4 us: exchange(): lax.ppermute(last, axis, forward)]
    all_to_all x0 -> x2, blocking collectives: none -> 35.6 us  [the longest x1 21.9 us: shards(): received = lax.all_to_all(shared, 'row', 0, 0)]
    dot_general x6 -> x2, matrix products: 26.1 us -> 1.16 us  [the longest x1 0.94 us: shards(): row_spread = jnp.dot(row_pick, swapped, precision=highest)]
    all_to_all x0 -> x1, starting transfers between devices: none -> 20.4 us  [shards(): lax.all_to_all(jnp.broadcast_to(message[None], (peers, 1, LANES)), ('row'...]
    ppermute x28 -> x11, waiting for transfers between devices: 28.7 us -> 9.85 us  [the longest x5 7.91 us: exchange(): lax.ppermute(first, axis, backward)]
    pallas_call x0 -> x7, Pallas kernels: none -> 14.2 us  [the longest x1 8.45 us: shards(): pl.pallas_call(functools.partial(second_apply, row_count, col_count), out...]
  transfers between devices with their start and end apart: 28 -> 12, of which waited for: 12 -> 5; matrix products, arithmetic and copies ran while one was open for 2% -> 12% of each run, Pallas kernels for 0% -> 0%
where the time goes in v2:
time: 142 us; the launch traced here: 141 us
  starting transfers between devices  54.4 us (38%)
  blocking collectives  35.6 us (25%)
  local copies, waits for them, and re-layouts  18.4 us (13%)
  Pallas kernels  14.2 us (10%)
  waiting for transfers between devices  10.3 us (7%)
  other arithmetic  6.49 us (5%)
    all_to_all x1, blocking collectives, shards(): received = lax.all_to_all(shared, 'row', 0, 0)  21.9 us
    ppermute x5, starting transfers between devices, exchange(): lax.ppermute(last, axis, forward)  21.4 us
    all_to_all x1, starting transfers between devices, shards(): lax.all_to_all(jnp.broadcast_to(message[None], (peers, 1, LANES)), ('row'...  20.4 us
    all_to_all x1, blocking collectives, shards(): received = lax.all_to_all(shared, ('tm', 'col'), 0, 0)  13.8 us
    unnamed x33, local copies, waits for them, and re-layouts  9.21 us
    pallas_call x1, Pallas kernels, shards(): pl.pallas_call(functools.partial(second_apply, row_count, col_count), out...  8.45 us
    ppermute x5, waiting for transfers between devices, exchange(): lax.ppermute(first, axis, backward)  7.91 us
    ppermute x5, starting transfers between devices, exchange(): lax.ppermute(first, axis, backward)  7.39 us
  transfers between devices with their start and end apart: 12, of which 5 were waited for; matrix products, arithmetic and copies ran while one was open for 12% of the time, Pallas kernels for 0%

profile of v2, /device:TPU:1, one launch (start us, length us, event | category | flops | bytes accessed | tf_op | source)
XLA Modules:
  0.0 141.0 jit_solution(5669508545158318611)
XLA Ops:
  0.8 1.0 pad_maximum_fusion
  1.7 4.4 %collective-permute-start = (f32[4,24,256]{2,1,0:T(8,128)S(1)}, f32[4,24,256]{2,1,0:T(8,128)S(1)}, u32[]{:S(2)}, u32[]{:S(2)}) collective-permute-start(f32[4,24,256]{2,1,0:T(8,128)S(1)} %get-tuple-element.36), channel_id=1, source_target_pairs={{0,4},{4,8},{8,12},{12,16},{16,20},{20,24},{24,28},{28,32},{32,36}... | collective-permute-start | bytes 294920 | tf_op jit(solution)/shard_map/ppermute | solution.py:317
  6.2 1.4 %collective-permute-start.1 = (f32[4,24,256]{2,1,0:T(8,128)S(1)}, f32[4,24,256]{2,1,0:T(8,128)S(1)}, u32[]{:S(2)}, u32[]{:S(2)}) collective-permute-start(f32[4,24,256]{2,1,0:T(8,128)S(1)} %get-tuple-element.35), channel_id=1, source_target_pairs={{4,0},{8,4},{12,8},{16,12},{20,16},{24,20},{28,24},{32,28},{36,32}... | collective-permute-start | bytes 294920 | tf_op jit(solution)/shard_map/ppermute | solution.py:317
  7.6 4.5 %fusion = (bf16[1024,1024]{1,0:T(8,128)(2,1)S(1)}, bf16[1024,1024]{1,0:T(8,128)(2,1)}) fusion(f32[1024,1024]{1,0:T(8,128)} %param.7), kind=kLoop, calls=%fused_computation.2 | loop fusion | flops 4194304 | bytes 8388608 | tf_op jit(solution)/shard_map/convert_element_type | solution.py:331
  12.9 3.1 %collective-permute-start.2 = (f32[4,80,128]{2,1,0:T(8,128)}, f32[4,80,128]{2,1,0:T(8,128)S(1)}, u32[]{:S(2)}, u32[]{:S(2)}) collective-permute-start(f32[4,80,128]{2,1,0:T(8,128)} %get-tuple-element.18), channel_id=1, source_target_pairs={{0,1},{1,2},{2,3},{4,5},{5,6},{6,7},{8,9},{9,10},{10,11},{12,13},{... | collective-permute-start | bytes 491528 | tf_op jit(solution)/shard_map/ppermute | solution.py:317
  16.1 1.3 collective-permute-start.3
  18.6 3.5 %collective-permute-done.3.right = f32[4,80,128]{2,1,0:T(8,128)S(1)} collective-permute-done((f32[4,80,128]{2,1,0:T(8,128)S(1)}, f32[4,80,128]{2,1,0:T(8,128)S(1)}, u32[]{:S(2)}, u32[]{:S(2)}) %collective-permute-start.3) | collective-permute-done | bytes 163872 | tf_op jit(solution)/shard_map/ppermute | solution.py:317
  22.8 1.6 %copy-done = bf16[1024,1024]{1,0:T(8,128)(2,1)S(1)} copy-done((bf16[1024,1024]{1,0:T(8,128)(2,1)S(1)}, bf16[1024,1024]{1,0:T(8,128)(2,1)}, u32[]{:S(2)}) %copy-start) | copy-done | bytes 2097176
  24.4 0.9 copy-done.7
  25.3 3.6 %shard_map.56 = (f32[3,272,128]{2,1,0:T(8,128)S(1)}, f32[80,384]{1,0:T(8,128)S(1)}, f32[104,384]{1,0:T(8,128)S(1)}) custom-call(f32[4,80,384]{2,1,0:T(8,128)S(1)} %get-tuple-element.17.tall.block, f32[4,80,128]{2,1,0:T(8,128)S(1)} %collective-permute-done.2.left, f32[4,80,128]{2,1,0:T(8,128)S(1)} %copy-done.7, f32[8,128]{1,0:T(8,128)S(1)} %get-tuple-element.20.cells, ...), custom_call_target="tpu_custom_call" | custom-call | tf_op jit(solution)/shard_map/pallas_call | solution.py:362
  28.9 6.2 %collective-permute-start.4 = (f32[104,384]{1,0:T(8,128)S(1)}, f32[104,384]{1,0:T(8,128)S(1)}, u32[]{:S(2)}, u32[]{:S(2)}) collective-permute-start(f32[104,384]{1,0:T(8,128)S(1)} %get-tuple-element.22), channel_id=1, source_target_pairs={{0,64},{64,128},{128,192},{192,256},{256,320},{320,384},{384,448},... | collective-permute-start | bytes 479240 | tf_op jit(solution)/shard_map/ppermute | solution.py:317
  35.1 1.9 %collective-permute-start.5 = (f32[104,384]{1,0:T(8,128)S(1)}, f32[104,384]{1,0:T(8,128)S(1)}, u32[]{:S(2)}, u32[]{:S(2)}) collective-permute-start(f32[104,384]{1,0:T(8,128)S(1)} %get-tuple-element.22), channel_id=1, source_target_pairs={{64,0},{128,64},{192,128},{256,192},{320,256},{384,320},{448,384},... | collective-permute-start | bytes 479240 | tf_op jit(solution)/shard_map/ppermute | solution.py:317
  37.3 4.4 %collective-permute-done.5.after = f32[104,384]{1,0:T(8,128)S(1)} collective-permute-done((f32[104,384]{1,0:T(8,128)S(1)}, f32[104,384]{1,0:T(8,128)S(1)}, u32[]{:S(2)}, u32[]{:S(2)}) %collective-permute-start.5) | collective-permute-done | bytes 159776 | tf_op jit(solution)/shard_map/ppermute | solution.py:317
  42.9 4.2 %collective-permute-start.6 = (f32[3,24,384]{2,1,0:T(8,128)}, f32[3,24,384]{2,1,0:T(8,128)}, u32[]{:S(2)}, u32[]{:S(2)}) collective-permute-start(f32[3,24,384]{2,1,0:T(8,128)} %get-tuple-element.34), channel_id=1, source_target_pairs={{0,4},{4,8},{8,12},{12,16},{16,20},{20,24},{24,28},{28,32},{32,36}... | collective-permute-start | bytes 331784 | tf_op jit(solution)/shard_map/ppermute | solution.py:317
  47.1 1.3 collective-permute-start.7
  49.1 20.4 %all-to-all-start = ((f32[64,1,384]{2,1,0:T(1,128)}), f32[64,1,384]{2,1,0:T(1,128)}, u32[]{:S(2)}, u32[]{:S(2)}) async-start(f32[64,1,384]{2,1,0:T(1,128)} %broadcast_in_dim.24), calls=%async_computation | async-start | bytes 196608 | tf_op jit(solution)/shard_map/all_to_all | solution.py:371
  69.6 0.9 constant_dynamic-update-slice_fusion.2
  70.5 0.9 constant_dynamic-update-slice_fusion
  72.1 3.5 %collective-permute-start.8 = (f32[3,80,128]{2,1,0:T(8,128)}, f32[3,80,128]{2,1,0:T(8,128)}, u32[]{:S(2)}, u32[]{:S(2)}) collective-permute-start(f32[3,80,128]{2,1,0:T(8,128)} %get-tuple-element.32), channel_id=1, source_target_pairs={{0,1},{1,2},{2,3},{4,5},{5,6},{6,7},{8,9},{9,10},{10,11},{12,13},{... | collective-permute-start | bytes 368648 | tf_op jit(solution)/shard_map/ppermute | solution.py:317
  75.6 1.5 %collective-permute-start.9 = (f32[3,80,128]{2,1,0:T(8,128)}, f32[3,80,128]{2,1,0:T(8,128)}, u32[]{:S(2)}, u32[]{:S(2)}) collective-permute-start(f32[3,80,128]{2,1,0:T(8,128)} %get-tuple-element.31), channel_id=1, source_target_pairs={{1,0},{2,1},{3,2},{5,4},{6,5},{7,6},{9,8},{10,9},{11,10},{13,12},{... | collective-permute-start | bytes 368648 | tf_op jit(solution)/shard_map/ppermute | solution.py:317
  77.1 0.9 fusion.25.row_spread
  78.0 1.4 %copy.26 = f32[32,2,16]{2,1,0:T(2,128)} copy(f32[32,2,16]{0,1,2:T(2,128)} %bitcast.26) | data formatting | bytes 8192 | tf_op jit(solution)/shard_map/transpose | solution.py:346
  79.4 1.4 pad.4.col_mix
  80.8 1.5 %reshape_reshape.3 = f32[16,2,32]{2,1,0:T(2,128)} reshape(f32[32,2,16]{2,1,0:T(2,128)} %copy.26) | data formatting | bytes 8192 | tf_op jit(solution)/shard_map/reshape;reshape | solution.py:348
  82.3 1.3 copy.27
  85.1 1.6 %copy-done.1 = bf16[1024,1024]{1,0:T(8,128)(2,1)S(1)} copy-done((bf16[1024,1024]{1,0:T(8,128)(2,1)S(1)}, bf16[1024,1024]{1,0:T(8,128)(2,1)}, u32[]{:S(2)}) %copy-start.1) | copy-done | bytes 2097176
  86.7 0.9 copy-done.3
  89.1 8.4 %shard_map.58 = (f32[96,256]{1,0:T(8,128)S(1)}, f32[96,256]{1,0:T(8,128)S(1)}, f32[1,128]{1,0:T(1,128)S(1)}) custom-call(s32[2]{0:T(128)S(1)} %pad_add_fusion.place, f32[64,384]{1,0:T(8,128)S(1)} %bitcast.20, f32[4,80,384]{2,1,0:T(8,128)S(1)} %get-tuple-element.17.tall.block, f32[3,272,128]{2,1,0:T(8,128)S(1)} %get-tuple-element.21.result, ...), custom_call_target="tpu_custom_call" | custom-call | tf_op jit(solution)/shard_map/pallas_call | solution.py:376
  97.6 5.2 %collective-permute-start.10 = (f32[96,256]{1,0:T(8,128)S(1)}, f32[96,256]{1,0:T(8,128)S(1)}, u32[]{:S(2)}, u32[]{:S(2)}) collective-permute-start(f32[96,256]{1,0:T(8,128)S(1)} %get-tuple-element.26.second), channel_id=1, source_target_pairs={{0,64},{64,128},{128,192},{192,256},{256,320},{320,384},{384,448},... | collective-permute-start | bytes 294920 | tf_op jit(solution)/shard_map/ppermute | solution.py:395
  102.8 1.6 %collective-permute-done.10.before = f32[96,256]{1,0:T(8,128)S(1)} collective-permute-done((f32[96,256]{1,0:T(8,128)S(1)}, f32[96,256]{1,0:T(8,128)S(1)}, u32[]{:S(2)}, u32[]{:S(2)}) %collective-permute-start.10) | collective-permute-done | bytes 98336 | tf_op jit(solution)/shard_map/ppermute | solution.py:395
  104.5 13.8 %all_to_all.15.received = f32[32,1,128]{2,1,0:T(1,128)S(1)} all-to-all(f32[32,1,128]{2,1,0:T(1,128)S(1)} %shard_map.59), channel_id=1, replica_groups=mesh['tm'=8,'row'=16,'col'=4] {'tm','col'}, dimensions={0} | all-to-all | bytes 32768 | tf_op jit(solution)/shard_map/all_to_all | solution.py:398
  118.3 21.9 %all_to_all.16.received = f32[16,1,128]{2,1,0:T(1,128)S(1)} all-to-all(f32[16,1,128]{2,1,0:T(1,128)S(1)} %shard_map.60), channel_id=1, replica_groups=mesh['tm'=8,'row'=16,'col'=4] {'row'}, dimensions={0} | all-to-all | bytes 16384 | tf_op jit(solution)/shard_map/all_to_all | solution.py:400
  (53 shorter events, 10.4 us)
Async XLA Ops:
  1.7 10.4 %collective-permute-start = (f32[4,24,256]{2,1,0:T(8,128)S(1)}, f32[4,24,256]{2,1,0:T(8,128)S(1)}, u32[]{:S(2)}, u32[]{:S(2)}) collective-permute-start(f32[4,24,256]{2,1,0:T(8,128)S(1)} %get-tuple-element.36), channel_id=1, source_target_pairs={{0,4},{4,8},{8,12},{12,16},{16,20},{20,24},{24,28},{28,32},{32,36}... | collective-permute-start | bytes 294920 | tf_op jit(solution)/shard_map/ppermute | solution.py:317
  6.1 6.0 %copy-start.4 = (f32[3,1,32,256]{3,2,1,0:T(8,128)S(1)}, f32[3,1,32,256]{3,2,1,0:T(8,128)}, u32[]{:S(2)}) copy-start(f32[3,1,32,256]{3,2,1,0:T(8,128)} %param.5) | copy-start | bytes 294916
  6.1 6.0 %copy-start.8 = (s32[1,32,256]{2,1,0:T(8,128)S(1)}, s32[1,32,256]{2,1,0:T(8,128)}, u32[]{:S(2)}) copy-start(s32[1,32,256]{2,1,0:T(8,128)} %param.6) | copy-start | bytes 98308
  6.1 11.2 %copy-start.12 = (f32[64,64]{1,0:T(8,128)S(1)}, f32[64,64]{1,0:T(8,128)}, u32[]{:S(2)}) copy-start(f32[64,64]{1,0:T(8,128)} %param.9) | copy-start | bytes 49156
  6.2 11.3 %copy-start.13 = (f32[32,32]{1,0:T(8,128)S(1)}, f32[32,32]{1,0:T(8,128)}, u32[]{:S(2)}) copy-start(f32[32,32]{1,0:T(8,128)} %param.8) | copy-start | bytes 12292
  6.2 5.9 %collective-permute-start.1 = (f32[4,24,256]{2,1,0:T(8,128)S(1)}, f32[4,24,256]{2,1,0:T(8,128)S(1)}, u32[]{:S(2)}, u32[]{:S(2)}) collective-permute-start(f32[4,24,256]{2,1,0:T(8,128)S(1)} %get-tuple-element.35), channel_id=1, source_target_pairs={{4,0},{8,4},{12,8},{16,12},{20,16},{24,20},{28,24},{32,28},{36,32}... | collective-permute-start | bytes 294920 | tf_op jit(solution)/shard_map/ppermute | solution.py:317
  12.9 5.7 %collective-permute-start.2 = (f32[4,80,128]{2,1,0:T(8,128)}, f32[4,80,128]{2,1,0:T(8,128)S(1)}, u32[]{:S(2)}, u32[]{:S(2)}) collective-permute-start(f32[4,80,128]{2,1,0:T(8,128)} %get-tuple-element.18), channel_id=1, source_target_pairs={{0,1},{1,2},{2,3},{4,5},{5,6},{6,7},{8,9},{9,10},{10,11},{12,13},{... | collective-permute-start | bytes 491528 | tf_op jit(solution)/shard_map/ppermute | solution.py:317
  16.1 6.1 %collective-permute-start.3 = (f32[4,80,128]{2,1,0:T(8,128)S(1)}, f32[4,80,128]{2,1,0:T(8,128)S(1)}, u32[]{:S(2)}, u32[]{:S(2)}) collective-permute-start(f32[4,80,128]{2,1,0:T(8,128)S(1)} %get-tuple-element.19), channel_id=1, source_target_pairs={{1,0},{2,1},{3,2},{5,4},{6,5},{7,6},{9,8},{10,9},{11,10},{13,12},{... | collective-permute-start | bytes 491528 | tf_op jit(solution)/shard_map/ppermute | solution.py:317
  17.5 24.2 %copy-start.10 = (f32[64,64]{0,1:T(8,128)}, f32[64,64]{0,1:T(8,128)S(1)}, u32[]{:S(2)}) copy-start(f32[64,64]{0,1:T(8,128)S(1)} %copy.28) | copy-start | bytes 49156
  17.6 19.4 %copy-start.11 = (f32[32,32]{0,1:T(8,128)}, f32[32,32]{0,1:T(8,128)S(1)}, u32[]{:S(2)}) copy-start(f32[32,32]{0,1:T(8,128)S(1)} %copy.25) | copy-start | bytes 12292
  22.1 0.7 copy-start.6
  22.8 1.6 %copy-start = (bf16[1024,1024]{1,0:T(8,128)(2,1)S(1)}, bf16[1024,1024]{1,0:T(8,128)(2,1)}, u32[]{:S(2)}) copy-start(bf16[1024,1024]{1,0:T(8,128)(2,1)} %get-tuple-element.30.high_w) | copy-start | bytes 6291460
  24.4 0.9 copy-start.7
  28.9 12.8 %copy-start.2 = (f32[80,384]{1,0:T(8,128)}, f32[80,384]{1,0:T(8,128)S(1)}, u32[]{:S(2)}) copy-start(f32[80,384]{1,0:T(8,128)S(1)} %get-tuple-element.23.screen) | copy-start | bytes 368644
  28.9 8.4 %collective-permute-start.4 = (f32[104,384]{1,0:T(8,128)S(1)}, f32[104,384]{1,0:T(8,128)S(1)}, u32[]{:S(2)}, u32[]{:S(2)}) collective-permute-start(f32[104,384]{1,0:T(8,128)S(1)} %get-tuple-element.22), channel_id=1, source_target_pairs={{0,64},{64,128},{128,192},{192,256},{256,320},{320,384},{384,448},... | collective-permute-start | bytes 479240 | tf_op jit(solution)/shard_map/ppermute | solution.py:317
  35.1 6.6 %collective-permute-start.5 = (f32[104,384]{1,0:T(8,128)S(1)}, f32[104,384]{1,0:T(8,128)S(1)}, u32[]{:S(2)}, u32[]{:S(2)}) collective-permute-start(f32[104,384]{1,0:T(8,128)S(1)} %get-tuple-element.22), channel_id=1, source_target_pairs={{64,0},{128,64},{192,128},{256,192},{320,256},{384,320},{448,384},... | collective-permute-start | bytes 479240 | tf_op jit(solution)/shard_map/ppermute | solution.py:317
  42.9 26.7 %collective-permute-start.6 = (f32[3,24,384]{2,1,0:T(8,128)}, f32[3,24,384]{2,1,0:T(8,128)}, u32[]{:S(2)}, u32[]{:S(2)}) collective-permute-start(f32[3,24,384]{2,1,0:T(8,128)} %get-tuple-element.34), channel_id=1, source_target_pairs={{0,4},{4,8},{8,12},{12,16},{16,20},{20,24},{24,28},{28,32},{32,36}... | collective-permute-start | bytes 331784 | tf_op jit(solution)/shard_map/ppermute | solution.py:317
  47.1 23.4 %collective-permute-start.7 = (f32[3,24,384]{2,1,0:T(8,128)}, f32[3,24,384]{2,1,0:T(8,128)}, u32[]{:S(2)}, u32[]{:S(2)}) collective-permute-start(f32[3,24,384]{2,1,0:T(8,128)} %get-tuple-element.33), channel_id=1, source_target_pairs={{4,0},{8,4},{12,8},{16,12},{20,16},{24,20},{28,24},{32,28},{36,32}... | collective-permute-start | bytes 331784 | tf_op jit(solution)/shard_map/ppermute | solution.py:317
  49.1 35.1 %all-to-all-start = ((f32[64,1,384]{2,1,0:T(1,128)}), f32[64,1,384]{2,1,0:T(1,128)}, u32[]{:S(2)}, u32[]{:S(2)}) async-start(f32[64,1,384]{2,1,0:T(1,128)} %broadcast_in_dim.24), calls=%async_computation | async-start | bytes 196608 | tf_op jit(solution)/shard_map/all_to_all | solution.py:371
  72.1 12.9 %collective-permute-start.8 = (f32[3,80,128]{2,1,0:T(8,128)}, f32[3,80,128]{2,1,0:T(8,128)}, u32[]{:S(2)}, u32[]{:S(2)}) collective-permute-start(f32[3,80,128]{2,1,0:T(8,128)} %get-tuple-element.32), channel_id=1, source_target_pairs={{0,1},{1,2},{2,3},{4,5},{5,6},{6,7},{8,9},{9,10},{10,11},{12,13},{... | collective-permute-start | bytes 368648 | tf_op jit(solution)/shard_map/ppermute | solution.py:317
  75.6 9.5 %collective-permute-start.9 = (f32[3,80,128]{2,1,0:T(8,128)}, f32[3,80,128]{2,1,0:T(8,128)}, u32[]{:S(2)}, u32[]{:S(2)}) collective-permute-start(f32[3,80,128]{2,1,0:T(8,128)} %get-tuple-element.31), channel_id=1, source_target_pairs={{1,0},{2,1},{3,2},{5,4},{6,5},{7,6},{9,8},{10,9},{11,10},{13,12},{... | collective-permute-start | bytes 368648 | tf_op jit(solution)/shard_map/ppermute | solution.py:317
  85.1 1.6 %copy-start.1 = (bf16[1024,1024]{1,0:T(8,128)(2,1)S(1)}, bf16[1024,1024]{1,0:T(8,128)(2,1)}, u32[]{:S(2)}) copy-start(bf16[1024,1024]{1,0:T(8,128)(2,1)} %get-tuple-element.30.high_w) | copy-start | bytes 6291460
  86.7 0.9 copy-start.3
  87.6 0.8 copy-start.5
  88.4 0.7 copy-start.9
  97.6 6.8 %collective-permute-start.10 = (f32[96,256]{1,0:T(8,128)S(1)}, f32[96,256]{1,0:T(8,128)S(1)}, u32[]{:S(2)}, u32[]{:S(2)}) collective-permute-start(f32[96,256]{1,0:T(8,128)S(1)} %get-tuple-element.26.second), channel_id=1, source_target_pairs={{0,64},{64,128},{128,192},{192,256},{256,320},{320,384},{384,448},... | collective-permute-start | bytes 294920 | tf_op jit(solution)/shard_map/ppermute | solution.py:395

commit v3 on v2

v3 whole, which is shorter than its diff:
```python
import functools

import jax
import jax.numpy as jnp
from jax import lax
from jax.experimental import pallas as pl
from jax.experimental.pallas import tpu as pltpu
from jax.sharding import PartitionSpec as P

CELL = 16
RIM = 24
SIDE = 56
seam_screen = 0.1
keep_screen = 2.0
highest = lax.Precision.HIGHEST
f32 = jnp.float32
bf16 = jnp.bfloat16

ROWS = 32
COLS = 256
TALL = ROWS + 2 * RIM
LANES = 384
PATCH_ROWS = 16
PATCH_COLS = 22
PATCHES = PATCH_ROWS * PATCH_COLS
FLAT = 272
SPREAD = 96


def call(body, outs, kinds, scratch=(), limit=8):
    specs = [pl.BlockSpec(memory_space=pltpu.SMEM) if kind == "s" else pl.BlockSpec() for kind in kinds]
    return pl.pallas_call(
        body,
        out_shape=[jax.ShapeDtypeStruct(shape, f32) for shape in outs],
        in_specs=specs,
        scratch_shapes=list(scratch),
        compiler_params=pltpu.CompilerParams(vmem_limit_bytes=limit * 1024 * 1024),
    )


def lanes_of(shape):
    return lax.broadcasted_iota(jnp.int32, shape, len(shape) - 1)


def rows_of(ref, start, count):
    return jnp.concatenate([ref[group, pl.ds(start, count), :] for group in range(3)], axis=1)


def put_rows(ref, start, count, value):
    for group in range(3):
        ref[group, pl.ds(start, count), :] = value[:, 128 * group : 128 * group + 128]


def stripe_of(ref, start):
    return jnp.concatenate([ref.at[group][pl.ds(start, PATCH_ROWS, stride=CELL), :] for group in range(3)], axis=1)


def swap_blocks(parts):
    lane = lanes_of(parts[0].shape)
    for step in (1, 2):
        taken = (lane // (32 * step)) % 2 == 1
        fresh = list(parts)
        for low in range(4):
            if low & step:
                continue
            first, second = parts[low], parts[low + step]
            fresh[low] = jnp.where(taken, pltpu.roll(second, 32 * step, 1), first)
            fresh[low + step] = jnp.where(taken, second, pltpu.roll(first, 128 - 32 * step, 1))
        parts = fresh
    return parts


def patch_apply(span_of, field, result, inverse, high_w, low_w, keep, high_x, low_x, solved):
    start, stop = span_of
    used = pl.ds(0, PATCH_ROWS * (stop - start))

    for block in range(8):
        slabs = [stripe_of(field, 4 * block + row) for row in range(4)]
        for parity in range(2):
            if parity:
                slabs = [pltpu.roll(slab, LANES - CELL, 1) for slab in slabs]
            for group in range(3):
                parts = swap_blocks([slab[:, 128 * group : 128 * group + 128] for slab in slabs])
                for inner in range(4):
                    place = 8 * group + 2 * inner + parity
                    if not start <= place < stop:
                        continue
                    upper = parts[inner].astype(bf16)
                    lower = (parts[inner] - upper.astype(f32)).astype(bf16)
                    where = (pl.ds(PATCH_ROWS * (place - start), PATCH_ROWS), pl.ds(128 * block, 128))
                    high_x[where] = upper
                    low_x[where] = lower
    for part in range(16):
        span = pl.ds(64 * part, 64)
        upper = inverse[span, :].astype(bf16)
        high_w[span, :] = upper
        low_w[span, :] = (inverse[span, :] - upper.astype(f32)).astype(bf16)
    for part in range(4):
        span = pl.ds(256 * part, 256)
        dot = functools.partial(jnp.dot, preferred_element_type=f32)
        total = dot(high_x[used, :], high_w[:, span]) + dot(high_x[used, :], low_w[:, span])
        total = total + dot(low_x[used, :], high_w[:, span])
        solved[used, span] = total * keep[pl.ds(PATCH_ROWS * start, PATCH_ROWS * (stop - start)), :]
    put_rows(result, FLAT - CELL, CELL, jnp.zeros((CELL, LANES), f32))
    for block in range(8):
        sums = None
        for parity in range(2):
            slabs = [[] for _ in range(4)]
            for group in range(3):
                parts = []
                for inner in range(4):
                    place = 8 * group + 2 * inner + parity
                    if not start <= place < stop:
                        parts.append(jnp.zeros((PATCH_ROWS, 128), f32))
                    else:
                        parts.append(solved[pl.ds(PATCH_ROWS * (place - start), PATCH_ROWS), pl.ds(128 * block, 128)])
                for row, piece in enumerate(swap_blocks(parts)):
                    slabs[row].append(piece)
            wide = [jnp.concatenate(pieces, axis=1) for pieces in slabs]
            if parity:
                sums = [total + pltpu.roll(slab, CELL, 1) for total, slab in zip(sums, wide)]
            else:
                sums = wide
        for row in range(4):
            total = sums[row]
            if block >= 4:
                total = total + stripe_of(result, 4 * block + row)
            for group in range(3):
                spot = pl.ds(4 * block + row, PATCH_ROWS, stride=CELL)
                result.at[group][spot, :] = total[:, 128 * group : 128 * group + 128]


def inside_of(place, row_count, col_count, rim):
    row = lax.broadcasted_iota(jnp.int32, (TALL, LANES), 0) + (place[0] * ROWS - RIM)
    lane = lanes_of((TALL, LANES))
    col = lane + (place[1] * COLS - SIDE)
    near = (lane >= SIDE - rim) & (lane < SIDE + COLS + rim)
    return (row >= 0) & (row < ROWS * row_count) & (col >= 0) & (col < COLS * col_count) & near


def merge_sides(middle, left, right):
    lane = lanes_of(left.shape)
    first = jnp.where(lane < SIDE, left, middle[:, :128])
    last = jnp.where((lane >= SIDE) & (lane < 2 * SIDE), right, middle[:, 256:])
    return jnp.concatenate([first, middle[:, 128:256], last], axis=1)


def cell_sums(blocks):
    rows = [jnp.sum(block[CELL * half : CELL * half + CELL], axis=0, keepdims=True) for block in blocks for half in range(2)]
    lane = lax.broadcasted_iota(jnp.int32, (LANES, 128), 0) - SIDE
    cell = lanes_of((LANES, 128))
    inside = (lane >= CELL * cell) & (lane < CELL * cell + CELL) & (cell < COLS // CELL)
    stacked = jnp.concatenate(rows, axis=0)
    return jnp.dot(stacked, inside.astype(f32), precision=highest, preferred_element_type=f32)


def assemble(low, block, mask, high, tall, to_right, to_left, cells):
    own = []
    for channel in range(4):
        if channel < 3:
            middle = block[channel]
        else:
            middle = jnp.where(mask[...] == 1, seam_screen, keep_screen).astype(f32)
        column = jnp.concatenate([low[channel], middle, high[channel]], axis=0)
        wide = jnp.concatenate([column, jnp.zeros((TALL, 128), f32)], axis=1)
        wide = pltpu.roll(wide, SIDE, 1)
        tall[channel] = wide
        to_right[channel] = wide[:, 256:]
        to_left[channel] = wide[:, :128]
        own.append(wide[RIM : RIM + ROWS])
    cells[...] = cell_sums(own)


def prepare(row_count, col_count, place, row_coupling, col_coupling, row_mix, row_spread, col_mix, col_spread, keep):
    dot = functools.partial(jnp.dot, precision=highest, preferred_element_type=f32)
    turned = functools.partial(
        lax.dot_general, dimension_numbers=(((1,), (1,)), ((), ())), precision=highest, preferred_element_type=f32
    )
    coarse_rows, coarse_cols = 2 * row_count, CELL * col_count

    def matrix(shape, rule):
        return rule(lax.broadcasted_iota(jnp.int32, shape, 0), lanes_of(shape)).astype(f32)

    order = matrix((coarse_rows, coarse_rows), lambda i, j: (j // 2 == i % row_count) & (j % 2 == i // row_count))
    swapped = turned(row_coupling[...], order)
    row_mix[...] = dot(order, swapped)
    row_pick = matrix((SPREAD, coarse_rows), lambda i, j: (i + place[0] * ROWS - ROWS + CELL * 2) // CELL - 2 == j)
    row_spread[...] = dot(row_pick, swapped)
    col_turned = turned(matrix((128, coarse_cols), lambda i, j: i == j), col_coupling[...])
    col_mix[...] = dot(col_turned, matrix((coarse_cols, 128), lambda i, j: i == j))

    def column(cell, lane):
        col = lane + (place[1] * COLS - SIDE)
        return (col >= CELL * cell) & (col < CELL * cell + CELL)

    col_spread[...] = dot(col_turned, matrix((coarse_cols, LANES), column))
    index = lax.broadcasted_iota(jnp.int32, (PATCHES, 1), 0)
    kind = index % PATCH_ROWS
    patch_row = 2 * place[0] + kind % 5 - 1
    patch_col = CELL * place[1] + index // PATCH_ROWS - 3
    kept = (kind < 15) & (kind % 5 < 4) & (patch_row >= 0) & (patch_row < coarse_rows)
    keep[...] = (kept & (patch_col >= 0) & (patch_col < coarse_cols)).astype(f32)


def edges(block, mask, last, first):
    for channel in range(3):
        last[channel] = block[channel, ROWS - RIM :]
        first[channel] = block[channel, :RIM]
    screen = jnp.where(mask[...] == 1, seam_screen, keep_screen).astype(f32)
    last[3] = screen[ROWS - RIM :]
    first[3] = screen[:RIM]


def first_apply(
    row_count, col_count, place, tall, left, right, cells, inverse, keep, result, screen, share,
    field, high_x, low_x, solved, high_w, low_w,
):
    put_rows(field, 240, FLAT - 240, jnp.zeros((FLAT - 240, LANES), f32))
    for channel in range(3):
        put_rows(field, TALL * channel, TALL, merge_sides(tall[channel], left[channel], right[channel]))
    screen[...] = merge_sides(tall[3], left[3], right[3])
    patch_apply((0, PATCH_COLS), field, result, inverse, high_w, low_w, keep, high_x, low_x, solved)
    inside = inside_of(place, row_count, col_count, 40)
    for channel in range(3):
        whole = rows_of(result, TALL * channel, TALL)
        put_rows(result, TALL * channel, TALL, jnp.where(inside, whole, 0.0))
        share[pl.ds(ROWS * channel, ROWS), :] = rows_of(result, TALL * channel + RIM, ROWS)
    share[pl.ds(3 * ROWS, 8), :] = jnp.concatenate([cells[...], jnp.zeros((8, 256), f32)], axis=1)


def first_image(copies, row_count, col_count, place, result, before, after, screen, cells, image, last, first, message):
    inside = inside_of(place, row_count, col_count, RIM)[RIM : RIM + ROWS]
    blocks = []
    for channel in range(3):
        base = TALL * channel + RIM
        center = rows_of(result, base, ROWS)
        near = rows_of(result, base - 1, ROWS) + rows_of(result, base + 1, ROWS)
        near = near + pltpu.roll(center, 1, 1) + pltpu.roll(center, LANES - 1, 1)
        span = pl.ds(ROWS * channel, ROWS)
        value = (screen[pl.ds(RIM, ROWS), :] + 6.0) * center - near - before[span, :] - after[span, :]
        value = jnp.where(inside, value, 0.0)
        image[channel] = value
        last[channel] = value[ROWS - RIM :]
        first[channel] = value[:RIM]
        blocks.append(value)
    sums = cell_sums(blocks)
    beside = before[pl.ds(3 * ROWS, 8), :128] + after[pl.ds(3 * ROWS, 8), :128]
    rows = [cells[0:6], beside[0:6], sums, cells[6:8]]
    rows = [part[row : row + 1] for part in rows for row in range(part.shape[0])]
    lane = lanes_of((1, 128))
    packed = []
    for group in range(3):
        total = jnp.zeros((1, 128), f32)
        for spot in range(8):
            if 8 * group + spot < len(rows):
                row = rows[8 * group + spot]
                row = pltpu.roll(row, CELL * spot, 1) if spot else row
                total = jnp.where(lane // CELL == spot, row, total)
        packed.append(total)
    message[...] = jnp.broadcast_to(jnp.concatenate(packed, axis=1)[None], (copies, 1, LANES))


def second_apply(
    row_count, col_count, place, gathered, block, result, image, low, high, screen, inverse,
    keep, row_mix, col_mix, row_spread, col_spread, first, second, partial,
    field, output, high_x, low_x, solved, high_w, low_w, coarse, beside, late, letters,
):
    dot = functools.partial(jnp.dot, precision=highest, preferred_element_type=f32)
    coarse_rows = 2 * row_count
    lane = lanes_of((row_count, 128))
    for group in range(3):
        letters[group] = gathered[:, 0, 128 * group : 128 * group + 128]

    def grid_of(index):
        halves = []
        for half in range(2):
            chunk = 2 * index + half
            total = jnp.zeros((row_count, 128), f32)
            for col in range(col_count):
                piece = letters.at[chunk // 8][pl.ds(col, row_count, stride=col_count), :]
                shift = (CELL * col - CELL * (chunk % 8)) % 128
                piece = pltpu.roll(piece, shift, 1) if shift else piece
                total = jnp.where(lane // CELL == col, piece, total)
            halves.append(total)
        return jnp.concatenate(halves, axis=0)

    def beside_each_other(tall, width):
        count = tall.shape[0] // coarse_rows
        return jnp.concatenate([tall[coarse_rows * i : coarse_rows * (i + 1)] for i in range(count)], axis=1)

    def spread(tall, targets):
        wide = dot(row_spread[...], beside_each_other(dot(tall, col_spread[...]), LANES))
        for index, (ref, channel) in enumerate(targets):
            ref[channel] = wide[:, LANES * index : LANES * (index + 1)]

    screen_cells = grid_of(9)
    grid_lane = lanes_of((coarse_rows, 128))
    zero_row = jnp.zeros((1, 128), f32)
    inside = inside_of(place, row_count, col_count, RIM)
    tall_lane = lanes_of((ROWS, LANES))
    own = (tall_lane >= SIDE) & (tall_lane < SIDE + COLS)
    put_rows(field, 240, FLAT - 240, jnp.zeros((FLAT - 240, LANES), f32))
    sums = jnp.concatenate([grid_of(index) for index in range(6)], axis=0)
    spread(sums, [(coarse, 0), (coarse, 1), (coarse, 2), (beside, 0), (beside, 1), (beside, 2)])
    for channel in range(3):
        center = coarse[channel, pl.ds(8, TALL), :]
        near = coarse[channel, pl.ds(7, TALL), :] + coarse[channel, pl.ds(9, TALL), :]
        near = near + pltpu.roll(center, 1, 1) + pltpu.roll(center, LANES - 1, 1)
        value = (screen[...] + 6.0) * center - near - beside[channel, pl.ds(8, TALL), :]
        middle = jnp.concatenate([low[channel], image[channel], high[channel]], axis=0)
        value = value + middle
        put_rows(field, TALL * channel, TALL, jnp.where(inside, value, 0.0))
    levels = dot(row_mix[...], beside_each_other(dot(sums, col_mix[...]), 128))
    late_sums = []
    for channel in range(3):
        level = levels[:, 128 * channel : 128 * channel + 128]
        level_beside = levels[:, 384 + 128 * channel : 512 + 128 * channel]
        even, odd = level[:row_count], level[row_count:]
        above = jnp.concatenate([zero_row, odd[:-1], even], axis=0)
        below = jnp.concatenate([odd, even[1:], zero_row], axis=0)
        before = jnp.where(grid_lane == 0, 0.0, pltpu.roll(level, 1, 1))
        after = jnp.where(grid_lane == CELL * col_count - 1, 0.0, pltpu.roll(level, 127, 1))
        image_sums = grid_of(6 + channel) + (screen_cells + 576.0) * level
        late_sums.append(image_sums - 16.0 * (above + below + before + after) - 256.0 * level_beside)
    spread(jnp.concatenate(late_sums, axis=0), [(late, 0), (late, 1), (late, 2)])
    patch_apply((2, PATCH_COLS - 2), field, output, inverse, high_w, low_w, keep, high_x, low_x, solved)
    totals = [jnp.zeros((ROWS, LANES), f32) for _ in range(4)]
    for channel in range(3):
        whole = rows_of(output, TALL * channel, TALL) + late[channel, pl.ds(8, TALL), :]
        put_rows(output, TALL * channel, TALL, jnp.where(inside, whole, 0.0))
        base = TALL * channel + RIM
        new = rows_of(output, base, ROWS)
        near = rows_of(output, base - 1, ROWS) + rows_of(output, base + 1, ROWS)
        near = near + pltpu.roll(new, 1, 1) + pltpu.roll(new, LANES - 1, 1)
        new_image = (screen[pl.ds(RIM, ROWS), :] + 6.0) * new - near
        old = jnp.where(own, rows_of(result, base, ROWS) + coarse[channel, pl.ds(8 + RIM, ROWS), :], 0.0)
        new = jnp.where(own, new, 0.0)
        old_image = jnp.where(own, rows_of(field, base, ROWS), 0.0)
        totals[0] = totals[0] + block[channel, pl.ds(RIM, ROWS), :] * old
        totals[1] = totals[1] + old * old_image
        totals[2] = totals[2] + old_image * new
        totals[3] = totals[3] + new * new_image
        first[pl.ds(ROWS * channel, ROWS), :] = pltpu.roll(old, LANES - SIDE, 1)[:, :COLS]
        second[pl.ds(ROWS * channel, ROWS), :] = pltpu.roll(new, LANES - SIDE, 1)[:, :COLS]
    lane = lanes_of((1, 128))
    packed = jnp.zeros((1, 128), f32)
    for index, total in enumerate(totals):
        value = jnp.sum(jnp.sum(total, axis=0, keepdims=True), axis=1, keepdims=True)
        packed = jnp.where(lane == index, value, packed)
    partial[...] = packed


def couple(copies, second, before, partial, shared):
    product = second[...] * before[...]
    value = jnp.sum(jnp.sum(product, axis=0, keepdims=True), axis=1, keepdims=True)
    packed = partial[...] - jnp.where(lanes_of((1, 128)) == 3, 2.0 * value, 0.0)
    shared[...] = jnp.broadcast_to(packed[None], (copies, 1, 128))


def regroup(copies, received, shared):
    total = jnp.sum(received[...], axis=0, keepdims=True)
    shared[...] = jnp.broadcast_to(total, (copies, 1, 128))


def combine(received, first, second, solution_block):
    total = jnp.sum(received[...], axis=0)
    lane = lanes_of((1, 128))
    inner0, curve0, cross, curve_second = [
        jnp.sum(jnp.where(lane == index, total, 0.0), axis=1, keepdims=True) for index in range(4)
    ]
    step0 = inner0 / curve0
    inner1 = inner0 - 2.0 * step0 * curve0 + step0 * step0 * cross
    grow = 1.0 + inner1 / inner0
    curve1 = grow * grow * curve0 - 2.0 * grow * step0 * cross + step0 * step0 * curve_second
    step1 = inner1 / curve1
    solution_block[...] = (step0 + step1 * grow) * first[...] - (step1 * step0) * second[...]


def exchange(last, first, axis):
    count = lax.axis_size(axis)
    forward = [(i, i + 1) for i in range(count - 1)]
    backward = [(target, source) for source, target in forward]
    return lax.ppermute(last, axis, forward), lax.ppermute(first, axis, backward)


def shards(right_side, seam_mask, patch_inverse, row_coupling, col_coupling):
    frame_count, row_count, col_count = (lax.axis_size(axis) for axis in ("tm", "row", "col"))
    peers = row_count * col_count
    coarse_rows = 2 * row_count
    place = jnp.stack([lax.axis_index("row"), lax.axis_index("col")]).astype(jnp.int32)
    block = right_side.reshape(3, ROWS, COLS)
    mask = seam_mask.reshape(ROWS, COLS)
    last, first = call(edges, [(4, RIM, COLS)] * 2, "vv")(block, mask)
    low, high = exchange(last, first, "row")

    mixers = call(
        functools.partial(prepare, row_count, col_count),
        [(coarse_rows, coarse_rows), (SPREAD, coarse_rows), (128, 128), (128, LANES), (PATCHES, 1)],
        "svv",
    )(place, row_coupling, col_coupling)

    tall, to_right, to_left, cells = call(
        assemble, [(4, TALL, LANES), (4, TALL, 128), (4, TALL, 128), (8, 128)], "hhhh"
    )(low, block, mask, high)
    left, right = exchange(to_right, to_left, "col")
    left, right, *mixers = lax.optimization_barrier((left, right, *mixers))
    row_mix, row_spread, col_mix, col_spread, keep = mixers
    work = [
        pltpu.VMEM((PATCHES, 1024), bf16),
        pltpu.VMEM((PATCHES, 1024), bf16),
        pltpu.VMEM((PATCHES, 1024), f32),
        pltpu.VMEM((1024, 1024), bf16),
        pltpu.VMEM((1024, 1024), bf16),
    ]
    flat = pltpu.VMEM((3, FLAT, 128), f32)
    result, screen, share = call(
        functools.partial(first_apply, row_count, col_count),
        [(3, FLAT, 128), (TALL, LANES), (3 * ROWS + 8, LANES)],
        "svvvvvv",
        [flat] + work,
        16,
    )(place, tall, left, right, cells, patch_inverse, keep)
    before, after = exchange(share, share, "tm")
    image, last, first, message = call(
        functools.partial(first_image, peers, row_count, col_count),
        [(3, ROWS, LANES), (3, RIM, LANES), (3, RIM, LANES), (peers, 1, LANES)],
        "svvvvv",
    )(place, result, before, after, screen, cells)
    low, high = exchange(last, first, "row")
    message, low, high = lax.optimization_barrier((message, low, high))
    gathered = lax.all_to_all(message, ("row", "col"), 0, 0)
    first, second, partial = call(
        functools.partial(second_apply, row_count, col_count),
        [(3 * ROWS, COLS), (3 * ROWS, COLS), (1, 128)],
        "s" + "v" * 13,
        [flat] * 2 + work + [pltpu.VMEM((3, SPREAD, LANES), f32)] * 3 + [pltpu.VMEM((3, peers, 128), f32)],
        20,
    )(
        place, gathered, tall, result, image, low, high, screen, patch_inverse, keep,
        row_mix, col_mix, row_spread, col_spread,
    )
    forward = [(i, i + 1) for i in range(frame_count - 1)]
    previous = lax.ppermute(second, "tm", forward)
    (shared,) = call(functools.partial(couple, frame_count), [(frame_count, 1, 128)], "vvv")(second, previous, partial)
    received = lax.all_to_all(shared, "tm", 0, 0)
    (shared,) = call(functools.partial(regroup, peers), [(peers, 1, 128)], "v")(received)
    received = lax.all_to_all(shared, ("row", "col"), 0, 0)
    (answer,) = call(combine, [(3 * ROWS, COLS)], "vvv")(received, first, second)
    return answer.reshape(right_side.shape)


def solution(mesh):
    in_specs = (P(None, "tm", "row", "col"), P("tm", "row", "col"), P(), P(), P())
    out_specs = P(None, "tm", "row", "col")
    return jax.shard_map(shards, mesh=mesh, in_specs=in_specs, out_specs=out_specs, check_vma=False)
```

time: 142 us -> 125 us (0.88)
  starting transfers between devices: 54.4 us -> 28.2 us
  blocking collectives: 35.6 us -> 60 us
  local copies, waits for them, and re-layouts: 18.4 us -> 5.32 us
  other arithmetic: 6.49 us -> 0.08 us
  waiting for transfers between devices: 10.3 us -> 15.4 us
    all_to_all x2 -> x3, blocking collectives: 35.6 us -> 60 us  [the longest x1 32.5 us: shards(): gathered = lax.all_to_all(message, ('row', 'col'), 0, 0)]
    all_to_all x1 -> x0, starting transfers between devices: 20.4 us -> none  [shards(): lax.all_to_all(jnp.broadcast_to(message[None], (peers, 1, LANES)), ('row'...]
    ppermute x5 -> x4, starting transfers between devices: 21.4 us -> 13.4 us  [exchange(): lax.ppermute(last, axis, forward)]
    convert_element_type x2 -> x0, other arithmetic: 4.64 us -> none  [the longest x1 4.48 us: shards(): low_w = (patch_inverse - rounded).astype(bf16)]
    ppermute x5 -> x4, waiting for transfers between devices: 7.91 us -> 11.9 us  [exchange(): lax.ppermute(first, axis, backward)]
    unnamed x33 -> x12, local copies, waits for them, and re-layouts: 9.21 us -> 5.32 us
    transpose x3 -> x0, local copies, waits for them, and re-layouts: 3.34 us -> none  [the longest x2 2.02 us: shards(): row_coupling.reshape(coarse_rows, row_count, 2).transpose(0, 2, 1)]
    ppermute x5 -> x4, starting transfers between devices: 7.39 us -> 9.87 us  [exchange(): lax.ppermute(first, axis, backward)]
  transfers between devices with their start and end apart: 12 -> 9, of which waited for: 5 -> 8; matrix products, arithmetic and copies ran while one was open for 12% -> 0% of each run, Pallas kernels for 0% -> 1%
where the time goes in v3:
time: 125 us; the launch traced here: 124 us
  blocking collectives  60 us (48%)
  starting transfers between devices  28.2 us (23%)
  waiting for transfers between devices  15.4 us (12%)
  Pallas kernels  14.9 us (12%)
  local copies, waits for them, and re-layouts  5.32 us (4%)
    all_to_all x1, blocking collectives, shards(): gathered = lax.all_to_all(message, ('row', 'col'), 0, 0)  32.5 us
    all_to_all x1, blocking collectives, shards(): received = lax.all_to_all(shared, ('row', 'col'), 0, 0)  17.4 us
    ppermute x4, starting transfers between devices, exchange(): lax.ppermute(last, axis, forward)  13.4 us
    ppermute x4, waiting for transfers between devices, exchange(): lax.ppermute(first, axis, backward)  11.9 us
    all_to_all x1, blocking collectives, shards(): received = lax.all_to_all(shared, 'tm', 0, 0)  10.1 us
    ppermute x4, starting transfers between devices, exchange(): lax.ppermute(first, axis, backward)  9.87 us
    pallas_call x1, Pallas kernels, shards(): call(functools.partial(second_apply, row_count, col_count), [(3 * ROWS, C...  6.33 us
    unnamed x12, local copies, waits for them, and re-layouts  5.32 us
  transfers between devices with their start and end apart: 9, of which 8 were waited for; matrix products, arithmetic and copies ran while one was open for 0% of the time, Pallas kernels for 1%

profile of v3, /device:TPU:1, one launch (start us, length us, event | category | flops | bytes accessed | tf_op | source)
XLA Modules:
  0.0 124.0 jit_solution(9638997652147747168)
XLA Ops:
  0.0 0.9 copy-done.2
  0.9 0.8 copy-done.3
  1.7 4.4 %collective-permute-start = (f32[4,24,256]{2,1,0:T(8,128)S(1)}, f32[4,24,256]{2,1,0:T(8,128)S(1)}, u32[]{:S(2)}, u32[]{:S(2)}) collective-permute-start(f32[4,24,256]{2,1,0:T(8,128)S(1)} %get-tuple-element.36), channel_id=1, source_target_pairs={{0,4},{4,8},{8,12},{12,16},{16,20},{20,24},{24,28},{28,32},{32,36}... | collective-permute-start | bytes 294920 | tf_op jit(solution)/shard_map/ppermute | solution.py:383
  6.1 1.3 %collective-permute-start.1 = (f32[4,24,256]{2,1,0:T(8,128)S(1)}, f32[4,24,256]{2,1,0:T(8,128)S(1)}, u32[]{:S(2)}, u32[]{:S(2)}) collective-permute-start(f32[4,24,256]{2,1,0:T(8,128)S(1)} %get-tuple-element.37), channel_id=1, source_target_pairs={{4,0},{8,4},{12,8},{16,12},{20,16},{24,20},{28,24},{32,28},{36,32}... | collective-permute-start | bytes 294920 | tf_op jit(solution)/shard_map/ppermute | solution.py:383
  7.4 0.3 collective-permute-done.low
  7.7 3.9 %collective-permute-done.1.high = f32[4,24,256]{2,1,0:T(8,128)S(1)} collective-permute-done((f32[4,24,256]{2,1,0:T(8,128)S(1)}, f32[4,24,256]{2,1,0:T(8,128)S(1)}, u32[]{:S(2)}, u32[]{:S(2)}) %collective-permute-start.1) | collective-permute-done | bytes 98336 | tf_op jit(solution)/shard_map/ppermute | solution.py:383
  11.6 0.3 shard_map.56
  11.9 3.1 %collective-permute-start.2 = (f32[4,80,128]{2,1,0:T(8,128)S(1)}, f32[4,80,128]{2,1,0:T(8,128)S(1)}, u32[]{:S(2)}, u32[]{:S(2)}) collective-permute-start(f32[4,80,128]{2,1,0:T(8,128)S(1)} %get-tuple-element.39), channel_id=1, source_target_pairs={{0,1},{1,2},{2,3},{4,5},{5,6},{6,7},{8,9},{9,10},{10,11},{12,13},{... | collective-permute-start | bytes 491528 | tf_op jit(solution)/shard_map/ppermute | solution.py:383
  15.1 1.3 %collective-permute-start.3 = (f32[4,80,128]{2,1,0:T(8,128)S(1)}, f32[4,80,128]{2,1,0:T(8,128)S(1)}, u32[]{:S(2)}, u32[]{:S(2)}) collective-permute-start(f32[4,80,128]{2,1,0:T(8,128)S(1)} %get-tuple-element.40), channel_id=1, source_target_pairs={{1,0},{2,1},{3,2},{5,4},{6,5},{7,6},{9,8},{10,9},{11,10},{13,12},{... | collective-permute-start | bytes 491528 | tf_op jit(solution)/shard_map/ppermute | solution.py:383
  16.4 0.8 copy-done.4
  17.2 0.7 copy-done.5
  17.9 1.3 %shard_map.57 = (f32[32,32]{1,0:T(8,128)S(1)}, f32[96,32]{1,0:T(8,128)S(1)}, f32[128,128]{1,0:T(8,128)S(1)}, f32[128,384]{1,0:T(8,128)S(1)}, f32[352,1]{1,0:T(8,128)S(1)}) custom-call(s32[2]{0:T(128)S(1)} %pad_add_fusion.place, f32[32,32]{1,0:T(8,128)S(1)} %copy-done.5, f32[64,64]{1,0:T(8,128)S(1)} %copy-done.4), custom_call_target="tpu_custom_call" | custom-call | tf_op jit(solution)/shard_map/pallas_call | solution.py:396
  19.3 1.9 %collective-permute-done.3.right = f32[4,80,128]{2,1,0:T(8,128)S(1)} collective-permute-done((f32[4,80,128]{2,1,0:T(8,128)S(1)}, f32[4,80,128]{2,1,0:T(8,128)S(1)}, u32[]{:S(2)}, u32[]{:S(2)}) %collective-permute-start.3) | collective-permute-done | bytes 163872 | tf_op jit(solution)/shard_map/ppermute | solution.py:383
  21.1 2.2 %copy-done = f32[1024,1024]{1,0:T(8,128)S(1)} copy-done((f32[1024,1024]{1,0:T(8,128)S(1)}, f32[1024,1024]{1,0:T(8,128)}, u32[]{:S(2)}) %copy-start) | copy-done | bytes 4194328
  23.3 4.8 %shard_map.58 = (f32[3,272,128]{2,1,0:T(8,128)S(1)}, f32[80,384]{1,0:T(8,128)S(1)}, f32[104,384]{1,0:T(8,128)S(1)}) custom-call(s32[2]{0:T(128)S(1)} %pad_add_fusion.place, f32[4,80,384]{2,1,0:T(8,128)S(1)} %get-tuple-element.38.tall.block, f32[4,80,128]{2,1,0:T(8,128)S(1)} %collective-permute-done.2.left, f32[4,80,128]{2,1,0:T(8,128)S(1)} %collective-permute-done.3.right, ...), custom_call_target="tpu_custom_call" | custom-call | tf_op jit(solution)/shard_map/pallas_call | solution.py:416
  28.2 6.0 %collective-permute-start.5 = (f32[104,384]{1,0:T(8,128)S(1)}, f32[104,384]{1,0:T(8,128)S(1)}, u32[]{:S(2)}, u32[]{:S(2)}) collective-permute-start(f32[104,384]{1,0:T(8,128)S(1)} %get-tuple-element.51), channel_id=1, source_target_pairs={{64,0},{128,64},{192,128},{256,192},{320,256},{384,320},{448,384},... | collective-permute-start | bytes 479240 | tf_op jit(solution)/shard_map/ppermute | solution.py:383
  34.2 2.4 %collective-permute-start.4 = (f32[104,384]{1,0:T(8,128)S(1)}, f32[104,384]{1,0:T(8,128)S(1)}, u32[]{:S(2)}, u32[]{:S(2)}) collective-permute-start(f32[104,384]{1,0:T(8,128)S(1)} %get-tuple-element.51), channel_id=1, source_target_pairs={{0,64},{64,128},{128,192},{192,256},{256,320},{320,384},{384,448},... | collective-permute-start | bytes 479240 | tf_op jit(solution)/shard_map/ppermute | solution.py:383
  36.5 1.0 collective-permute-done.5.after
  37.5 1.2 collective-permute-done.4.before
  38.7 1.1 shard_map.59
  39.8 3.5 %collective-permute-start.6 = (f32[3,24,384]{2,1,0:T(8,128)S(1)}, f32[3,24,384]{2,1,0:T(8,128)S(1)}, u32[]{:S(2)}, u32[]{:S(2)}) collective-permute-start(f32[3,24,384]{2,1,0:T(8,128)S(1)} %get-tuple-element.54), channel_id=1, source_target_pairs={{0,4},{4,8},{8,12},{12,16},{16,20},{20,24},{24,28},{28,32},{32,36}... | collective-permute-start | bytes 331784 | tf_op jit(solution)/shard_map/ppermute | solution.py:383
  43.3 1.3 %collective-permute-start.7 = (f32[3,24,384]{2,1,0:T(8,128)S(1)}, f32[3,24,384]{2,1,0:T(8,128)S(1)}, u32[]{:S(2)}, u32[]{:S(2)}) collective-permute-start(f32[3,24,384]{2,1,0:T(8,128)S(1)} %get-tuple-element.55), channel_id=1, source_target_pairs={{4,0},{8,4},{12,8},{16,12},{20,16},{24,20},{28,24},{32,28},{36,32}... | collective-permute-start | bytes 331784 | tf_op jit(solution)/shard_map/ppermute | solution.py:383
  44.6 0.4 collective-permute-done.6.low
  45.1 5.1 %collective-permute-done.7.high = f32[3,24,384]{2,1,0:T(8,128)S(1)} collective-permute-done((f32[3,24,384]{2,1,0:T(8,128)S(1)}, f32[3,24,384]{2,1,0:T(8,128)S(1)}, u32[]{:S(2)}, u32[]{:S(2)}) %collective-permute-start.7) | collective-permute-done | bytes 110624 | tf_op jit(solution)/shard_map/ppermute | solution.py:383
  50.1 32.5 %all_to_all.15.gathered = f32[64,1,384]{2,1,0:T(1,128)S(1)} all-to-all(f32[64,1,384]{2,1,0:T(1,128)S(1)} %get-tuple-element.56), channel_id=1, replica_groups=mesh['tm'=8,'row'=16,'col'=4] {'row','col'}, dimensions={0} | all-to-all | bytes 196608 | tf_op jit(solution)/shard_map/all_to_all | solution.py:431
  82.7 6.3 %shard_map.60 = (f32[96,256]{1,0:T(8,128)S(1)}, f32[96,256]{1,0:T(8,128)S(1)}, f32[1,128]{1,0:T(1,128)S(1)}) custom-call(s32[2]{0:T(128)S(1)} %pad_add_fusion.place, f32[64,1,384]{2,1,0:T(1,128)S(1)} %all_to_all.15.gathered, f32[4,80,384]{2,1,0:T(8,128)S(1)} %get-tuple-element.38.tall.block, f32[3,272,128]{2,1,0:T(8,128)S(1)} %get-tuple-element.50.result, ...), custom_call_target="tpu_custom_call" | custom-call | tf_op jit(solution)/shard_map/pallas_call | solution.py:432
  89.0 5.0 %collective-permute-start.8 = (f32[96,256]{1,0:T(8,128)S(1)}, f32[96,256]{1,0:T(8,128)S(1)}, u32[]{:S(2)}, u32[]{:S(2)}) collective-permute-start(f32[96,256]{1,0:T(8,128)S(1)} %get-tuple-element.64.second), channel_id=1, source_target_pairs={{0,64},{64,128},{128,192},{192,256},{256,320},{320,384},{384,448},... | collective-permute-start | bytes 294920 | tf_op jit(solution)/shard_map/ppermute | solution.py:443
  94.0 1.6 %collective-permute-done.8.before = f32[96,256]{1,0:T(8,128)S(1)} collective-permute-done((f32[96,256]{1,0:T(8,128)S(1)}, f32[96,256]{1,0:T(8,128)S(1)}, u32[]{:S(2)}, u32[]{:S(2)}) %collective-permute-start.8) | collective-permute-done | bytes 98336 | tf_op jit(solution)/shard_map/ppermute | solution.py:443
  95.6 0.1 shard_map.61
  95.7 10.1 %all_to_all.16.received = f32[8,1,128]{2,1,0:T(1,128)S(1)} all-to-all(f32[8,1,128]{2,1,0:T(1,128)S(1)} %shard_map.61), channel_id=1, replica_groups=mesh['tm'=8,'row'=16,'col'=4] {'tm'}, dimensions={0} | all-to-all | bytes 8192 | tf_op jit(solution)/shard_map/all_to_all | solution.py:445
  105.8 17.4 %all_to_all.17.received = f32[64,1,128]{2,1,0:T(1,128)S(1)} all-to-all(f32[64,1,128]{2,1,0:T(1,128)S(1)} %shard_map.62), channel_id=1, replica_groups=mesh['tm'=8,'row'=16,'col'=4] {'row','col'}, dimensions={0} | all-to-all | bytes 65536 | tf_op jit(solution)/shard_map/all_to_all | solution.py:447
  123.2 0.8 shard_map.63
  (11 shorter events, 0.1 us)
Async XLA Ops:
  0.0 0.9 copy-start.2
  0.9 0.8 copy-start.3
  1.7 6.0 %collective-permute-start = (f32[4,24,256]{2,1,0:T(8,128)S(1)}, f32[4,24,256]{2,1,0:T(8,128)S(1)}, u32[]{:S(2)}, u32[]{:S(2)}) collective-permute-start(f32[4,24,256]{2,1,0:T(8,128)S(1)} %get-tuple-element.36), channel_id=1, source_target_pairs={{0,4},{4,8},{8,12},{12,16},{16,20},{20,24},{24,28},{28,32},{32,36}... | collective-permute-start | bytes 294920 | tf_op jit(solution)/shard_map/ppermute | solution.py:383
  6.1 5.5 %collective-permute-start.1 = (f32[4,24,256]{2,1,0:T(8,128)S(1)}, f32[4,24,256]{2,1,0:T(8,128)S(1)}, u32[]{:S(2)}, u32[]{:S(2)}) collective-permute-start(f32[4,24,256]{2,1,0:T(8,128)S(1)} %get-tuple-element.37), channel_id=1, source_target_pairs={{4,0},{8,4},{12,8},{16,12},{20,16},{24,20},{28,24},{32,28},{36,32}... | collective-permute-start | bytes 294920 | tf_op jit(solution)/shard_map/ppermute | solution.py:383
  11.9 7.3 %collective-permute-start.2 = (f32[4,80,128]{2,1,0:T(8,128)S(1)}, f32[4,80,128]{2,1,0:T(8,128)S(1)}, u32[]{:S(2)}, u32[]{:S(2)}) collective-permute-start(f32[4,80,128]{2,1,0:T(8,128)S(1)} %get-tuple-element.39), channel_id=1, source_target_pairs={{0,1},{1,2},{2,3},{4,5},{5,6},{6,7},{8,9},{9,10},{10,11},{12,13},{... | collective-permute-start | bytes 491528 | tf_op jit(solution)/shard_map/ppermute | solution.py:383
  15.1 6.1 %collective-permute-start.3 = (f32[4,80,128]{2,1,0:T(8,128)S(1)}, f32[4,80,128]{2,1,0:T(8,128)S(1)}, u32[]{:S(2)}, u32[]{:S(2)}) collective-permute-start(f32[4,80,128]{2,1,0:T(8,128)S(1)} %get-tuple-element.40), channel_id=1, source_target_pairs={{1,0},{2,1},{3,2},{5,4},{6,5},{7,6},{9,8},{10,9},{11,10},{13,12},{... | collective-permute-start | bytes 491528 | tf_op jit(solution)/shard_map/ppermute | solution.py:383
  16.4 0.8 copy-start.4
  17.2 0.7 copy-start.5
  21.1 2.2 %copy-start = (f32[1024,1024]{1,0:T(8,128)S(1)}, f32[1024,1024]{1,0:T(8,128)}, u32[]{:S(2)}) copy-start(f32[1024,1024]{1,0:T(8,128)} %inverse.3) | copy-start | bytes 12582916
  23.3 59.3 %copy-start.1 = (f32[1024,1024]{1,0:T(8,128)S(1)}, f32[1024,1024]{1,0:T(8,128)}, u32[]{:S(2)}) copy-start(f32[1024,1024]{1,0:T(8,128)} %inverse.3) | copy-start | bytes 12582916
  28.2 9.4 %collective-permute-start.5 = (f32[104,384]{1,0:T(8,128)S(1)}, f32[104,384]{1,0:T(8,128)S(1)}, u32[]{:S(2)}, u32[]{:S(2)}) collective-permute-start(f32[104,384]{1,0:T(8,128)S(1)} %get-tuple-element.51), channel_id=1, source_target_pairs={{64,0},{128,64},{192,128},{256,192},{320,256},{384,320},{448,384},... | collective-permute-start | bytes 479240 | tf_op jit(solution)/shard_map/ppermute | solution.py:383
  34.2 4.6 %collective-permute-start.4 = (f32[104,384]{1,0:T(8,128)S(1)}, f32[104,384]{1,0:T(8,128)S(1)}, u32[]{:S(2)}, u32[]{:S(2)}) collective-permute-start(f32[104,384]{1,0:T(8,128)S(1)} %get-tuple-element.51), channel_id=1, source_target_pairs={{0,64},{64,128},{128,192},{192,256},{256,320},{320,384},{384,448},... | collective-permute-start | bytes 479240 | tf_op jit(solution)/shard_map/ppermute | solution.py:383
  39.8 5.3 %collective-permute-start.6 = (f32[3,24,384]{2,1,0:T(8,128)S(1)}, f32[3,24,384]{2,1,0:T(8,128)S(1)}, u32[]{:S(2)}, u32[]{:S(2)}) collective-permute-start(f32[3,24,384]{2,1,0:T(8,128)S(1)} %get-tuple-element.54), channel_id=1, source_target_pairs={{0,4},{4,8},{8,12},{12,16},{16,20},{20,24},{24,28},{28,32},{32,36}... | collective-permute-start | bytes 331784 | tf_op jit(solution)/shard_map/ppermute | solution.py:383
  43.3 6.8 %collective-permute-start.7 = (f32[3,24,384]{2,1,0:T(8,128)S(1)}, f32[3,24,384]{2,1,0:T(8,128)S(1)}, u32[]{:S(2)}, u32[]{:S(2)}) collective-permute-start(f32[3,24,384]{2,1,0:T(8,128)S(1)} %get-tuple-element.55), channel_id=1, source_target_pairs={{4,0},{8,4},{12,8},{16,12},{20,16},{24,20},{28,24},{32,28},{36,32}... | collective-permute-start | bytes 331784 | tf_op jit(solution)/shard_map/ppermute | solution.py:383
  89.0 6.6 %collective-permute-start.8 = (f32[96,256]{1,0:T(8,128)S(1)}, f32[96,256]{1,0:T(8,128)S(1)}, u32[]{:S(2)}, u32[]{:S(2)}) collective-permute-start(f32[96,256]{1,0:T(8,128)S(1)} %get-tuple-element.64.second), channel_id=1, source_target_pairs={{0,64},{64,128},{128,192},{192,256},{256,320},{320,384},{384,448},... | collective-permute-start | bytes 294920 | tf_op jit(solution)/shard_map/ppermute | solution.py:443

commit v4 on v3

--- a/solution.py
+++ b/solution.py
@@ -27,11 +27,11 @@
 SPREAD = 96
 
 
-def call(body, outs, kinds, scratch=(), limit=8):
+def call(body, outs, kinds, scratch=(), limit=8, kept=f32):
     specs = [pl.BlockSpec(memory_space=pltpu.SMEM) if kind == "s" else pl.BlockSpec() for kind in kinds]
     return pl.pallas_call(
         body,
-        out_shape=[jax.ShapeDtypeStruct(shape, f32) for shape in outs],
+        out_shape=[jax.ShapeDtypeStruct(shape, kept) for shape in outs],
         in_specs=specs,
         scratch_shapes=list(scratch),
         compiler_params=pltpu.CompilerParams(vmem_limit_bytes=limit * 1024 * 1024),
@@ -70,7 +70,7 @@
     return parts
 
 
-def patch_apply(span_of, field, result, inverse, high_w, low_w, keep, high_x, low_x, solved):
+def patch_apply(span_of, field, result, high_w, low_w, keep, high_x, low_x, solved):
     start, stop = span_of
     used = pl.ds(0, PATCH_ROWS * (stop - start))
 
@@ -90,11 +90,6 @@
                     where = (pl.ds(PATCH_ROWS * (place - start), PATCH_ROWS), pl.ds(128 * block, 128))
                     high_x[where] = upper
                     low_x[where] = lower
-    for part in range(16):
-        span = pl.ds(64 * part, 64)
-        upper = inverse[span, :].astype(bf16)
-        high_w[span, :] = upper
-        low_w[span, :] = (inverse[span, :] - upper.astype(f32)).astype(bf16)
     for part in range(4):
         span = pl.ds(256 * part, 256)
         dot = functools.partial(jnp.dot, preferred_element_type=f32)
@@ -138,7 +133,15 @@
     return (row >= 0) & (row < ROWS * row_count) & (col >= 0) & (col < COLS * col_count) & near
 
 
+def fold_rows(edge):
+    half = TALL // 2
+    lane = lanes_of((half, 128))
+    return jnp.where(lane < 64, edge[:half], pltpu.roll(edge[half:], 64, 1))
+
+
 def merge_sides(middle, left, right):
+    left = jnp.concatenate([left, pltpu.roll(left, 64, 1)], axis=0)
+    right = jnp.concatenate([pltpu.roll(right, SIDE, 1), pltpu.roll(right, SIDE + 64, 1)], axis=0)
     lane = lanes_of(left.shape)
     first = jnp.where(lane < SIDE, left, middle[:, :128])
     last = jnp.where((lane >= SIDE) & (lane < 2 * SIDE), right, middle[:, 256:])
@@ -154,24 +157,20 @@
     return jnp.dot(stacked, inside.astype(f32), precision=highest, preferred_element_type=f32)
 
 
-def assemble(low, block, mask, high, tall, to_right, to_left, cells):
+def assemble(low, middle, high, tall, to_right, to_left, cells):
     own = []
     for channel in range(4):
-        if channel < 3:
-            middle = block[channel]
-        else:
-            middle = jnp.where(mask[...] == 1, seam_screen, keep_screen).astype(f32)
-        column = jnp.concatenate([low[channel], middle, high[channel]], axis=0)
+        column = jnp.concatenate([low[channel], middle[channel], high[channel]], axis=0)
         wide = jnp.concatenate([column, jnp.zeros((TALL, 128), f32)], axis=1)
         wide = pltpu.roll(wide, SIDE, 1)
         tall[channel] = wide
-        to_right[channel] = wide[:, 256:]
-        to_left[channel] = wide[:, :128]
+        to_right[channel] = fold_rows(wide[:, 256:])
+        to_left[channel] = fold_rows(pltpu.roll(wide[:, :128], 128 - SIDE, 1))
         own.append(wide[RIM : RIM + ROWS])
     cells[...] = cell_sums(own)
 
 
-def prepare(row_count, col_count, place, row_coupling, col_coupling, row_mix, row_spread, col_mix, col_spread, keep):
+def prepare(row_count, col_count, place, row_coupling, col_coupling, row_mix, row_spread, col_mix, col_spread):
     dot = functools.partial(jnp.dot, precision=highest, preferred_element_type=f32)
     turned = functools.partial(
         lax.dot_general, dimension_numbers=(((1,), (1,)), ((), ())), precision=highest, preferred_element_type=f32
@@ -194,32 +193,36 @@
         return (col >= CELL * cell) & (col < CELL * cell + CELL)
 
     col_spread[...] = dot(col_turned, matrix((coarse_cols, LANES), column))
-    index = lax.broadcasted_iota(jnp.int32, (PATCHES, 1), 0)
-    kind = index % PATCH_ROWS
-    patch_row = 2 * place[0] + kind % 5 - 1
-    patch_col = CELL * place[1] + index // PATCH_ROWS - 3
-    kept = (kind < 15) & (kind % 5 < 4) & (patch_row >= 0) & (patch_row < coarse_rows)
-    keep[...] = (kept & (patch_col >= 0) & (patch_col < coarse_cols)).astype(f32)
-
-
-def edges(block, mask, last, first):
-    for channel in range(3):
+
+
+def split(whole, upper, lower):
+    for part in range(16):
+        span = pl.ds(64 * part, 64)
+        high = whole[span, :].astype(bf16)
+        upper[span, :] = high
+        lower[span, :] = (whole[span, :] - high.astype(f32)).astype(bf16)
+
+
+def edges(block, mask, last, first, middle):
+    for channel in range(3):
+        middle[channel] = block[channel]
         last[channel] = block[channel, ROWS - RIM :]
         first[channel] = block[channel, :RIM]
     screen = jnp.where(mask[...] == 1, seam_screen, keep_screen).astype(f32)
+    middle[3] = screen
     last[3] = screen[ROWS - RIM :]
     first[3] = screen[:RIM]
 
 
 def first_apply(
-    row_count, col_count, place, tall, left, right, cells, inverse, keep, result, screen, share,
-    field, high_x, low_x, solved, high_w, low_w,
+    row_count, col_count, place, tall, left, right, cells, high_w, low_w, keep, result, screen, share,
+    field, high_x, low_x, solved,
 ):
     put_rows(field, 240, FLAT - 240, jnp.zeros((FLAT - 240, LANES), f32))
     for channel in range(3):
         put_rows(field, TALL * channel, TALL, merge_sides(tall[channel], left[channel], right[channel]))
     screen[...] = merge_sides(tall[3], left[3], right[3])
-    patch_apply((0, PATCH_COLS), field, result, inverse, high_w, low_w, keep, high_x, low_x, solved)
+    patch_apply((0, PATCH_COLS), field, result, high_w, low_w, keep, high_x, low_x, solved)
     inside = inside_of(place, row_count, col_count, 40)
     for channel in range(3):
         whole = rows_of(result, TALL * channel, TALL)
@@ -323,7 +326,8 @@
         image_sums = grid_of(6 + channel) + (screen_cells + 576.0) * level
         late_sums.append(image_sums - 16.0 * (above + below + before + after) - 256.0 * level_beside)
     spread(jnp.concatenate(late_sums, axis=0), [(late, 0), (late, 1), (late, 2)])
-    patch_apply((2, PATCH_COLS - 2), field, output, inverse, high_w, low_w, keep, high_x, low_x, solved)
+    split(inverse, high_w, low_w)
+    patch_apply((2, PATCH_COLS - 2), field, output, high_w, low_w, keep, high_x, low_x, solved)
     totals = [jnp.zeros((ROWS, LANES), f32) for _ in range(4)]
     for channel in range(3):
         whole = rows_of(output, TALL * channel, TALL) + late[channel, pl.ds(8, TALL), :]
@@ -390,36 +394,36 @@
     place = jnp.stack([lax.axis_index("row"), lax.axis_index("col")]).astype(jnp.int32)
     block = right_side.reshape(3, ROWS, COLS)
     mask = seam_mask.reshape(ROWS, COLS)
-    last, first = call(edges, [(4, RIM, COLS)] * 2, "vv")(block, mask)
+    last, first, middle = call(edges, [(4, RIM, COLS)] * 2 + [(4, ROWS, COLS)], "vv")(block, mask)
     low, high = exchange(last, first, "row")
 
-    mixers = call(
-        functools.partial(prepare, row_count, col_count),
-        [(coarse_rows, coarse_rows), (SPREAD, coarse_rows), (128, 128), (128, LANES), (PATCHES, 1)],
-        "svv",
-    )(place, row_coupling, col_coupling)
+    index = lax.broadcasted_iota(jnp.int32, (PATCHES, 1), 0)
+    kind = index % PATCH_ROWS
+    patch_row = 2 * place[0] + kind % 5 - 1
+    patch_col = CELL * place[1] + index // PATCH_ROWS - 3
+    kept = (kind < 15) & (kind % 5 < 4) & (patch_row >= 0) & (patch_row < coarse_rows)
+    keep = (kept & (patch_col >= 0) & (patch_col < CELL * col_count)).astype(f32)
 
     tall, to_right, to_left, cells = call(
-        assemble, [(4, TALL, LANES), (4, TALL, 128), (4, TALL, 128), (8, 128)], "hhhh"
-    )(low, block, mask, high)
+        assemble, [(4, TALL, LANES), (4, TALL // 2, 128), (4, TALL // 2, 128), (8, 128)], "vvv"
+    )(low, middle, high)
+    to_right, to_left, whole = lax.optimization_barrier((to_right, to_left, patch_inverse))
     left, right = exchange(to_right, to_left, "col")
-    left, right, *mixers = lax.optimization_barrier((left, right, *mixers))
-    row_mix, row_spread, col_mix, col_spread, keep = mixers
+    high_w, low_w = call(split, [(1024, 1024)] * 2, "v", limit=16, kept=bf16)(whole)
+    left, right, high_w, low_w = lax.optimization_barrier((left, right, high_w, low_w))
     work = [
         pltpu.VMEM((PATCHES, 1024), bf16),
         pltpu.VMEM((PATCHES, 1024), bf16),
         pltpu.VMEM((PATCHES, 1024), f32),
-        pltpu.VMEM((1024, 1024), bf16),
-        pltpu.VMEM((1024, 1024), bf16),
     ]
     flat = pltpu.VMEM((3, FLAT, 128), f32)
     result, screen, share = call(
         functools.partial(first_apply, row_count, col_count),
         [(3, FLAT, 128), (TALL, LANES), (3 * ROWS + 8, LANES)],
-        "svvvvvv",
+        "svvvvvvv",
         [flat] + work,
         16,
-    )(place, tall, left, right, cells, patch_inverse, keep)
+    )(place, tall, left, right, cells, high_w, low_w, keep)
     before, after = exchange(share, share, "tm")
     image, last, first, message = call(
         functools.partial(first_image, peers, row_count, col_count),
@@ -427,13 +431,18 @@
         "svvvvv",
     )(place, result, before, after, screen, cells)
     low, high = exchange(last, first, "row")
-    message, low, high = lax.optimization_barrier((message, low, high))
+    message, row_coupling, col_coupling = lax.optimization_barrier((message, row_coupling, col_coupling))
+    row_mix, row_spread, col_mix, col_spread = call(
+        functools.partial(prepare, row_count, col_count),
+        [(coarse_rows, coarse_rows), (SPREAD, coarse_rows), (128, 128), (128, LANES)],
+        "svv",
+    )(place, row_coupling, col_coupling)
     gathered = lax.all_to_all(message, ("row", "col"), 0, 0)
     first, second, partial = call(
         functools.partial(second_apply, row_count, col_count),
         [(3 * ROWS, COLS), (3 * ROWS, COLS), (1, 128)],
         "s" + "v" * 13,
-        [flat] * 2 + work + [pltpu.VMEM((3, SPREAD, LANES), f32)] * 3 + [pltpu.VMEM((3, peers, 128), f32)],
+        [flat] * 2 + work + [pltpu.VMEM((1024, 1024), bf16)] * 2 + [pltpu.VMEM((3, SPREAD, LANES), f32)] * 3 + [pltpu.VMEM((3, peers, 128), f32)],
         20,
     )(
         place, gathered, tall, result, image, low, high, screen, patch_inverse, keep,

time: 125 us -> 120 us (0.960)
  blocking collectives: 60 us -> 31.9 us
  starting transfers between devices: 28.2 us -> 45.8 us
  waiting for transfers between devices: 15.4 us -> 19.3 us
    all_to_all x1 -> x0, blocking collectives: 32.5 us -> none  [shards(): gathered = lax.all_to_all(message, ('row', 'col'), 0, 0)]
    all_to_all x0 -> x1, starting transfers between devices: none -> 17.8 us  [shards(): gathered = lax.all_to_all(message, ('row', 'col'), 0, 0)]
    all_to_all x0 -> x1, waiting for transfers between devices: none -> 6.01 us  [shards(): gathered = lax.all_to_all(message, ('row', 'col'), 0, 0)]
    all_to_all x1, blocking collectives: 17.4 us -> 21.8 us  [shards(): received = lax.all_to_all(shared, ('row', 'col'), 0, 0)]
    ppermute x4, waiting for transfers between devices: 11.9 us -> 8.78 us  [exchange(): lax.ppermute(first, axis, backward)]
  transfers between devices with their start and end apart: 9 -> 10, of which waited for: 8 -> 9; matrix products, arithmetic and copies ran while one was open for 0% -> 0% of each run, Pallas kernels for 1% -> 2%
where the time goes in v4:
time: 120 us; the launch traced here: 119 us
  starting transfers between devices  45.8 us (38%)
  blocking collectives  31.9 us (27%)
  waiting for transfers between devices  19.3 us (16%)
  Pallas kernels  16 us (13%)
  local copies, waits for them, and re-layouts  6.03 us (5%)
    all_to_all x1, blocking collectives, shards(): received = lax.all_to_all(shared, ('row', 'col'), 0, 0)  21.8 us
    all_to_all x1, starting transfers between devices, shards(): gathered = lax.all_to_all(message, ('row', 'col'), 0, 0)  17.8 us
    ppermute x4, starting transfers between devices, exchange(): lax.ppermute(last, axis, forward)  12.8 us
    all_to_all x1, blocking collectives, shards(): received = lax.all_to_all(shared, 'tm', 0, 0)  10.1 us
    ppermute x4, starting transfers between devices, exchange(): lax.ppermute(first, axis, backward)  10 us
    ppermute x4, waiting for transfers between devices, exchange(): lax.ppermute(first, axis, backward)  8.78 us
    pallas_call x1, Pallas kernels, shards(): call(functools.partial(second_apply, row_count, col_count), [(3 * ROWS, C...  6.33 us
    unnamed x12, local copies, waits for them, and re-layouts  6.03 us
  transfers between devices with their start and end apart: 10, of which 9 were waited for; matrix products, arithmetic and copies ran while one was open for 0% of the time, Pallas kernels for 2%

profile of v4, /device:TPU:1, one launch (start us, length us, event | category | flops | bytes accessed | tf_op | source)
XLA Modules:
  0.0 119.4 jit_solution(11900779743268788534)
XLA Ops:
  0.0 0.9 copy-done.2
  0.9 0.8 copy-done.4
  1.7 4.4 %collective-permute-start = (f32[4,24,256]{2,1,0:T(8,128)S(1)}, f32[4,24,256]{2,1,0:T(8,128)S(1)}, u32[]{:S(2)}, u32[]{:S(2)}) collective-permute-start(f32[4,24,256]{2,1,0:T(8,128)S(1)} %get-tuple-element.38), channel_id=1, source_target_pairs={{0,4},{4,8},{8,12},{12,16},{16,20},{20,24},{24,28},{28,32},{32,36}... | collective-permute-start | bytes 294920 | tf_op jit(solution)/shard_map/ppermute | solution.py:387
  6.1 1.3 %collective-permute-start.1 = (f32[4,24,256]{2,1,0:T(8,128)S(1)}, f32[4,24,256]{2,1,0:T(8,128)S(1)}, u32[]{:S(2)}, u32[]{:S(2)}) collective-permute-start(f32[4,24,256]{2,1,0:T(8,128)S(1)} %get-tuple-element.40), channel_id=1, source_target_pairs={{4,0},{8,4},{12,8},{16,12},{20,16},{24,20},{28,24},{32,28},{36,32}... | collective-permute-start | bytes 294920 | tf_op jit(solution)/shard_map/ppermute | solution.py:387
  7.4 0.2 fusion.16.keep
  7.7 3.9 %collective-permute-done.1.high = f32[4,24,256]{2,1,0:T(8,128)S(1)} collective-permute-done((f32[4,24,256]{2,1,0:T(8,128)S(1)}, f32[4,24,256]{2,1,0:T(8,128)S(1)}, u32[]{:S(2)}, u32[]{:S(2)}) %collective-permute-start.1) | collective-permute-done | bytes 98336 | tf_op jit(solution)/shard_map/ppermute | solution.py:387
  11.6 0.4 shard_map.56
  12.0 3.1 %collective-permute-start.2 = (f32[4,40,128]{2,1,0:T(8,128)S(1)}, f32[4,40,128]{2,1,0:T(8,128)S(1)}, u32[]{:S(2)}, u32[]{:S(2)}) collective-permute-start(f32[4,40,128]{2,1,0:T(8,128)S(1)} %get-tuple-element.44), channel_id=1, source_target_pairs={{0,1},{1,2},{2,3},{4,5},{5,6},{6,7},{8,9},{9,10},{10,11},{12,13},{... | collective-permute-start | bytes 245768 | tf_op jit(solution)/shard_map/ppermute | solution.py:387
  15.1 1.3 %collective-permute-start.3 = (f32[4,40,128]{2,1,0:T(8,128)S(1)}, f32[4,40,128]{2,1,0:T(8,128)S(1)}, u32[]{:S(2)}, u32[]{:S(2)}) collective-permute-start(f32[4,40,128]{2,1,0:T(8,128)S(1)} %get-tuple-element.45), channel_id=1, source_target_pairs={{1,0},{2,1},{3,2},{5,4},{6,5},{7,6},{9,8},{10,9},{11,10},{13,12},{... | collective-permute-start | bytes 245768 | tf_op jit(solution)/shard_map/ppermute | solution.py:387
  16.5 2.2 %copy-done = f32[1024,1024]{1,0:T(8,128)S(1)} copy-done((f32[1024,1024]{1,0:T(8,128)S(1)}, f32[1024,1024]{1,0:T(8,128)}, u32[]{:S(2)}) %copy-start) | copy-done | bytes 4194328
  18.7 0.7 shard_map.57
  19.4 1.0 collective-permute-done.3.right
  20.3 4.8 %shard_map.58 = (f32[3,272,128]{2,1,0:T(8,128)S(1)}, f32[80,384]{1,0:T(8,128)S(1)}, f32[104,384]{1,0:T(8,128)S(1)}) custom-call(s32[2]{0:T(128)S(1)} %pad_add_fusion.place, f32[4,80,384]{2,1,0:T(8,128)S(1)} %get-tuple-element.41.tall.block, f32[4,40,128]{2,1,0:T(8,128)S(1)} %collective-permute-done.2.left, f32[4,40,128]{2,1,0:T(8,128)S(1)} %collective-permute-done.3.right, ...), custom_call_target="tpu_custom_call" | custom-call | tf_op jit(solution)/shard_map/pallas_call | solution.py:420
  25.1 6.0 %collective-permute-start.5 = (f32[104,384]{1,0:T(8,128)S(1)}, f32[104,384]{1,0:T(8,128)S(1)}, u32[]{:S(2)}, u32[]{:S(2)}) collective-permute-start(f32[104,384]{1,0:T(8,128)S(1)} %get-tuple-element.55), channel_id=1, source_target_pairs={{64,0},{128,64},{192,128},{256,192},{320,256},{384,320},{448,384},... | collective-permute-start | bytes 479240 | tf_op jit(solution)/shard_map/ppermute | solution.py:387
  31.1 2.4 %collective-permute-start.4 = (f32[104,384]{1,0:T(8,128)S(1)}, f32[104,384]{1,0:T(8,128)S(1)}, u32[]{:S(2)}, u32[]{:S(2)}) collective-permute-start(f32[104,384]{1,0:T(8,128)S(1)} %get-tuple-element.55), channel_id=1, source_target_pairs={{0,64},{64,128},{128,192},{192,256},{256,320},{320,384},{384,448},... | collective-permute-start | bytes 479240 | tf_op jit(solution)/shard_map/ppermute | solution.py:387
  33.5 1.0 collective-permute-done.5.after
  34.5 1.2 collective-permute-done.4.before
  35.7 1.7 %shard_map.59 = (f32[3,32,384]{2,1,0:T(8,128)S(1)}, f32[3,24,384]{2,1,0:T(8,128)S(1)}, f32[3,24,384]{2,1,0:T(8,128)S(1)}, f32[64,1,384]{2,1,0:T(1,128)}) custom-call(s32[2]{0:T(128)S(1)} %pad_add_fusion.place, f32[3,272,128]{2,1,0:T(8,128)S(1)} %get-tuple-element.54.result, f32[104,384]{1,0:T(8,128)S(1)} %collective-permute-done.4.before, ...), custom_call_target="tpu_custom_call" | custom-call | tf_op jit(solution)/shard_map/pallas_call | solution.py:428
  37.4 17.8 %all-to-all-start = ((f32[64,1,384]{2,1,0:T(1,128)}), f32[64,1,384]{2,1,0:T(1,128)S(1)}, u32[]{:S(2)}, u32[]{:S(2)}) async-start(f32[64,1,384]{2,1,0:T(1,128)} %get-tuple-element.58), calls=%async_computation | async-start | bytes 196608 | tf_op jit(solution)/shard_map/all_to_all | solution.py:440
  55.2 2.9 %collective-permute-start.6 = (f32[3,24,384]{2,1,0:T(8,128)S(1)}, f32[3,24,384]{2,1,0:T(8,128)S(1)}, u32[]{:S(2)}, u32[]{:S(2)}) collective-permute-start(f32[3,24,384]{2,1,0:T(8,128)S(1)} %get-tuple-element.60), channel_id=1, source_target_pairs={{0,4},{4,8},{8,12},{12,16},{16,20},{20,24},{24,28},{28,32},{32,36}... | collective-permute-start | bytes 331784 | tf_op jit(solution)/shard_map/ppermute | solution.py:387
  58.1 1.5 %collective-permute-start.7 = (f32[3,24,384]{2,1,0:T(8,128)S(1)}, f32[3,24,384]{2,1,0:T(8,128)S(1)}, u32[]{:S(2)}, u32[]{:S(2)}) collective-permute-start(f32[3,24,384]{2,1,0:T(8,128)S(1)} %get-tuple-element.61), channel_id=1, source_target_pairs={{4,0},{8,4},{12,8},{16,12},{20,16},{24,20},{28,24},{32,28},{36,32}... | collective-permute-start | bytes 331784 | tf_op jit(solution)/shard_map/ppermute | solution.py:387
  59.6 1.2 shard_map.60
  60.8 1.6 %collective-permute-done.6.low = f32[3,24,384]{2,1,0:T(8,128)S(1)} collective-permute-done((f32[3,24,384]{2,1,0:T(8,128)S(1)}, f32[3,24,384]{2,1,0:T(8,128)S(1)}, u32[]{:S(2)}, u32[]{:S(2)}) %collective-permute-start.6) | collective-permute-done | bytes 110624 | tf_op jit(solution)/shard_map/ppermute | solution.py:387
  62.4 2.9 %collective-permute-done.7.high = f32[3,24,384]{2,1,0:T(8,128)S(1)} collective-permute-done((f32[3,24,384]{2,1,0:T(8,128)S(1)}, f32[3,24,384]{2,1,0:T(8,128)S(1)}, u32[]{:S(2)}, u32[]{:S(2)}) %collective-permute-start.7) | collective-permute-done | bytes 110624 | tf_op jit(solution)/shard_map/ppermute | solution.py:387
  65.3 6.0 %all-to-all-done.gathered = f32[64,1,384]{2,1,0:T(1,128)S(1)} async-done(((f32[64,1,384]{2,1,0:T(1,128)}), f32[64,1,384]{2,1,0:T(1,128)S(1)}, u32[]{:S(2)}, u32[]{:S(2)}) %all-to-all-start) | async-done | bytes 98336 | tf_op jit(solution)/shard_map/all_to_all | solution.py:440
  71.3 2.2 %copy-done.1 = f32[1024,1024]{1,0:T(8,128)S(1)} copy-done((f32[1024,1024]{1,0:T(8,128)S(1)}, f32[1024,1024]{1,0:T(8,128)}, u32[]{:S(2)}) %copy-start.1) | copy-done | bytes 4194328
  73.5 6.3 %shard_map.61 = (f32[96,256]{1,0:T(8,128)S(1)}, f32[96,256]{1,0:T(8,128)S(1)}, f32[1,128]{1,0:T(1,128)S(1)}) custom-call(s32[2]{0:T(128)S(1)} %pad_add_fusion.place, f32[64,1,384]{2,1,0:T(1,128)S(1)} %all-to-all-done.gathered, f32[4,80,384]{2,1,0:T(8,128)S(1)} %get-tuple-element.41.tall.block, f32[3,272,128]{2,1,0:T(8,128)S(1)} %get-tuple-element.54.result, ...), custom_call_target="tpu_custom_call" | custom-call | tf_op jit(solution)/shard_map/pallas_call | solution.py:441
  79.8 5.1 %collective-permute-start.8 = (f32[96,256]{1,0:T(8,128)S(1)}, f32[96,256]{1,0:T(8,128)S(1)}, u32[]{:S(2)}, u32[]{:S(2)}) collective-permute-start(f32[96,256]{1,0:T(8,128)S(1)} %get-tuple-element.68.second), channel_id=1, source_target_pairs={{0,64},{64,128},{128,192},{192,256},{256,320},{320,384},{384,448},... | collective-permute-start | bytes 294920 | tf_op jit(solution)/shard_map/ppermute | solution.py:452
  84.9 1.6 %collective-permute-done.8.before = f32[96,256]{1,0:T(8,128)S(1)} collective-permute-done((f32[96,256]{1,0:T(8,128)S(1)}, f32[96,256]{1,0:T(8,128)S(1)}, u32[]{:S(2)}, u32[]{:S(2)}) %collective-permute-start.8) | collective-permute-done | bytes 98336 | tf_op jit(solution)/shard_map/ppermute | solution.py:452
  86.6 10.1 %all_to_all.15.received = f32[8,1,128]{2,1,0:T(1,128)S(1)} all-to-all(f32[8,1,128]{2,1,0:T(1,128)S(1)} %shard_map.62), channel_id=1, replica_groups=mesh['tm'=8,'row'=16,'col'=4] {'tm'}, dimensions={0} | all-to-all | bytes 8192 | tf_op jit(solution)/shard_map/all_to_all | solution.py:454
  96.8 21.8 %all_to_all.16.received = f32[64,1,128]{2,1,0:T(1,128)S(1)} all-to-all(f32[64,1,128]{2,1,0:T(1,128)S(1)} %shard_map.63), channel_id=1, replica_groups=mesh['tm'=8,'row'=16,'col'=4] {'row','col'}, dimensions={0} | all-to-all | bytes 65536 | tf_op jit(solution)/shard_map/all_to_all | solution.py:456
  118.6 0.8 shard_map.64
  (14 shorter events, 0.4 us)
Async XLA Ops:
  0.0 0.9 copy-start.2
  0.9 0.8 copy-start.4
  1.7 6.0 %collective-permute-start = (f32[4,24,256]{2,1,0:T(8,128)S(1)}, f32[4,24,256]{2,1,0:T(8,128)S(1)}, u32[]{:S(2)}, u32[]{:S(2)}) collective-permute-start(f32[4,24,256]{2,1,0:T(8,128)S(1)} %get-tuple-element.38), channel_id=1, source_target_pairs={{0,4},{4,8},{8,12},{12,16},{16,20},{20,24},{24,28},{28,32},{32,36}... | collective-permute-start | bytes 294920 | tf_op jit(solution)/shard_map/ppermute | solution.py:387
  6.1 5.5 %collective-permute-start.1 = (f32[4,24,256]{2,1,0:T(8,128)S(1)}, f32[4,24,256]{2,1,0:T(8,128)S(1)}, u32[]{:S(2)}, u32[]{:S(2)}) collective-permute-start(f32[4,24,256]{2,1,0:T(8,128)S(1)} %get-tuple-element.40), channel_id=1, source_target_pairs={{4,0},{8,4},{12,8},{16,12},{20,16},{24,20},{28,24},{32,28},{36,32}... | collective-permute-start | bytes 294920 | tf_op jit(solution)/shard_map/ppermute | solution.py:387
  12.0 7.4 %collective-permute-start.2 = (f32[4,40,128]{2,1,0:T(8,128)S(1)}, f32[4,40,128]{2,1,0:T(8,128)S(1)}, u32[]{:S(2)}, u32[]{:S(2)}) collective-permute-start(f32[4,40,128]{2,1,0:T(8,128)S(1)} %get-tuple-element.44), channel_id=1, source_target_pairs={{0,1},{1,2},{2,3},{4,5},{5,6},{6,7},{8,9},{9,10},{10,11},{12,13},{... | collective-permute-start | bytes 245768 | tf_op jit(solution)/shard_map/ppermute | solution.py:387
  15.1 5.2 %collective-permute-start.3 = (f32[4,40,128]{2,1,0:T(8,128)S(1)}, f32[4,40,128]{2,1,0:T(8,128)S(1)}, u32[]{:S(2)}, u32[]{:S(2)}) collective-permute-start(f32[4,40,128]{2,1,0:T(8,128)S(1)} %get-tuple-element.45), channel_id=1, source_target_pairs={{1,0},{2,1},{3,2},{5,4},{6,5},{7,6},{9,8},{10,9},{11,10},{13,12},{... | collective-permute-start | bytes 245768 | tf_op jit(solution)/shard_map/ppermute | solution.py:387
  16.5 2.2 %copy-start = (f32[1024,1024]{1,0:T(8,128)S(1)}, f32[1024,1024]{1,0:T(8,128)}, u32[]{:S(2)}) copy-start(f32[1024,1024]{1,0:T(8,128)} %inverse.1) | copy-start | bytes 12582916
  20.3 39.3 %copy-start.3 = (f32[64,64]{1,0:T(8,128)S(1)}, f32[64,64]{1,0:T(8,128)}, u32[]{:S(2)}) copy-start(f32[64,64]{1,0:T(8,128)} %col_coupling) | copy-start | bytes 49156
  20.3 39.3 %copy-start.5 = (f32[32,32]{1,0:T(8,128)S(1)}, f32[32,32]{1,0:T(8,128)}, u32[]{:S(2)}) copy-start(f32[32,32]{1,0:T(8,128)} %row_coupling) | copy-start | bytes 12292
  25.1 9.4 %collective-permute-start.5 = (f32[104,384]{1,0:T(8,128)S(1)}, f32[104,384]{1,0:T(8,128)S(1)}, u32[]{:S(2)}, u32[]{:S(2)}) collective-permute-start(f32[104,384]{1,0:T(8,128)S(1)} %get-tuple-element.55), channel_id=1, source_target_pairs={{64,0},{128,64},{192,128},{256,192},{320,256},{384,320},{448,384},... | collective-permute-start | bytes 479240 | tf_op jit(solution)/shard_map/ppermute | solution.py:387
  31.1 4.6 %collective-permute-start.4 = (f32[104,384]{1,0:T(8,128)S(1)}, f32[104,384]{1,0:T(8,128)S(1)}, u32[]{:S(2)}, u32[]{:S(2)}) collective-permute-start(f32[104,384]{1,0:T(8,128)S(1)} %get-tuple-element.55), channel_id=1, source_target_pairs={{0,64},{64,128},{128,192},{192,256},{256,320},{320,384},{384,448},... | collective-permute-start | bytes 479240 | tf_op jit(solution)/shard_map/ppermute | solution.py:387
  37.4 33.9 %all-to-all-start = ((f32[64,1,384]{2,1,0:T(1,128)}), f32[64,1,384]{2,1,0:T(1,128)S(1)}, u32[]{:S(2)}, u32[]{:S(2)}) async-start(f32[64,1,384]{2,1,0:T(1,128)} %get-tuple-element.58), calls=%async_computation | async-start | bytes 196608 | tf_op jit(solution)/shard_map/all_to_all | solution.py:440
  55.2 7.2 %collective-permute-start.6 = (f32[3,24,384]{2,1,0:T(8,128)S(1)}, f32[3,24,384]{2,1,0:T(8,128)S(1)}, u32[]{:S(2)}, u32[]{:S(2)}) collective-permute-start(f32[3,24,384]{2,1,0:T(8,128)S(1)} %get-tuple-element.60), channel_id=1, source_target_pairs={{0,4},{4,8},{8,12},{12,16},{16,20},{20,24},{24,28},{28,32},{32,36}... | collective-permute-start | bytes 331784 | tf_op jit(solution)/shard_map/ppermute | solution.py:387
  58.1 7.1 %collective-permute-start.7 = (f32[3,24,384]{2,1,0:T(8,128)S(1)}, f32[3,24,384]{2,1,0:T(8,128)S(1)}, u32[]{:S(2)}, u32[]{:S(2)}) collective-permute-start(f32[3,24,384]{2,1,0:T(8,128)S(1)} %get-tuple-element.61), channel_id=1, source_target_pairs={{4,0},{8,4},{12,8},{16,12},{20,16},{24,20},{28,24},{32,28},{36,32}... | collective-permute-start | bytes 331784 | tf_op jit(solution)/shard_map/ppermute | solution.py:387
  71.3 2.2 %copy-start.1 = (f32[1024,1024]{1,0:T(8,128)S(1)}, f32[1024,1024]{1,0:T(8,128)}, u32[]{:S(2)}) copy-start(f32[1024,1024]{1,0:T(8,128)} %inverse.1) | copy-start | bytes 12582916
  79.8 6.8 %collective-permute-start.8 = (f32[96,256]{1,0:T(8,128)S(1)}, f32[96,256]{1,0:T(8,128)S(1)}, u32[]{:S(2)}, u32[]{:S(2)}) collective-permute-start(f32[96,256]{1,0:T(8,128)S(1)} %get-tuple-element.68.second), channel_id=1, source_target_pairs={{0,64},{64,128},{128,192},{192,256},{256,320},{320,384},{384,448},... | collective-permute-start | bytes 294920 | tf_op jit(solution)/shard_map/ppermute | solution.py:452

commit v5 on v4

--- a/solution.py
+++ b/solution.py
@@ -450,10 +450,11 @@
     )
     forward = [(i, i + 1) for i in range(frame_count - 1)]
     previous = lax.ppermute(second, "tm", forward)
-    (shared,) = call(functools.partial(couple, frame_count), [(frame_count, 1, 128)], "vvv")(second, previous, partial)
-    received = lax.all_to_all(shared, "tm", 0, 0)
-    (shared,) = call(functools.partial(regroup, peers), [(peers, 1, 128)], "v")(received)
-    received = lax.all_to_all(shared, ("row", "col"), 0, 0)
+    group = frame_count * col_count
+    (shared,) = call(functools.partial(couple, group), [(group, 1, 128)], "vvv")(second, previous, partial)
+    received = lax.all_to_all(shared, ("tm", "col"), 0, 0)
+    (shared,) = call(functools.partial(regroup, row_count), [(row_count, 1, 128)], "v")(received)
+    received = lax.all_to_all(shared, "row", 0, 0)
     (answer,) = call(combine, [(3 * ROWS, COLS)], "vvv")(received, first, second)
     return answer.reshape(right_side.shape)
 

time: 120 us -> 119 us (level)
  no operation moved by 1% of the time
where the time goes in v5:
time: 119 us
  starting transfers between devices  45.8 us (38%)
  blocking collectives  31.4 us (26%)
  waiting for transfers between devices  19.3 us (16%)
  Pallas kernels  16 us (13%)
  local copies, waits for them, and re-layouts  6.03 us (5%)
    all_to_all x1, blocking collectives, shards(): received = lax.all_to_all(shared, 'row', 0, 0)  18.1 us
    all_to_all x1, starting transfers between devices, shards(): gathered = lax.all_to_all(message, ('row', 'col'), 0, 0)  17.8 us
    all_to_all x1, blocking collectives, shards(): received = lax.all_to_all(shared, ('tm', 'col'), 0, 0)  13.3 us
    ppermute x4, starting transfers between devices, exchange(): lax.ppermute(last, axis, forward)  12.8 us
    ppermute x4, starting transfers between devices, exchange(): lax.ppermute(first, axis, backward)  10 us
    ppermute x4, waiting for transfers between devices, exchange(): lax.ppermute(first, axis, backward)  8.78 us
    pallas_call x1, Pallas kernels, shards(): call(functools.partial(second_apply, row_count, col_count), [(3 * ROWS, C...  6.33 us
    unnamed x12, local copies, waits for them, and re-layouts  6.03 us
  transfers between devices with their start and end apart: 10, of which 9 were waited for; matrix products, arithmetic and copies ran while one was open for 0% of the time, Pallas kernels for 2%

profile of v5, /device:TPU:1, one launch (start us, length us, event | category | flops | bytes accessed | tf_op | source)
XLA Modules:
  0.0 118.9 jit_solution(8718449671468695772)
XLA Ops:
  0.0 0.9 copy-done.2
  0.9 0.8 copy-done.4
  1.7 4.4 %collective-permute-start = (f32[4,24,256]{2,1,0:T(8,128)S(1)}, f32[4,24,256]{2,1,0:T(8,128)S(1)}, u32[]{:S(2)}, u32[]{:S(2)}) collective-permute-start(f32[4,24,256]{2,1,0:T(8,128)S(1)} %get-tuple-element.38), channel_id=1, source_target_pairs={{0,4},{4,8},{8,12},{12,16},{16,20},{20,24},{24,28},{28,32},{32,36}... | collective-permute-start | bytes 294920 | tf_op jit(solution)/shard_map/ppermute | solution.py:387
  6.1 1.3 %collective-permute-start.1 = (f32[4,24,256]{2,1,0:T(8,128)S(1)}, f32[4,24,256]{2,1,0:T(8,128)S(1)}, u32[]{:S(2)}, u32[]{:S(2)}) collective-permute-start(f32[4,24,256]{2,1,0:T(8,128)S(1)} %get-tuple-element.40), channel_id=1, source_target_pairs={{4,0},{8,4},{12,8},{16,12},{20,16},{24,20},{28,24},{32,28},{36,32}... | collective-permute-start | bytes 294920 | tf_op jit(solution)/shard_map/ppermute | solution.py:387
  7.4 0.2 fusion.16.keep
  7.7 3.9 %collective-permute-done.1.high = f32[4,24,256]{2,1,0:T(8,128)S(1)} collective-permute-done((f32[4,24,256]{2,1,0:T(8,128)S(1)}, f32[4,24,256]{2,1,0:T(8,128)S(1)}, u32[]{:S(2)}, u32[]{:S(2)}) %collective-permute-start.1) | collective-permute-done | bytes 98336 | tf_op jit(solution)/shard_map/ppermute | solution.py:387
  11.6 0.4 shard_map.56
  12.0 3.1 %collective-permute-start.2 = (f32[4,40,128]{2,1,0:T(8,128)S(1)}, f32[4,40,128]{2,1,0:T(8,128)S(1)}, u32[]{:S(2)}, u32[]{:S(2)}) collective-permute-start(f32[4,40,128]{2,1,0:T(8,128)S(1)} %get-tuple-element.44), channel_id=1, source_target_pairs={{0,1},{1,2},{2,3},{4,5},{5,6},{6,7},{8,9},{9,10},{10,11},{12,13},{... | collective-permute-start | bytes 245768 | tf_op jit(solution)/shard_map/ppermute | solution.py:387
  15.1 1.3 %collective-permute-start.3 = (f32[4,40,128]{2,1,0:T(8,128)S(1)}, f32[4,40,128]{2,1,0:T(8,128)S(1)}, u32[]{:S(2)}, u32[]{:S(2)}) collective-permute-start(f32[4,40,128]{2,1,0:T(8,128)S(1)} %get-tuple-element.45), channel_id=1, source_target_pairs={{1,0},{2,1},{3,2},{5,4},{6,5},{7,6},{9,8},{10,9},{11,10},{13,12},{... | collective-permute-start | bytes 245768 | tf_op jit(solution)/shard_map/ppermute | solution.py:387
  16.5 2.2 %copy-done = f32[1024,1024]{1,0:T(8,128)S(1)} copy-done((f32[1024,1024]{1,0:T(8,128)S(1)}, f32[1024,1024]{1,0:T(8,128)}, u32[]{:S(2)}) %copy-start) | copy-done | bytes 4194328
  18.7 0.7 shard_map.57
  19.4 1.0 collective-permute-done.3.right
  20.3 4.8 %shard_map.58 = (f32[3,272,128]{2,1,0:T(8,128)S(1)}, f32[80,384]{1,0:T(8,128)S(1)}, f32[104,384]{1,0:T(8,128)S(1)}) custom-call(s32[2]{0:T(128)S(1)} %pad_add_fusion.place, f32[4,80,384]{2,1,0:T(8,128)S(1)} %get-tuple-element.41.tall.block, f32[4,40,128]{2,1,0:T(8,128)S(1)} %collective-permute-done.2.left, f32[4,40,128]{2,1,0:T(8,128)S(1)} %collective-permute-done.3.right, ...), custom_call_target="tpu_custom_call" | custom-call | tf_op jit(solution)/shard_map/pallas_call | solution.py:420
  25.1 6.0 %collective-permute-start.5 = (f32[104,384]{1,0:T(8,128)S(1)}, f32[104,384]{1,0:T(8,128)S(1)}, u32[]{:S(2)}, u32[]{:S(2)}) collective-permute-start(f32[104,384]{1,0:T(8,128)S(1)} %get-tuple-element.55), channel_id=1, source_target_pairs={{64,0},{128,64},{192,128},{256,192},{320,256},{384,320},{448,384},... | collective-permute-start | bytes 479240 | tf_op jit(solution)/shard_map/ppermute | solution.py:387
  31.1 2.4 %collective-permute-start.4 = (f32[104,384]{1,0:T(8,128)S(1)}, f32[104,384]{1,0:T(8,128)S(1)}, u32[]{:S(2)}, u32[]{:S(2)}) collective-permute-start(f32[104,384]{1,0:T(8,128)S(1)} %get-tuple-element.55), channel_id=1, source_target_pairs={{0,64},{64,128},{128,192},{192,256},{256,320},{320,384},{384,448},... | collective-permute-start | bytes 479240 | tf_op jit(solution)/shard_map/ppermute | solution.py:387
  33.5 1.0 collective-permute-done.5.after
  34.5 1.2 collective-permute-done.4.before
  35.7 1.7 %shard_map.59 = (f32[3,32,384]{2,1,0:T(8,128)S(1)}, f32[3,24,384]{2,1,0:T(8,128)S(1)}, f32[3,24,384]{2,1,0:T(8,128)S(1)}, f32[64,1,384]{2,1,0:T(1,128)}) custom-call(s32[2]{0:T(128)S(1)} %pad_add_fusion.place, f32[3,272,128]{2,1,0:T(8,128)S(1)} %get-tuple-element.54.result, f32[104,384]{1,0:T(8,128)S(1)} %collective-permute-done.4.before, ...), custom_call_target="tpu_custom_call" | custom-call | tf_op jit(solution)/shard_map/pallas_call | solution.py:428
  37.4 17.8 %all-to-all-start = ((f32[64,1,384]{2,1,0:T(1,128)}), f32[64,1,384]{2,1,0:T(1,128)S(1)}, u32[]{:S(2)}, u32[]{:S(2)}) async-start(f32[64,1,384]{2,1,0:T(1,128)} %get-tuple-element.58), calls=%async_computation | async-start | bytes 196608 | tf_op jit(solution)/shard_map/all_to_all | solution.py:440
  55.2 2.9 %collective-permute-start.6 = (f32[3,24,384]{2,1,0:T(8,128)S(1)}, f32[3,24,384]{2,1,0:T(8,128)S(1)}, u32[]{:S(2)}, u32[]{:S(2)}) collective-permute-start(f32[3,24,384]{2,1,0:T(8,128)S(1)} %get-tuple-element.60), channel_id=1, source_target_pairs={{0,4},{4,8},{8,12},{12,16},{16,20},{20,24},{24,28},{28,32},{32,36}... | collective-permute-start | bytes 331784 | tf_op jit(solution)/shard_map/ppermute | solution.py:387
  58.1 1.5 %collective-permute-start.7 = (f32[3,24,384]{2,1,0:T(8,128)S(1)}, f32[3,24,384]{2,1,0:T(8,128)S(1)}, u32[]{:S(2)}, u32[]{:S(2)}) collective-permute-start(f32[3,24,384]{2,1,0:T(8,128)S(1)} %get-tuple-element.61), channel_id=1, source_target_pairs={{4,0},{8,4},{12,8},{16,12},{20,16},{24,20},{28,24},{32,28},{36,32}... | collective-permute-start | bytes 331784 | tf_op jit(solution)/shard_map/ppermute | solution.py:387
  59.6 1.2 shard_map.60
  60.8 1.6 %collective-permute-done.6.low = f32[3,24,384]{2,1,0:T(8,128)S(1)} collective-permute-done((f32[3,24,384]{2,1,0:T(8,128)S(1)}, f32[3,24,384]{2,1,0:T(8,128)S(1)}, u32[]{:S(2)}, u32[]{:S(2)}) %collective-permute-start.6) | collective-permute-done | bytes 110624 | tf_op jit(solution)/shard_map/ppermute | solution.py:387
  62.4 2.9 %collective-permute-done.7.high = f32[3,24,384]{2,1,0:T(8,128)S(1)} collective-permute-done((f32[3,24,384]{2,1,0:T(8,128)S(1)}, f32[3,24,384]{2,1,0:T(8,128)S(1)}, u32[]{:S(2)}, u32[]{:S(2)}) %collective-permute-start.7) | collective-permute-done | bytes 110624 | tf_op jit(solution)/shard_map/ppermute | solution.py:387
  65.3 6.0 %all-to-all-done.gathered = f32[64,1,384]{2,1,0:T(1,128)S(1)} async-done(((f32[64,1,384]{2,1,0:T(1,128)}), f32[64,1,384]{2,1,0:T(1,128)S(1)}, u32[]{:S(2)}, u32[]{:S(2)}) %all-to-all-start) | async-done | bytes 98336 | tf_op jit(solution)/shard_map/all_to_all | solution.py:440
  71.3 2.2 %copy-done.1 = f32[1024,1024]{1,0:T(8,128)S(1)} copy-done((f32[1024,1024]{1,0:T(8,128)S(1)}, f32[1024,1024]{1,0:T(8,128)}, u32[]{:S(2)}) %copy-start.1) | copy-done | bytes 4194328
  73.5 6.3 %shard_map.61 = (f32[96,256]{1,0:T(8,128)S(1)}, f32[96,256]{1,0:T(8,128)S(1)}, f32[1,128]{1,0:T(1,128)S(1)}) custom-call(s32[2]{0:T(128)S(1)} %pad_add_fusion.place, f32[64,1,384]{2,1,0:T(1,128)S(1)} %all-to-all-done.gathered, f32[4,80,384]{2,1,0:T(8,128)S(1)} %get-tuple-element.41.tall.block, f32[3,272,128]{2,1,0:T(8,128)S(1)} %get-tuple-element.54.result, ...), custom_call_target="tpu_custom_call" | custom-call | tf_op jit(solution)/shard_map/pallas_call | solution.py:441
  79.8 5.1 %collective-permute-start.8 = (f32[96,256]{1,0:T(8,128)S(1)}, f32[96,256]{1,0:T(8,128)S(1)}, u32[]{:S(2)}, u32[]{:S(2)}) collective-permute-start(f32[96,256]{1,0:T(8,128)S(1)} %get-tuple-element.68.second), channel_id=1, source_target_pairs={{0,64},{64,128},{128,192},{192,256},{256,320},{320,384},{384,448},... | collective-permute-start | bytes 294920 | tf_op jit(solution)/shard_map/ppermute | solution.py:452
  84.9 1.6 %collective-permute-done.8.before = f32[96,256]{1,0:T(8,128)S(1)} collective-permute-done((f32[96,256]{1,0:T(8,128)S(1)}, f32[96,256]{1,0:T(8,128)S(1)}, u32[]{:S(2)}, u32[]{:S(2)}) %collective-permute-start.8) | collective-permute-done | bytes 98336 | tf_op jit(solution)/shard_map/ppermute | solution.py:452
  86.7 13.3 %all_to_all.15.received = f32[32,1,128]{2,1,0:T(1,128)S(1)} all-to-all(f32[32,1,128]{2,1,0:T(1,128)S(1)} %shard_map.62), channel_id=1, replica_groups=mesh['tm'=8,'row'=16,'col'=4] {'tm','col'}, dimensions={0} | all-to-all | bytes 32768 | tf_op jit(solution)/shard_map/all_to_all | solution.py:455
  100.0 18.1 %all_to_all.16.received = f32[16,1,128]{2,1,0:T(1,128)S(1)} all-to-all(f32[16,1,128]{2,1,0:T(1,128)S(1)} %shard_map.63), channel_id=1, replica_groups=mesh['tm'=8,'row'=16,'col'=4] {'row'}, dimensions={0} | all-to-all | bytes 16384 | tf_op jit(solution)/shard_map/all_to_all | solution.py:457
  118.1 0.8 shard_map.64
  (14 shorter events, 0.4 us)
Async XLA Ops:
  0.0 0.9 copy-start.2
  0.9 0.8 copy-start.4
  1.7 6.0 %collective-permute-start = (f32[4,24,256]{2,1,0:T(8,128)S(1)}, f32[4,24,256]{2,1,0:T(8,128)S(1)}, u32[]{:S(2)}, u32[]{:S(2)}) collective-permute-start(f32[4,24,256]{2,1,0:T(8,128)S(1)} %get-tuple-element.38), channel_id=1, source_target_pairs={{0,4},{4,8},{8,12},{12,16},{16,20},{20,24},{24,28},{28,32},{32,36}... | collective-permute-start | bytes 294920 | tf_op jit(solution)/shard_map/ppermute | solution.py:387
  6.1 5.5 %collective-permute-start.1 = (f32[4,24,256]{2,1,0:T(8,128)S(1)}, f32[4,24,256]{2,1,0:T(8,128)S(1)}, u32[]{:S(2)}, u32[]{:S(2)}) collective-permute-start(f32[4,24,256]{2,1,0:T(8,128)S(1)} %get-tuple-element.40), channel_id=1, source_target_pairs={{4,0},{8,4},{12,8},{16,12},{20,16},{24,20},{28,24},{32,28},{36,32}... | collective-permute-start | bytes 294920 | tf_op jit(solution)/shard_map/ppermute | solution.py:387
  12.0 7.4 %collective-permute-start.2 = (f32[4,40,128]{2,1,0:T(8,128)S(1)}, f32[4,40,128]{2,1,0:T(8,128)S(1)}, u32[]{:S(2)}, u32[]{:S(2)}) collective-permute-start(f32[4,40,128]{2,1,0:T(8,128)S(1)} %get-tuple-element.44), channel_id=1, source_target_pairs={{0,1},{1,2},{2,3},{4,5},{5,6},{6,7},{8,9},{9,10},{10,11},{12,13},{... | collective-permute-start | bytes 245768 | tf_op jit(solution)/shard_map/ppermute | solution.py:387
  15.1 5.2 %collective-permute-start.3 = (f32[4,40,128]{2,1,0:T(8,128)S(1)}, f32[4,40,128]{2,1,0:T(8,128)S(1)}, u32[]{:S(2)}, u32[]{:S(2)}) collective-permute-start(f32[4,40,128]{2,1,0:T(8,128)S(1)} %get-tuple-element.45), channel_id=1, source_target_pairs={{1,0},{2,1},{3,2},{5,4},{6,5},{7,6},{9,8},{10,9},{11,10},{13,12},{... | collective-permute-start | bytes 245768 | tf_op jit(solution)/shard_map/ppermute | solution.py:387
  16.5 2.2 %copy-start = (f32[1024,1024]{1,0:T(8,128)S(1)}, f32[1024,1024]{1,0:T(8,128)}, u32[]{:S(2)}) copy-start(f32[1024,1024]{1,0:T(8,128)} %inverse.1) | copy-start | bytes 12582916
  20.3 39.3 %copy-start.3 = (f32[64,64]{1,0:T(8,128)S(1)}, f32[64,64]{1,0:T(8,128)}, u32[]{:S(2)}) copy-start(f32[64,64]{1,0:T(8,128)} %col_coupling) | copy-start | bytes 49156
  20.3 39.3 %copy-start.5 = (f32[32,32]{1,0:T(8,128)S(1)}, f32[32,32]{1,0:T(8,128)}, u32[]{:S(2)}) copy-start(f32[32,32]{1,0:T(8,128)} %row_coupling) | copy-start | bytes 12292
  25.1 9.4 %collective-permute-start.5 = (f32[104,384]{1,0:T(8,128)S(1)}, f32[104,384]{1,0:T(8,128)S(1)}, u32[]{:S(2)}, u32[]{:S(2)}) collective-permute-start(f32[104,384]{1,0:T(8,128)S(1)} %get-tuple-element.55), channel_id=1, source_target_pairs={{64,0},{128,64},{192,128},{256,192},{320,256},{384,320},{448,384},... | collective-permute-start | bytes 479240 | tf_op jit(solution)/shard_map/ppermute | solution.py:387
  31.1 4.6 %collective-permute-start.4 = (f32[104,384]{1,0:T(8,128)S(1)}, f32[104,384]{1,0:T(8,128)S(1)}, u32[]{:S(2)}, u32[]{:S(2)}) collective-permute-start(f32[104,384]{1,0:T(8,128)S(1)} %get-tuple-element.55), channel_id=1, source_target_pairs={{0,64},{64,128},{128,192},{192,256},{256,320},{320,384},{384,448},... | collective-permute-start | bytes 479240 | tf_op jit(solution)/shard_map/ppermute | solution.py:387
  37.4 33.9 %all-to-all-start = ((f32[64,1,384]{2,1,0:T(1,128)}), f32[64,1,384]{2,1,0:T(1,128)S(1)}, u32[]{:S(2)}, u32[]{:S(2)}) async-start(f32[64,1,384]{2,1,0:T(1,128)} %get-tuple-element.58), calls=%async_computation | async-start | bytes 196608 | tf_op jit(solution)/shard_map/all_to_all | solution.py:440
  55.2 7.2 %collective-permute-start.6 = (f32[3,24,384]{2,1,0:T(8,128)S(1)}, f32[3,24,384]{2,1,0:T(8,128)S(1)}, u32[]{:S(2)}, u32[]{:S(2)}) collective-permute-start(f32[3,24,384]{2,1,0:T(8,128)S(1)} %get-tuple-element.60), channel_id=1, source_target_pairs={{0,4},{4,8},{8,12},{12,16},{16,20},{20,24},{24,28},{28,32},{32,36}... | collective-permute-start | bytes 331784 | tf_op jit(solution)/shard_map/ppermute | solution.py:387
  58.1 7.1 %collective-permute-start.7 = (f32[3,24,384]{2,1,0:T(8,128)S(1)}, f32[3,24,384]{2,1,0:T(8,128)S(1)}, u32[]{:S(2)}, u32[]{:S(2)}) collective-permute-start(f32[3,24,384]{2,1,0:T(8,128)S(1)} %get-tuple-element.61), channel_id=1, source_target_pairs={{4,0},{8,4},{12,8},{16,12},{20,16},{24,20},{28,24},{32,28},{36,32}... | collective-permute-start | bytes 331784 | tf_op jit(solution)/shard_map/ppermute | solution.py:387
  71.3 2.2 %copy-start.1 = (f32[1024,1024]{1,0:T(8,128)S(1)}, f32[1024,1024]{1,0:T(8,128)}, u32[]{:S(2)}) copy-start(f32[1024,1024]{1,0:T(8,128)} %inverse.1) | copy-start | bytes 12582916
  79.8 6.8 %collective-permute-start.8 = (f32[96,256]{1,0:T(8,128)S(1)}, f32[96,256]{1,0:T(8,128)S(1)}, u32[]{:S(2)}, u32[]{:S(2)}) collective-permute-start(f32[96,256]{1,0:T(8,128)S(1)} %get-tuple-element.68.second), channel_id=1, source_target_pairs={{0,64},{64,128},{128,192},{192,256},{256,320},{320,384},{384,448},... | collective-permute-start | bytes 294920 | tf_op jit(solution)/shard_map/ppermute | solution.py:452
